TPU v7x, 32 devices: a whole 2x2x4 slice. The times are simulated.
32 devices in a mesh: ctx: 8 (over y, x, core), head: 4 (over z).
Axes of the slice: x: 2, y: 2, z: 4, core: 2. Of those that a mesh axis runs over, the one named last changes fastest.
Arguments:
- query: bfloat16 [4096, 2048], P('ctx', 'head'), may hold values from -6 to 6
- key: bfloat16 [4096, 2048], P('ctx', 'head'), may hold values from -6 to 6
- value: bfloat16 [4096, 2048], P('ctx', 'head'), may hold values from -6 to 6
- out_grad: bfloat16 [4096, 2048], P('ctx', 'head'), may hold values from -6 to 6
- links: int32 [32, 6], replicated, may hold values from -1 to 29, as said below
Outputs:
- query_grad: bfloat16 [4096, 2048], P('ctx', 'head')
- key_grad: bfloat16 [4096, 2048], P('ctx', 'head')
- value_grad: bfloat16 [4096, 2048], P('ctx', 'head')
Inputs may be any that keep to these rules, and one draw needn't show every extreme that they name: `links`: entry (b, s) is -1 or the index of a block at most b - 2. Over the 6 entries of all query blocks held by one index of ctx, at most 3 name blocks held by any one index of ctx (itself included), and on every index of ctx some index is named exactly 3 times.
All inputs are finite; a program needn't handle non-finite values.
Results may differ from a plain program's by a relative error of at most 0.01.
Values may be sent and summed in bfloat16 or wider, within the bound.
No kernel may reach another device: no remote copies, remote signals or barrier semaphores. Data moves between devices by JAX's collectives and lax.ppermute only.
A program may use at most 192 MiB of HBM per device.

v0:
```python
import functools
import math

import jax
import jax.numpy as jnp
from jax import lax
from jax.experimental import pallas as pl
from jax.experimental.pallas import tpu as pltpu
from jax.sharding import PartitionSpec as P

HEAD_DIM = 128
BLK = 128
WIN = 2
LINKS = 6
SPAN = WIN + LINKS
NEG_FILL = -1e30
VMEM_LIMIT = 48 * 1024 * 1024


def swapped(x, by):
    count = lax.axis_size("ctx")
    return lax.ppermute(x, "ctx", [(i, i ^ by) for i in range(count)])


def split_heads_kernel(members, groups, *refs):
    first, second = refs[:2]
    outs = refs[2 : 2 + groups]
    sems = refs[2 + groups]
    chip = lax.axis_index("ctx") // members
    copies = []
    for s in range(groups):
        column = pl.multiple_of((chip ^ s) * HEAD_DIM, HEAD_DIM)
        for t, source in enumerate((first, second)):
            copies.append(
                pltpu.make_async_copy(
                    source.at[:, pl.ds(column, HEAD_DIM)], outs[s].at[t], sems.at[2 * s + t]
                )
            )
    for copy in copies:
        copy.start()
    for copy in copies:
        copy.wait()


def split_heads(first, second, members, groups):
    rows = first.shape[0]
    return pl.pallas_call(
        functools.partial(split_heads_kernel, members, groups),
        out_shape=[jax.ShapeDtypeStruct((2, rows, HEAD_DIM), first.dtype)] * groups,
        in_specs=[pl.BlockSpec(memory_space=pl.ANY)] * 2,
        out_specs=[pl.BlockSpec(memory_space=pl.ANY)] * groups,
        scratch_shapes=[pltpu.SemaphoreType.DMA((2 * groups,))],
        cost_estimate=pl.CostEstimate(
            flops=0, bytes_accessed=4 * first.size * first.dtype.itemsize, transcendentals=0
        ),
        name="split_heads",
    )(first, second)


def join_heads_kernel(members, groups, *refs):
    dq_parts = refs[:groups]
    pair_parts = refs[groups : 2 * groups]
    outs = refs[2 * groups : 2 * groups + 3]
    sems = refs[2 * groups + 3]
    chip = lax.axis_index("ctx") // members
    copies = []
    for s in range(groups):
        column = pl.multiple_of((chip ^ s) * HEAD_DIM, HEAD_DIM)
        for t, source in enumerate((dq_parts[s], pair_parts[s].at[0], pair_parts[s].at[1])):
            copies.append(
                pltpu.make_async_copy(
                    source, outs[t].at[:, pl.ds(column, HEAD_DIM)], sems.at[3 * s + t]
                )
            )
    for copy in copies:
        copy.start()
    for copy in copies:
        copy.wait()


def join_heads(dq_parts, pair_parts, members, groups):
    rows = dq_parts[0].shape[0]
    out = jax.ShapeDtypeStruct((rows, groups * HEAD_DIM), jnp.bfloat16)
    return pl.pallas_call(
        functools.partial(join_heads_kernel, members, groups),
        out_shape=[out] * 3,
        in_specs=[pl.BlockSpec(memory_space=pl.ANY)] * (2 * groups),
        out_specs=[pl.BlockSpec(memory_space=pl.ANY)] * 3,
        scratch_shapes=[pltpu.SemaphoreType.DMA((3 * groups,))],
        cost_estimate=pl.CostEstimate(
            flops=0, bytes_accessed=12 * rows * groups * HEAD_DIM, transcendentals=0
        ),
        name="join_heads",
    )(*dq_parts, *pair_parts)


def dot(left, right, dims):
    return lax.dot_general(left, right, (dims, ((), ())), preferred_element_type=jnp.float32)


def attend_kernel(shards, members, groups, rows, *refs):
    slots = members * groups
    links = refs[0]
    pairs = refs[1 : 1 + slots]
    asks = refs[1 + slots : 1 + slots + groups]
    refs = refs[1 + slots + groups :]
    dq_outs = refs[:groups]
    own_outs = refs[groups : 2 * groups]
    far_outs = refs[2 * groups : 2 * groups + members - 1]
    key_buf, value_buf, query_buf, grad_buf, key_acc, value_acc, sems = refs[
        2 * groups + members - 1 :
    ]
    device = lax.axis_index("ctx")
    local_blocks = rows // BLK
    stretch = local_blocks // 2
    copies = []
    for i in range(slots):
        place = pl.ds(i * rows, rows)
        copies.append(pltpu.make_async_copy(pairs[i].at[0], key_buf.at[place], sems.at[2 * i]))
        copies.append(
            pltpu.make_async_copy(pairs[i].at[1], value_buf.at[place], sems.at[2 * i + 1])
        )
    for s in range(groups):
        place = pl.ds(s * rows, rows)
        at = 2 * (slots + s)
        copies.append(pltpu.make_async_copy(asks[s].at[0], query_buf.at[place], sems.at[at]))
        copies.append(pltpu.make_async_copy(asks[s].at[1], grad_buf.at[place], sems.at[at + 1]))
    for copy in copies:
        copy.start()
    key_acc[...] = jnp.zeros_like(key_acc)
    value_acc[...] = jnp.zeros_like(value_acc)
    for copy in copies:
        copy.wait()

    scaling = HEAD_DIM**-0.5
    causal = lax.broadcasted_iota(jnp.int32, (BLK, BLK), 0) <= lax.broadcasted_iota(
        jnp.int32, (BLK, BLK), 1
    )

    def place_of(block):
        run = lax.div(block, stretch)
        late = run >= shards
        owner = jnp.where(late, 2 * shards - 1 - run, run)
        local = block - run * stretch + jnp.where(late, stretch, 0)
        apart = owner ^ device
        slot = lax.rem(apart, members) * groups + lax.div(apart, members)
        return pl.multiple_of((slot * local_blocks + local) * BLK, BLK)

    for s in range(groups):
        asker = device ^ (s * members)

        def step(local, _, s=s, asker=asker):
            early = asker * stretch + local
            block = jnp.where(
                local < stretch, early, (2 * shards - 1 - asker) * stretch + local - stretch
            )
            listed = [block, block - 1] + [links[block, i] for i in range(LINKS)]
            places = [place_of(jnp.maximum(j, 0)) for j in listed]
            here = pl.ds(pl.multiple_of(s * rows + local * BLK, BLK), BLK)
            q = query_buf[here, :]
            o = grad_buf[here, :]
            keys = jnp.concatenate([key_buf[pl.ds(p, BLK), :] for p in places], 0)
            values = jnp.concatenate([value_buf[pl.ds(p, BLK), :] for p in places], 0)
            raw = dot(keys, q, ((1,), (1,))).reshape(SPAN, BLK, BLK) * (
                scaling * math.log2(math.e)
            )
            parts = [jnp.where(causal, raw[0], NEG_FILL)]
            for i in range(1, SPAN):
                parts.append(raw[i] + jnp.where(listed[i] >= 0, 0.0, NEG_FILL))
            score = jnp.concatenate(parts, 0)
            top = jnp.max(score, axis=0, keepdims=True)
            prob = jnp.exp2(score - top)
            prob = prob * (1.0 / jnp.sum(prob, axis=0, keepdims=True))
            dprob = dot(values, o, ((1,), (1,)))
            delta = jnp.sum(prob * dprob, axis=0, keepdims=True)
            dscore = (prob * (dprob - delta)).astype(jnp.bfloat16)
            prob = prob.astype(jnp.bfloat16)
            dk = dot(dscore, q, ((1,), (0,)))
            dv = dot(prob, o, ((1,), (0,)))
            for i, p in enumerate(places):
                key_acc[pl.ds(p, BLK), :] += dk[i * BLK : (i + 1) * BLK]
                value_acc[pl.ds(p, BLK), :] += dv[i * BLK : (i + 1) * BLK]
            dq = dot(dscore, keys, ((0,), (0,))) * scaling
            dq_outs[s][pl.ds(pl.multiple_of(local * BLK, BLK), BLK), :] = dq.astype(jnp.bfloat16)
            return 0

        lax.fori_loop(0, local_blocks, step, 0)

    for s in range(groups):
        own_outs[s][0] = key_acc[s * rows : (s + 1) * rows, :] * scaling
        own_outs[s][1] = value_acc[s * rows : (s + 1) * rows, :]
    for r in range(1, members):
        for s in range(groups):
            at = slice((r * groups + s) * rows, (r * groups + s + 1) * rows)
            far_outs[r - 1][s, 0] = (key_acc[at, :] * scaling).astype(jnp.bfloat16)
            far_outs[r - 1][s, 1] = value_acc[at, :].astype(jnp.bfloat16)


def attend(links, pairs, asks, shards, members, groups):
    rows = asks[0].shape[1]
    slots = members * groups
    total = slots * rows
    blocks = groups * rows // BLK
    hbm = pl.BlockSpec(memory_space=pl.ANY)
    outs = (
        [jax.ShapeDtypeStruct((rows, HEAD_DIM), jnp.bfloat16)] * groups
        + [jax.ShapeDtypeStruct((2, rows, HEAD_DIM), jnp.float32)] * groups
        + [jax.ShapeDtypeStruct((groups, 2, rows, HEAD_DIM), jnp.bfloat16)] * (members - 1)
    )
    found = pl.pallas_call(
        functools.partial(attend_kernel, shards, members, groups, rows),
        out_shape=outs,
        in_specs=[pl.BlockSpec(memory_space=pltpu.SMEM)] + [hbm] * (slots + groups),
        out_specs=[pl.BlockSpec(memory_space=pltpu.VMEM)] * len(outs),
        scratch_shapes=[
            pltpu.VMEM((total, HEAD_DIM), jnp.bfloat16),
            pltpu.VMEM((total, HEAD_DIM), jnp.bfloat16),
            pltpu.VMEM((groups * rows, HEAD_DIM), jnp.bfloat16),
            pltpu.VMEM((groups * rows, HEAD_DIM), jnp.bfloat16),
            pltpu.VMEM((total, HEAD_DIM), jnp.float32),
            pltpu.VMEM((total, HEAD_DIM), jnp.float32),
            pltpu.SemaphoreType.DMA((2 * (slots + groups),)),
        ],
        compiler_params=pltpu.CompilerParams(vmem_limit_bytes=VMEM_LIMIT),
        cost_estimate=pl.CostEstimate(
            flops=10 * blocks * SPAN * BLK * BLK * HEAD_DIM,
            bytes_accessed=8 * total * HEAD_DIM,
            transcendentals=blocks * SPAN * BLK * BLK,
        ),
        name="attend",
    )(links, *pairs, *asks)
    return found[:groups], found[groups : 2 * groups], found[2 * groups :]


def per_device(query, key, value, out_grad, links):
    groups = query.shape[1] // HEAD_DIM
    shards = lax.axis_size("ctx")
    members = shards // groups

    pairs = split_heads(key, value, members, groups)
    asks = split_heads(query, out_grad, members, groups)
    pairs = [pairs[0]] + [swapped(pairs[s], s * members) for s in range(1, groups)]
    asks = [asks[0]] + [swapped(asks[s], s * members) for s in range(1, groups)]
    pairs = pairs + [swapped(pairs[s], r) for r in range(1, members) for s in range(groups)]

    dq_parts, own, far = attend(links, pairs, asks, shards, members, groups)

    dq_parts = [dq_parts[0]] + [swapped(dq_parts[s], s * members) for s in range(1, groups)]
    far = [swapped(far[r - 1], r) for r in range(1, members)]
    pair_parts = []
    for s in range(groups):
        total = own[s]
        for part in far:
            total = total + part[s].astype(jnp.float32)
        total = total.astype(jnp.bfloat16)
        pair_parts.append(total if s == 0 else swapped(total, s * members))
    return tuple(join_heads(dq_parts, pair_parts, members, groups))


def solution(mesh):
    return jax.shard_map(
        per_device,
        mesh=mesh,
        in_specs=(P("ctx", "head"), P("ctx", "head"), P("ctx", "head"), P("ctx", "head"), P()),
        out_specs=(P("ctx", "head"), P("ctx", "head"), P("ctx", "head")),
        check_vma=False,
    )
```

profile of v0, /device:TPU:0, one launch (start us, length us, event | category | flops | bytes accessed | tf_op | source)
XLA Modules:
  0.0 190.0 jit_solution(9013892929988701865)
XLA Ops:
  0.6 33.0 %split_heads.3 = (bf16[2,512,128]{2,1,0:T(8,128)(2,1)}, bf16[2,512,128]{2,1,0:T(8,128)(2,1)}, bf16[2,512,128]{2,1,0:T(8,128)(2,1)}, bf16[2,512,128]{2,1,0:T(8,128)(2,1)}) custom-call(bf16[512,512]{1,0:T(8,128)(2,1)} %refs_0_.4, bf16[512,512]{1,0:T(8,128)(2,1)} %refs_1_.3), custom_call_target="tpu_custom_call" | custom-call | bytes 2097152 | tf_op jit(solution)/shard_map/split_heads/pallas_call | solution.py:47
  33.6 3.0 %collective-permute-start.7 = (bf16[2,512,128]{2,1,0:T(8,128)(2,1)}, bf16[2,512,128]{2,1,0:T(8,128)(2,1)S(1)}, u32[]{:S(2)}, u32[]{:S(2)}) collective-permute-start(bf16[2,512,128]{2,1,0:T(8,128)(2,1)} %get-tuple-element.25), channel_id=1, source_target_pairs={{0,8},{4,12},{8,0},{12,4},{16,24},{20,28},{24,16},{28,20},{1,9},{5... | collective-permute-start | bytes 786440 | tf_op jit(solution)/shard_map/ppermute | solution.py:22
  36.6 1.5 collective-permute-start.8
  38.1 32.9 %split_heads.2 = (bf16[2,512,128]{2,1,0:T(8,128)(2,1)}, bf16[2,512,128]{2,1,0:T(8,128)(2,1)}, bf16[2,512,128]{2,1,0:T(8,128)(2,1)}, bf16[2,512,128]{2,1,0:T(8,128)(2,1)}) custom-call(bf16[512,512]{1,0:T(8,128)(2,1)} %refs_0_.3, bf16[512,512]{1,0:T(8,128)(2,1)} %refs_1_.2), custom_call_target="tpu_custom_call" | custom-call | bytes 2097152 | tf_op jit(solution)/shard_map/split_heads/pallas_call | solution.py:47
  71.1 0.0 copy-start.9
  71.1 0.6 collective-permute-start
  71.7 0.1 collective-permute-start.1
  71.7 2.9 %collective-permute-start.2 = (bf16[2,512,128]{2,1,0:T(8,128)(2,1)}, bf16[2,512,128]{2,1,0:T(8,128)(2,1)S(1)}, u32[]{:S(2)}, u32[]{:S(2)}) collective-permute-start(bf16[2,512,128]{2,1,0:T(8,128)(2,1)} %get-tuple-element.23), channel_id=1, source_target_pairs={{0,24},{4,28},{8,16},{12,20},{16,8},{20,12},{24,0},{28,4},{1,25},{... | collective-permute-start | bytes 786440 | tf_op jit(solution)/shard_map/ppermute | solution.py:22
  74.6 0.0 collective-permute-done.7.refs_10_
  74.6 0.0 copy-done.10
  74.6 0.1 collective-permute-start.9
  74.7 0.0 collective-permute-done.8.refs_11_
  74.7 0.0 collective-permute-start.3
  74.7 5.9 %collective-permute-done.refs_2_ = bf16[2,512,128]{2,1,0:T(8,128)(2,1)S(1)} collective-permute-done((bf16[2,512,128]{2,1,0:T(8,128)(2,1)}, bf16[2,512,128]{2,1,0:T(8,128)(2,1)S(1)}, u32[]{:S(2)}, u32[]{:S(2)}) %collective-permute-start) | collective-permute-done | bytes 262176 | tf_op jit(solution)/shard_map/ppermute | solution.py:22
  80.6 0.0 collective-permute-start.4
  80.6 9.7 %collective-permute-done.1.refs_3_ = bf16[2,512,128]{2,1,0:T(8,128)(2,1)S(1)} collective-permute-done((bf16[2,512,128]{2,1,0:T(8,128)(2,1)}, bf16[2,512,128]{2,1,0:T(8,128)(2,1)S(1)}, u32[]{:S(2)}, u32[]{:S(2)}) %collective-permute-start.1) | collective-permute-done | bytes 262176 | tf_op jit(solution)/shard_map/ppermute | solution.py:22
  90.3 0.0 collective-permute-start.5
  90.3 0.0 collective-permute-done.2.refs_4_
  90.3 0.5 collective-permute-start.6
  90.8 0.1 copy.8.refs_0_
  90.9 0.0 collective-permute-done.9.refs_12_
  90.9 0.0 collective-permute-done.3.refs_5_
  90.9 0.0 collective-permute-done.4.refs_6_
  90.9 0.9 collective-permute-done.5.refs_7_
  91.9 0.4 collective-permute-done.6.refs_8_
  92.2 0.9 copy-done.2
  93.2 22.6 %attend.1 = (bf16[512,128]{1,0:T(8,128)(2,1)S(1)}, bf16[512,128]{1,0:T(8,128)(2,1)S(1)}, bf16[512,128]{1,0:T(8,128)(2,1)S(1)}, bf16[512,128]{1,0:T(8,128)(2,1)S(...) custom-call(s32[32,6]{1,0:T(8,128)S(1)} %copy.8.refs_0_, ...), custom_call_target="tpu_custom_call" | custom-call | flops 2684354560 | bytes 4194304 | tf_op jit(solution)/shard_map/attend/pallas_call | solution.py:210
  115.8 0.2 collective-permute-start.13
  116.0 1.5 collective-permute-start.10
  117.5 1.2 collective-permute-done.13
  118.7 1.0 fusion
  119.7 1.4 collective-permute-start.16
  121.1 1.5 collective-permute-start.15
  122.6 0.5 collective-permute-start.14
  123.2 0.0 collective-permute-start.11
  123.2 0.0 collective-permute-done.10.refs_1_
  123.2 2.9 %collective-permute-start.12 = (bf16[512,128]{1,0:T(8,128)(2,1)S(1)}, bf16[512,128]{1,0:T(8,128)(2,1)S(1)}, u32[]{:S(2)}, u32[]{:S(2)}) collective-permute-start(bf16[512,128]{1,0:T(8,128)(2,1)S(1)} %get-tuple-element.31), channel_id=1, source_target_pairs={{0,24},{4,28},{8,16},{12,20},{16,8},{20,12},{24,0},{28,4},{1,25},{... | collective-permute-start | bytes 393224 | tf_op jit(solution)/shard_map/ppermute | solution.py:22
  126.1 14.0 %collective-permute-done.11.refs_2_ = bf16[512,128]{1,0:T(8,128)(2,1)S(1)} collective-permute-done((bf16[512,128]{1,0:T(8,128)(2,1)S(1)}, bf16[512,128]{1,0:T(8,128)(2,1)S(1)}, u32[]{:S(2)}, u32[]{:S(2)}) %collective-permute-start.11) | collective-permute-done | bytes 131104 | tf_op jit(solution)/shard_map/ppermute | solution.py:22
  140.2 0.0 collective-permute-done.12.refs_3_
  140.2 0.0 collective-permute-done.16.refs_7_
  140.2 0.0 collective-permute-done.15.refs_6_
  140.2 0.0 collective-permute-done.14.refs_5_
  140.2 0.6 copy-done.7
  140.8 0.1 copy-done.8
  140.9 0.1 copy-done.3
  141.0 0.1 copy-done.4
  141.1 0.1 copy-done.5
  141.2 48.9 %join_heads.1 = (bf16[512,512]{1,0:T(8,128)(2,1)}, bf16[512,512]{1,0:T(8,128)(2,1)}, bf16[512,512]{1,0:T(8,128)(2,1)}) custom-call(bf16[512,128]{1,0:T(8,128)(2,1)} %copy-done, bf16[512,128]{1,0:T(8,128)(2,1)} %copy-done.6, bf16[512,128]{1,0:T(8,128)(2,1)} %copy-done.7, bf16[512,128]{1,0:T(8,128)(2,1)} %copy-done.8, ...), custom_call_target="tpu_custom_call" | custom-call | bytes 3145728 | tf_op jit(solution)/shard_map/join_heads/pallas_call | solution.py:84
  (14 shorter events, 0.0 us)
Async XLA Ops:
  33.6 41.0 %collective-permute-start.7 = (bf16[2,512,128]{2,1,0:T(8,128)(2,1)}, bf16[2,512,128]{2,1,0:T(8,128)(2,1)S(1)}, u32[]{:S(2)}, u32[]{:S(2)}) collective-permute-start(bf16[2,512,128]{2,1,0:T(8,128)(2,1)} %get-tuple-element.25), channel_id=1, source_target_pairs={{0,8},{4,12},{8,0},{12,4},{16,24},{20,28},{24,16},{28,20},{1,9},{5... | collective-permute-start | bytes 786440 | tf_op jit(solution)/shard_map/ppermute | solution.py:22
  36.6 38.0 %copy-start.10 = (bf16[2,512,128]{2,1,0:T(8,128)(2,1)S(1)}, bf16[2,512,128]{2,1,0:T(8,128)(2,1)}, u32[]{:S(2)}) copy-start(bf16[2,512,128]{2,1,0:T(8,128)(2,1)} %get-tuple-element.27) | copy-start | bytes 786436
  36.6 55.6 %copy-start.1 = (bf16[2,512,128]{2,1,0:T(8,128)(2,1)S(1)}, bf16[2,512,128]{2,1,0:T(8,128)(2,1)}, u32[]{:S(2)}) copy-start(bf16[2,512,128]{2,1,0:T(8,128)(2,1)} %get-tuple-element.24.refs_9_) | copy-start | bytes 786436
  36.6 38.1 %collective-permute-start.8 = (bf16[2,512,128]{2,1,0:T(8,128)(2,1)}, bf16[2,512,128]{2,1,0:T(8,128)(2,1)S(1)}, u32[]{:S(2)}, u32[]{:S(2)}) collective-permute-start(bf16[2,512,128]{2,1,0:T(8,128)(2,1)} %get-tuple-element.26), channel_id=1, source_target_pairs={{0,16},{4,20},{8,24},{12,28},{16,0},{20,4},{24,8},{28,12},{1,17},{... | collective-permute-start | bytes 786440 | tf_op jit(solution)/shard_map/ppermute | solution.py:22
  71.1 19.8 %copy-start.9 = (s32[32,6]{0,1:T(8,128)S(1)}, s32[32,6]{0,1:T(8,128)}, u32[]{:S(2)}) copy-start(s32[32,6]{0,1:T(8,128)} %param.9) | copy-start | bytes 2308
  71.1 9.5 %collective-permute-start = (bf16[2,512,128]{2,1,0:T(8,128)(2,1)}, bf16[2,512,128]{2,1,0:T(8,128)(2,1)S(1)}, u32[]{:S(2)}, u32[]{:S(2)}) collective-permute-start(bf16[2,512,128]{2,1,0:T(8,128)(2,1)} %get-tuple-element.21), channel_id=1, source_target_pairs={{0,8},{4,12},{8,0},{12,4},{16,24},{20,28},{24,16},{28,20},{1,9},{5... | collective-permute-start | bytes 786440 | tf_op jit(solution)/shard_map/ppermute | solution.py:22
  71.7 18.7 %collective-permute-start.1 = (bf16[2,512,128]{2,1,0:T(8,128)(2,1)}, bf16[2,512,128]{2,1,0:T(8,128)(2,1)S(1)}, u32[]{:S(2)}, u32[]{:S(2)}) collective-permute-start(bf16[2,512,128]{2,1,0:T(8,128)(2,1)} %get-tuple-element.22), channel_id=1, source_target_pairs={{0,16},{4,20},{8,24},{12,28},{16,0},{20,4},{24,8},{28,12},{1,17},{... | collective-permute-start | bytes 786440 | tf_op jit(solution)/shard_map/ppermute | solution.py:22
  71.7 18.6 %collective-permute-start.2 = (bf16[2,512,128]{2,1,0:T(8,128)(2,1)}, bf16[2,512,128]{2,1,0:T(8,128)(2,1)S(1)}, u32[]{:S(2)}, u32[]{:S(2)}) collective-permute-start(bf16[2,512,128]{2,1,0:T(8,128)(2,1)} %get-tuple-element.23), channel_id=1, source_target_pairs={{0,24},{4,28},{8,16},{12,20},{16,8},{20,12},{24,0},{28,4},{1,25},{... | collective-permute-start | bytes 786440 | tf_op jit(solution)/shard_map/ppermute | solution.py:22
  74.6 16.3 %collective-permute-start.9 = (bf16[2,512,128]{2,1,0:T(8,128)(2,1)S(1)}, bf16[2,512,128]{2,1,0:T(8,128)(2,1)S(1)}, u32[]{:S(2)}, u32[]{:S(2)}) collective-permute-start(bf16[2,512,128]{2,1,0:T(8,128)(2,1)S(1)} %copy-done.10), channel_id=1, source_target_pairs={{0,24},{4,28},{8,16},{12,20},{16,8},{20,12},{24,0},{28,4},{1,25},{... | collective-permute-start | bytes 786440 | tf_op jit(solution)/shard_map/ppermute | solution.py:22
  74.7 16.2 %collective-permute-start.3 = (bf16[2,512,128]{2,1,0:T(8,128)(2,1)}, bf16[2,512,128]{2,1,0:T(8,128)(2,1)S(1)}, u32[]{:S(2)}, u32[]{:S(2)}) collective-permute-start(bf16[2,512,128]{2,1,0:T(8,128)(2,1)} %get-tuple-element.20.refs_1_), channel_id=1, source_target_pairs={{0,4},{4,0},{8,12},{12,8},{16,20},{20,16},{24,28},{28,24},{1,5},{5... | collective-permute-start | bytes 786440 | tf_op jit(solution)/shard_map/ppermute | solution.py:22
  80.6 10.3 %collective-permute-start.4 = (bf16[2,512,128]{2,1,0:T(8,128)(2,1)S(1)}, bf16[2,512,128]{2,1,0:T(8,128)(2,1)S(1)}, u32[]{:S(2)}, u32[]{:S(2)}) collective-permute-start(bf16[2,512,128]{2,1,0:T(8,128)(2,1)S(1)} %collective-permute-done.refs_2_), channel_id=1, source_target_pairs={{0,4},{4,0},{8,12},{12,8},{16,20},{20,16},{24,28},{28,24},{1,5},{5... | collective-permute-start | bytes 786440 | tf_op jit(solution)/shard_map/ppermute | solution.py:22
  90.3 1.5 collective-permute-start.5
  90.3 1.9 %collective-permute-start.6 = (bf16[2,512,128]{2,1,0:T(8,128)(2,1)S(1)}, bf16[2,512,128]{2,1,0:T(8,128)(2,1)S(1)}, u32[]{:S(2)}, u32[]{:S(2)}) collective-permute-start(bf16[2,512,128]{2,1,0:T(8,128)(2,1)S(1)} %collective-permute-done.2.refs_4_), channel_id=1, source_target_pairs={{0,4},{4,0},{8,12},{12,8},{16,20},{20,16},{24,28},{28,24},{1,5},{5... | collective-permute-start | bytes 786440 | tf_op jit(solution)/shard_map/ppermute | solution.py:22
  92.2 1.0 copy-start.2
  115.8 3.9 %copy-start = (bf16[512,128]{1,0:T(8,128)(2,1)}, bf16[512,128]{1,0:T(8,128)(2,1)S(1)}, u32[]{:S(2)}) copy-start(bf16[512,128]{1,0:T(8,128)(2,1)S(1)} %get-tuple-element.28.refs_0_) | copy-start | bytes 393220
  115.8 2.9 %collective-permute-start.13 = (bf16[4,2,512,128]{3,2,1,0:T(8,128)(2,1)}, bf16[4,2,512,128]{3,2,1,0:T(8,128)(2,1)S(1)}, u32[]{:S(2)}, u32[]{:S(2)}) collective-permute-start(bf16[4,2,512,128]{3,2,1,0:T(8,128)(2,1)} %get-tuple-element.33), channel_id=1, source_target_pairs={{0,4},{4,0},{8,12},{12,8},{16,20},{20,16},{24,28},{28,24},{1,5},{5... | collective-permute-start | bytes 3145736 | tf_op jit(solution)/shard_map/ppermute | solution.py:22
  116.0 7.2 %collective-permute-start.10 = (bf16[512,128]{1,0:T(8,128)(2,1)S(1)}, bf16[512,128]{1,0:T(8,128)(2,1)S(1)}, u32[]{:S(2)}, u32[]{:S(2)}) collective-permute-start(bf16[512,128]{1,0:T(8,128)(2,1)S(1)} %get-tuple-element.29), channel_id=1, source_target_pairs={{0,8},{4,12},{8,0},{12,4},{16,24},{20,28},{24,16},{28,20},{1,9},{5... | collective-permute-start | bytes 393224 | tf_op jit(solution)/shard_map/ppermute | solution.py:22
  119.7 20.5 %collective-permute-start.16 = (bf16[2,512,128]{2,1,0:T(8,128)(2,1)S(1)}, bf16[2,512,128]{2,1,0:T(8,128)(2,1)S(1)}, u32[]{:S(2)}, u32[]{:S(2)}) collective-permute-start(bf16[2,512,128]{2,1,0:T(8,128)(2,1)S(1)} %get-tuple-element.37), channel_id=1, source_target_pairs={{0,24},{4,28},{8,16},{12,20},{16,8},{20,12},{24,0},{28,4},{1,25},{... | collective-permute-start | bytes 786440 | tf_op jit(solution)/shard_map/ppermute | solution.py:22
  121.1 19.1 %collective-permute-start.15 = (bf16[2,512,128]{2,1,0:T(8,128)(2,1)S(1)}, bf16[2,512,128]{2,1,0:T(8,128)(2,1)S(1)}, u32[]{:S(2)}, u32[]{:S(2)}) collective-permute-start(bf16[2,512,128]{2,1,0:T(8,128)(2,1)S(1)} %get-tuple-element.38), channel_id=1, source_target_pairs={{0,16},{4,20},{8,24},{12,28},{16,0},{20,4},{24,8},{28,12},{1,17},{... | collective-permute-start | bytes 786440 | tf_op jit(solution)/shard_map/ppermute | solution.py:22
  122.6 17.6 %collective-permute-start.14 = (bf16[2,512,128]{2,1,0:T(8,128)(2,1)S(1)}, bf16[2,512,128]{2,1,0:T(8,128)(2,1)S(1)}, u32[]{:S(2)}, u32[]{:S(2)}) collective-permute-start(bf16[2,512,128]{2,1,0:T(8,128)(2,1)S(1)} %get-tuple-element.39), channel_id=1, source_target_pairs={{0,8},{4,12},{8,0},{12,4},{16,24},{20,28},{24,16},{28,20},{1,9},{5... | collective-permute-start | bytes 786440 | tf_op jit(solution)/shard_map/ppermute | solution.py:22
  123.2 17.0 %collective-permute-start.11 = (bf16[512,128]{1,0:T(8,128)(2,1)S(1)}, bf16[512,128]{1,0:T(8,128)(2,1)S(1)}, u32[]{:S(2)}, u32[]{:S(2)}) collective-permute-start(bf16[512,128]{1,0:T(8,128)(2,1)S(1)} %get-tuple-element.30), channel_id=1, source_target_pairs={{0,16},{4,20},{8,24},{12,28},{16,0},{20,4},{24,8},{28,12},{1,17},{... | collective-permute-start | bytes 393224 | tf_op jit(solution)/shard_map/ppermute | solution.py:22
  123.2 17.0 %copy-start.6 = (bf16[512,128]{1,0:T(8,128)(2,1)}, bf16[512,128]{1,0:T(8,128)(2,1)S(1)}, u32[]{:S(2)}) copy-start(bf16[512,128]{1,0:T(8,128)(2,1)S(1)} %collective-permute-done.10.refs_1_) | copy-start | bytes 393220
  123.2 17.0 %collective-permute-start.12 = (bf16[512,128]{1,0:T(8,128)(2,1)S(1)}, bf16[512,128]{1,0:T(8,128)(2,1)S(1)}, u32[]{:S(2)}, u32[]{:S(2)}) collective-permute-start(bf16[512,128]{1,0:T(8,128)(2,1)S(1)} %get-tuple-element.31), channel_id=1, source_target_pairs={{0,24},{4,28},{8,16},{12,20},{16,8},{20,12},{24,0},{28,4},{1,25},{... | collective-permute-start | bytes 393224 | tf_op jit(solution)/shard_map/ppermute | solution.py:22
  140.2 0.6 copy-start.7
  140.2 0.7 copy-start.8
  140.2 0.8 copy-start.3
  140.2 0.9 copy-start.4
  140.2 0.9 copy-start.5
where the time goes:
time: 190 us
  Pallas kernels  137 us (72%)
  waiting for transfers between devices  32.2 us (17%)
  starting transfers between devices  16.8 us (9%)
  local copies, waits for them, and re-layouts  1.99 us (1%)
    pallas_call x2, Pallas kernels, split_heads(): pl.pallas_call(functools.partial(split_heads_kernel, members, groups), ou...  65.9 us
    pallas_call x1, Pallas kernels, join_heads(): pl.pallas_call(functools.partial(join_heads_kernel, members, groups), out...  48.9 us
    ppermute x17, waiting for transfers between devices, swapped(): return lax.ppermute(x, 'ctx', [(i, i ^ by) for i in range(count)])  32.2 us
    pallas_call x1, Pallas kernels, attend(): pl.pallas_call(functools.partial(attend_kernel, shards, members, groups,...  22.6 us
    ppermute x17, starting transfers between devices, swapped(): return lax.ppermute(x, 'ctx', [(i, i ^ by) for i in range(count)])  16.8 us
  transfers between devices with their start and end apart: 17, of which 6 were waited for; matrix products, arithmetic and copies ran while one was open for 1% of the time, Pallas kernels for 17%

commit v1 on v0

--- a/solution.py
+++ b/solution.py
@@ -24,32 +24,23 @@
 
 def split_heads_kernel(members, groups, *refs):
     first, second = refs[:2]
-    outs = refs[2 : 2 + groups]
-    sems = refs[2 + groups]
+    outs = refs[2:]
     chip = lax.axis_index("ctx") // members
-    copies = []
-    for s in range(groups):
-        column = pl.multiple_of((chip ^ s) * HEAD_DIM, HEAD_DIM)
-        for t, source in enumerate((first, second)):
-            copies.append(
-                pltpu.make_async_copy(
-                    source.at[:, pl.ds(column, HEAD_DIM)], outs[s].at[t], sems.at[2 * s + t]
-                )
-            )
-    for copy in copies:
-        copy.start()
-    for copy in copies:
-        copy.wait()
+    for s in range(groups):
+        column = pl.ds(pl.multiple_of((chip ^ s) * HEAD_DIM, HEAD_DIM), HEAD_DIM)
+        outs[s][0] = first[:, column]
+        outs[s][1] = second[:, column]
 
 
 def split_heads(first, second, members, groups):
     rows = first.shape[0]
+    vmem = pl.BlockSpec(memory_space=pltpu.VMEM)
     return pl.pallas_call(
         functools.partial(split_heads_kernel, members, groups),
         out_shape=[jax.ShapeDtypeStruct((2, rows, HEAD_DIM), first.dtype)] * groups,
-        in_specs=[pl.BlockSpec(memory_space=pl.ANY)] * 2,
-        out_specs=[pl.BlockSpec(memory_space=pl.ANY)] * groups,
-        scratch_shapes=[pltpu.SemaphoreType.DMA((2 * groups,))],
+        in_specs=[vmem] * 2,
+        out_specs=[vmem] * groups,
+        compiler_params=pltpu.CompilerParams(vmem_limit_bytes=VMEM_LIMIT),
         cost_estimate=pl.CostEstimate(
             flops=0, bytes_accessed=4 * first.size * first.dtype.itemsize, transcendentals=0
         ),
@@ -60,33 +51,25 @@
 def join_heads_kernel(members, groups, *refs):
     dq_parts = refs[:groups]
     pair_parts = refs[groups : 2 * groups]
-    outs = refs[2 * groups : 2 * groups + 3]
-    sems = refs[2 * groups + 3]
+    outs = refs[2 * groups :]
     chip = lax.axis_index("ctx") // members
-    copies = []
-    for s in range(groups):
-        column = pl.multiple_of((chip ^ s) * HEAD_DIM, HEAD_DIM)
-        for t, source in enumerate((dq_parts[s], pair_parts[s].at[0], pair_parts[s].at[1])):
-            copies.append(
-                pltpu.make_async_copy(
-                    source, outs[t].at[:, pl.ds(column, HEAD_DIM)], sems.at[3 * s + t]
-                )
-            )
-    for copy in copies:
-        copy.start()
-    for copy in copies:
-        copy.wait()
+    for s in range(groups):
+        column = pl.ds(pl.multiple_of((chip ^ s) * HEAD_DIM, HEAD_DIM), HEAD_DIM)
+        outs[0][:, column] = dq_parts[s][...]
+        outs[1][:, column] = pair_parts[s][0]
+        outs[2][:, column] = pair_parts[s][1]
 
 
 def join_heads(dq_parts, pair_parts, members, groups):
     rows = dq_parts[0].shape[0]
+    vmem = pl.BlockSpec(memory_space=pltpu.VMEM)
     out = jax.ShapeDtypeStruct((rows, groups * HEAD_DIM), jnp.bfloat16)
     return pl.pallas_call(
         functools.partial(join_heads_kernel, members, groups),
         out_shape=[out] * 3,
-        in_specs=[pl.BlockSpec(memory_space=pl.ANY)] * (2 * groups),
-        out_specs=[pl.BlockSpec(memory_space=pl.ANY)] * 3,
-        scratch_shapes=[pltpu.SemaphoreType.DMA((3 * groups,))],
+        in_specs=[vmem] * (2 * groups),
+        out_specs=[vmem] * 3,
+        compiler_params=pltpu.CompilerParams(vmem_limit_bytes=VMEM_LIMIT),
         cost_estimate=pl.CostEstimate(
             flops=0, bytes_accessed=12 * rows * groups * HEAD_DIM, transcendentals=0
         ),

time: 190 us -> 80.5 us (0.42)
  Pallas kernels: 137 us -> 24.4 us
  waiting for transfers between devices: 32.2 us -> 35.8 us
    pallas_call x2, Pallas kernels: 65.9 us -> 0.36 us  [split_heads(): pl.pallas_call(functools.partial(split_heads_kernel, members, groups), ou...]
    pallas_call x1, Pallas kernels: 48.9 us -> 1.42 us  [join_heads(): pl.pallas_call(functools.partial(join_heads_kernel, members, groups), out...]
    ppermute x17, waiting for transfers between devices: 32.2 us -> 35.8 us  [swapped(): return lax.ppermute(x, 'ctx', [(i, i ^ by) for i in range(count)])]
  transfers between devices with their start and end apart: 17 -> 17, of which waited for: 6 -> 7; matrix products, arithmetic and copies ran while one was open for 1% -> 0% of each run, Pallas kernels for 17% -> 0%
where the time goes in v1:
time: 80.5 us; the launch traced here: 80.3 us
  waiting for transfers between devices  35.8 us (44%)
  Pallas kernels  24.4 us (30%)
  starting transfers between devices  17 us (21%)
  local copies, waits for them, and re-layouts  2.18 us (3%)
    ppermute x17, waiting for transfers between devices, swapped(): return lax.ppermute(x, 'ctx', [(i, i ^ by) for i in range(count)])  35.8 us
    pallas_call x1, Pallas kernels, attend(): pl.pallas_call(functools.partial(attend_kernel, shards, members, groups,...  22.6 us
    ppermute x17, starting transfers between devices, swapped(): return lax.ppermute(x, 'ctx', [(i, i ^ by) for i in range(count)])  17 us
    unnamed x11, local copies, waits for them, and re-layouts  2.18 us
  transfers between devices with their start and end apart: 17, of which 7 were waited for; matrix products, arithmetic and copies ran while one was open for 0% of the time, Pallas kernels for 0%

profile of v1, /device:TPU:0, one launch (start us, length us, event | category | flops | bytes accessed | tf_op | source)
XLA Modules:
  0.0 80.3 jit_solution(4788656185979014456)
XLA Ops:
  0.6 0.0 copy-start
  0.6 1.0 %copy-done = bf16[512,512]{1,0:T(8,128)(2,1)S(1)} copy-done((bf16[512,512]{1,0:T(8,128)(2,1)S(1)}, bf16[512,512]{1,0:T(8,128)(2,1)}, u32[]{:S(2)}) %copy-start) | copy-done | bytes 524312
  1.7 0.0 copy-start.1
  1.7 1.0 %copy-done.1 = bf16[512,512]{1,0:T(8,128)(2,1)S(1)} copy-done((bf16[512,512]{1,0:T(8,128)(2,1)S(1)}, bf16[512,512]{1,0:T(8,128)(2,1)}, u32[]{:S(2)}) %copy-start.1) | copy-done | bytes 524312
  2.7 0.2 split_heads.3
  2.9 3.0 %collective-permute-start.7 = (bf16[2,512,128]{2,1,0:T(8,128)(2,1)S(1)}, bf16[2,512,128]{2,1,0:T(8,128)(2,1)S(1)}, u32[]{:S(2)}, u32[]{:S(2)}) collective-permute-start(bf16[2,512,128]{2,1,0:T(8,128)(2,1)S(1)} %get-tuple-element.25), channel_id=1, source_target_pairs={{0,8},{4,12},{8,0},{12,4},{16,24},{20,28},{24,16},{28,20},{1,9},{5... | collective-permute-start | bytes 786440 | tf_op jit(solution)/shard_map/ppermute | solution.py:22
  5.9 1.5 %collective-permute-start.8 = (bf16[2,512,128]{2,1,0:T(8,128)(2,1)S(1)}, bf16[2,512,128]{2,1,0:T(8,128)(2,1)S(1)}, u32[]{:S(2)}, u32[]{:S(2)}) collective-permute-start(bf16[2,512,128]{2,1,0:T(8,128)(2,1)S(1)} %get-tuple-element.26), channel_id=1, source_target_pairs={{0,16},{4,20},{8,24},{12,28},{16,0},{20,4},{24,8},{28,12},{1,17},{... | collective-permute-start | bytes 786440 | tf_op jit(solution)/shard_map/ppermute | solution.py:22
  7.4 0.0 copy-done.2
  7.4 0.0 copy-done.3
  7.4 0.2 split_heads.2
  7.6 0.0 copy-start.4
  7.6 0.6 collective-permute-start
  8.2 0.4 collective-permute-start.1
  8.6 2.6 %collective-permute-start.2 = (bf16[2,512,128]{2,1,0:T(8,128)(2,1)S(1)}, bf16[2,512,128]{2,1,0:T(8,128)(2,1)S(1)}, u32[]{:S(2)}, u32[]{:S(2)}) collective-permute-start(bf16[2,512,128]{2,1,0:T(8,128)(2,1)S(1)} %get-tuple-element.23), channel_id=1, source_target_pairs={{0,24},{4,28},{8,16},{12,20},{16,8},{20,12},{24,0},{28,4},{1,25},{... | collective-permute-start | bytes 786440 | tf_op jit(solution)/shard_map/ppermute | solution.py:22
  11.2 1.9 %collective-permute-done.7.refs_10_ = bf16[2,512,128]{2,1,0:T(8,128)(2,1)S(1)} collective-permute-done((bf16[2,512,128]{2,1,0:T(8,128)(2,1)S(1)}, bf16[2,512,128]{2,1,0:T(8,128)(2,1)S(1)}, u32[]{:S(2)}, u32[]{:S(2)}) %collective-permute-start.7) | collective-permute-done | bytes 262176 | tf_op jit(solution)/shard_map/ppermute | solution.py:22
  13.0 3.0 %collective-permute-start.9 = (bf16[2,512,128]{2,1,0:T(8,128)(2,1)S(1)}, bf16[2,512,128]{2,1,0:T(8,128)(2,1)S(1)}, u32[]{:S(2)}, u32[]{:S(2)}) collective-permute-start(bf16[2,512,128]{2,1,0:T(8,128)(2,1)S(1)} %get-tuple-element.27), channel_id=1, source_target_pairs={{0,24},{4,28},{8,16},{12,20},{16,8},{20,12},{24,0},{28,4},{1,25},{... | collective-permute-start | bytes 786440 | tf_op jit(solution)/shard_map/ppermute | solution.py:22
  16.1 0.0 collective-permute-done.8.refs_11_
  16.1 0.0 collective-permute-start.3
  16.1 2.6 %collective-permute-done.refs_2_ = bf16[2,512,128]{2,1,0:T(8,128)(2,1)S(1)} collective-permute-done((bf16[2,512,128]{2,1,0:T(8,128)(2,1)S(1)}, bf16[2,512,128]{2,1,0:T(8,128)(2,1)S(1)}, u32[]{:S(2)}, u32[]{:S(2)}) %collective-permute-start) | collective-permute-done | bytes 262176 | tf_op jit(solution)/shard_map/ppermute | solution.py:22
  18.7 0.0 collective-permute-start.4
  18.7 11.9 %collective-permute-done.1.refs_3_ = bf16[2,512,128]{2,1,0:T(8,128)(2,1)S(1)} collective-permute-done((bf16[2,512,128]{2,1,0:T(8,128)(2,1)S(1)}, bf16[2,512,128]{2,1,0:T(8,128)(2,1)S(1)}, u32[]{:S(2)}, u32[]{:S(2)}) %collective-permute-start.1) | collective-permute-done | bytes 262176 | tf_op jit(solution)/shard_map/ppermute | solution.py:22
  30.5 0.0 collective-permute-start.5
  30.5 0.0 collective-permute-done.2.refs_4_
  30.5 0.5 collective-permute-start.6
  31.0 0.0 copy-done.4
  31.0 0.1 copy.8.refs_0_
  31.1 0.0 collective-permute-done.9.refs_12_
  31.1 0.0 collective-permute-done.3.refs_5_
  31.1 0.0 collective-permute-done.4.refs_6_
  31.2 0.9 %collective-permute-done.5.refs_7_ = bf16[2,512,128]{2,1,0:T(8,128)(2,1)S(1)} collective-permute-done((bf16[2,512,128]{2,1,0:T(8,128)(2,1)S(1)}, bf16[2,512,128]{2,1,0:T(8,128)(2,1)S(1)}, u32[]{:S(2)}, u32[]{:S(2)}) %collective-permute-start.5) | collective-permute-done | bytes 262176 | tf_op jit(solution)/shard_map/ppermute | solution.py:22
  32.1 0.4 collective-permute-done.6.refs_8_
  32.4 22.6 %attend.1 = (bf16[512,128]{1,0:T(8,128)(2,1)S(1)}, bf16[512,128]{1,0:T(8,128)(2,1)S(1)}, bf16[512,128]{1,0:T(8,128)(2,1)S(1)}, bf16[512,128]{1,0:T(8,128)(2,1)S(...) custom-call(s32[32,6]{1,0:T(8,128)S(1)} %copy.8.refs_0_, ...), custom_call_target="tpu_custom_call" | custom-call | flops 2684354560 | bytes 4194304 | tf_op jit(solution)/shard_map/attend/pallas_call | solution.py:193
  55.0 0.2 collective-permute-start.13
  55.2 0.0 collective-permute-start.10
  55.3 2.7 %collective-permute-done.13 = bf16[4,2,512,128]{3,2,1,0:T(8,128)(2,1)S(1)} collective-permute-done((bf16[4,2,512,128]{3,2,1,0:T(8,128)(2,1)}, bf16[4,2,512,128]{3,2,1,0:T(8,128)(2,1)S(1)}, u32[]{:S(2)}, u32[]{:S(2)}) %collective-permute-start.13) | collective-permute-done | bytes 1048608 | tf_op jit(solution)/shard_map/ppermute | solution.py:22
  58.0 0.2 fusion
  58.2 1.6 %collective-permute-start.16 = (bf16[2,512,128]{2,1,0:T(8,128)(2,1)S(1)}, bf16[2,512,128]{2,1,0:T(8,128)(2,1)S(1)}, u32[]{:S(2)}, u32[]{:S(2)}) collective-permute-start(bf16[2,512,128]{2,1,0:T(8,128)(2,1)S(1)} %get-tuple-element.37), channel_id=1, source_target_pairs={{0,24},{4,28},{8,16},{12,20},{16,8},{20,12},{24,0},{28,4},{1,25},{... | collective-permute-start | bytes 786440 | tf_op jit(solution)/shard_map/ppermute | solution.py:22
  59.8 0.1 collective-permute-start.15
  59.9 1.9 %collective-permute-start.14 = (bf16[2,512,128]{2,1,0:T(8,128)(2,1)S(1)}, bf16[2,512,128]{2,1,0:T(8,128)(2,1)S(1)}, u32[]{:S(2)}, u32[]{:S(2)}) collective-permute-start(bf16[2,512,128]{2,1,0:T(8,128)(2,1)S(1)} %get-tuple-element.39), channel_id=1, source_target_pairs={{0,8},{4,12},{8,0},{12,4},{16,24},{20,28},{24,16},{28,20},{1,9},{5... | collective-permute-start | bytes 786440 | tf_op jit(solution)/shard_map/ppermute | solution.py:22
  61.7 1.5 %collective-permute-start.11 = (bf16[512,128]{1,0:T(8,128)(2,1)S(1)}, bf16[512,128]{1,0:T(8,128)(2,1)S(1)}, u32[]{:S(2)}, u32[]{:S(2)}) collective-permute-start(bf16[512,128]{1,0:T(8,128)(2,1)S(1)} %get-tuple-element.30), channel_id=1, source_target_pairs={{0,16},{4,20},{8,24},{12,28},{16,0},{20,4},{24,8},{28,12},{1,17},{... | collective-permute-start | bytes 393224 | tf_op jit(solution)/shard_map/ppermute | solution.py:22
  63.3 0.0 collective-permute-done.10.refs_1_
  63.3 0.1 collective-permute-start.12
  63.4 15.5 %collective-permute-done.11.refs_2_ = bf16[512,128]{1,0:T(8,128)(2,1)S(1)} collective-permute-done((bf16[512,128]{1,0:T(8,128)(2,1)S(1)}, bf16[512,128]{1,0:T(8,128)(2,1)S(1)}, u32[]{:S(2)}, u32[]{:S(2)}) %collective-permute-start.11) | collective-permute-done | bytes 131104 | tf_op jit(solution)/shard_map/ppermute | solution.py:22
  78.8 0.0 collective-permute-done.12.refs_3_
  78.8 0.0 collective-permute-done.16.refs_7_
  78.8 0.0 collective-permute-done.15.refs_6_
  78.8 0.0 collective-permute-done.14.refs_5_
  78.9 1.4 %join_heads.1 = (bf16[512,512]{1,0:T(8,128)(2,1)}, bf16[512,512]{1,0:T(8,128)(2,1)}, bf16[512,512]{1,0:T(8,128)(2,1)}) custom-call(bf16[512,128]{1,0:T(8,128)(2,1)S(1)} %get-tuple-element.28.refs_0_, bf16[512,128]{1,0:T(8,128)(2,1)S(1)} %collective-permute-done.10.refs_1_, bf16[512,128]{1,0:T(8,128)(2,1)S(1)} %collective-permute-done.11.refs_2_, ...), custom_call_target="tpu_custom_call" | custom-call | bytes 3145728 | tf_op jit(solution)/shard_map/join_heads/pallas_call | solution.py:67
  (2 shorter events, 0.0 us)
Async XLA Ops:
  0.6 1.0 %copy-start = (bf16[512,512]{1,0:T(8,128)(2,1)S(1)}, bf16[512,512]{1,0:T(8,128)(2,1)}, u32[]{:S(2)}) copy-start(bf16[512,512]{1,0:T(8,128)(2,1)} %refs_0_.4) | copy-start | bytes 1572868
  1.7 1.0 %copy-start.1 = (bf16[512,512]{1,0:T(8,128)(2,1)S(1)}, bf16[512,512]{1,0:T(8,128)(2,1)}, u32[]{:S(2)}) copy-start(bf16[512,512]{1,0:T(8,128)(2,1)} %refs_1_.3) | copy-start | bytes 1572868
  2.7 4.7 %copy-start.2 = (bf16[512,512]{1,0:T(8,128)(2,1)S(1)}, bf16[512,512]{1,0:T(8,128)(2,1)}, u32[]{:S(2)}) copy-start(bf16[512,512]{1,0:T(8,128)(2,1)} %refs_0_.3) | copy-start | bytes 1572868
  2.7 4.7 %copy-start.3 = (bf16[512,512]{1,0:T(8,128)(2,1)S(1)}, bf16[512,512]{1,0:T(8,128)(2,1)}, u32[]{:S(2)}) copy-start(bf16[512,512]{1,0:T(8,128)(2,1)} %refs_1_.2) | copy-start | bytes 1572868
  2.9 10.1 %collective-permute-start.7 = (bf16[2,512,128]{2,1,0:T(8,128)(2,1)S(1)}, bf16[2,512,128]{2,1,0:T(8,128)(2,1)S(1)}, u32[]{:S(2)}, u32[]{:S(2)}) collective-permute-start(bf16[2,512,128]{2,1,0:T(8,128)(2,1)S(1)} %get-tuple-element.25), channel_id=1, source_target_pairs={{0,8},{4,12},{8,0},{12,4},{16,24},{20,28},{24,16},{28,20},{1,9},{5... | collective-permute-start | bytes 786440 | tf_op jit(solution)/shard_map/ppermute | solution.py:22
  5.9 10.2 %collective-permute-start.8 = (bf16[2,512,128]{2,1,0:T(8,128)(2,1)S(1)}, bf16[2,512,128]{2,1,0:T(8,128)(2,1)S(1)}, u32[]{:S(2)}, u32[]{:S(2)}) collective-permute-start(bf16[2,512,128]{2,1,0:T(8,128)(2,1)S(1)} %get-tuple-element.26), channel_id=1, source_target_pairs={{0,16},{4,20},{8,24},{12,28},{16,0},{20,4},{24,8},{28,12},{1,17},{... | collective-permute-start | bytes 786440 | tf_op jit(solution)/shard_map/ppermute | solution.py:22
  7.6 23.4 %copy-start.4 = (s32[32,6]{0,1:T(8,128)S(1)}, s32[32,6]{0,1:T(8,128)}, u32[]{:S(2)}) copy-start(s32[32,6]{0,1:T(8,128)} %param.9) | copy-start | bytes 2308
  7.6 11.0 %collective-permute-start = (bf16[2,512,128]{2,1,0:T(8,128)(2,1)S(1)}, bf16[2,512,128]{2,1,0:T(8,128)(2,1)S(1)}, u32[]{:S(2)}, u32[]{:S(2)}) collective-permute-start(bf16[2,512,128]{2,1,0:T(8,128)(2,1)S(1)} %get-tuple-element.21), channel_id=1, source_target_pairs={{0,8},{4,12},{8,0},{12,4},{16,24},{20,28},{24,16},{28,20},{1,9},{5... | collective-permute-start | bytes 786440 | tf_op jit(solution)/shard_map/ppermute | solution.py:22
  8.2 22.3 %collective-permute-start.1 = (bf16[2,512,128]{2,1,0:T(8,128)(2,1)S(1)}, bf16[2,512,128]{2,1,0:T(8,128)(2,1)S(1)}, u32[]{:S(2)}, u32[]{:S(2)}) collective-permute-start(bf16[2,512,128]{2,1,0:T(8,128)(2,1)S(1)} %get-tuple-element.22), channel_id=1, source_target_pairs={{0,16},{4,20},{8,24},{12,28},{16,0},{20,4},{24,8},{28,12},{1,17},{... | collective-permute-start | bytes 786440 | tf_op jit(solution)/shard_map/ppermute | solution.py:22
  8.6 21.9 %collective-permute-start.2 = (bf16[2,512,128]{2,1,0:T(8,128)(2,1)S(1)}, bf16[2,512,128]{2,1,0:T(8,128)(2,1)S(1)}, u32[]{:S(2)}, u32[]{:S(2)}) collective-permute-start(bf16[2,512,128]{2,1,0:T(8,128)(2,1)S(1)} %get-tuple-element.23), channel_id=1, source_target_pairs={{0,24},{4,28},{8,16},{12,20},{16,8},{20,12},{24,0},{28,4},{1,25},{... | collective-permute-start | bytes 786440 | tf_op jit(solution)/shard_map/ppermute | solution.py:22
  13.0 18.1 %collective-permute-start.9 = (bf16[2,512,128]{2,1,0:T(8,128)(2,1)S(1)}, bf16[2,512,128]{2,1,0:T(8,128)(2,1)S(1)}, u32[]{:S(2)}, u32[]{:S(2)}) collective-permute-start(bf16[2,512,128]{2,1,0:T(8,128)(2,1)S(1)} %get-tuple-element.27), channel_id=1, source_target_pairs={{0,24},{4,28},{8,16},{12,20},{16,8},{20,12},{24,0},{28,4},{1,25},{... | collective-permute-start | bytes 786440 | tf_op jit(solution)/shard_map/ppermute | solution.py:22
  16.1 15.1 %collective-permute-start.3 = (bf16[2,512,128]{2,1,0:T(8,128)(2,1)S(1)}, bf16[2,512,128]{2,1,0:T(8,128)(2,1)S(1)}, u32[]{:S(2)}, u32[]{:S(2)}) collective-permute-start(bf16[2,512,128]{2,1,0:T(8,128)(2,1)S(1)} %get-tuple-element.20.refs_1_), channel_id=1, source_target_pairs={{0,4},{4,0},{8,12},{12,8},{16,20},{20,16},{24,28},{28,24},{1,5},{5... | collective-permute-start | bytes 786440 | tf_op jit(solution)/shard_map/ppermute | solution.py:22
  18.7 12.5 %collective-permute-start.4 = (bf16[2,512,128]{2,1,0:T(8,128)(2,1)S(1)}, bf16[2,512,128]{2,1,0:T(8,128)(2,1)S(1)}, u32[]{:S(2)}, u32[]{:S(2)}) collective-permute-start(bf16[2,512,128]{2,1,0:T(8,128)(2,1)S(1)} %collective-permute-done.refs_2_), channel_id=1, source_target_pairs={{0,4},{4,0},{8,12},{12,8},{16,20},{20,16},{24,28},{28,24},{1,5},{5... | collective-permute-start | bytes 786440 | tf_op jit(solution)/shard_map/ppermute | solution.py:22
  30.5 1.5 %collective-permute-start.5 = (bf16[2,512,128]{2,1,0:T(8,128)(2,1)S(1)}, bf16[2,512,128]{2,1,0:T(8,128)(2,1)S(1)}, u32[]{:S(2)}, u32[]{:S(2)}) collective-permute-start(bf16[2,512,128]{2,1,0:T(8,128)(2,1)S(1)} %collective-permute-done.1.refs_3_), channel_id=1, source_target_pairs={{0,4},{4,0},{8,12},{12,8},{16,20},{20,16},{24,28},{28,24},{1,5},{5... | collective-permute-start | bytes 786440 | tf_op jit(solution)/shard_map/ppermute | solution.py:22
  30.5 1.9 %collective-permute-start.6 = (bf16[2,512,128]{2,1,0:T(8,128)(2,1)S(1)}, bf16[2,512,128]{2,1,0:T(8,128)(2,1)S(1)}, u32[]{:S(2)}, u32[]{:S(2)}) collective-permute-start(bf16[2,512,128]{2,1,0:T(8,128)(2,1)S(1)} %collective-permute-done.2.refs_4_), channel_id=1, source_target_pairs={{0,4},{4,0},{8,12},{12,8},{16,20},{20,16},{24,28},{28,24},{1,5},{5... | collective-permute-start | bytes 786440 | tf_op jit(solution)/shard_map/ppermute | solution.py:22
  55.0 2.9 %collective-permute-start.13 = (bf16[4,2,512,128]{3,2,1,0:T(8,128)(2,1)}, bf16[4,2,512,128]{3,2,1,0:T(8,128)(2,1)S(1)}, u32[]{:S(2)}, u32[]{:S(2)}) collective-permute-start(bf16[4,2,512,128]{3,2,1,0:T(8,128)(2,1)} %get-tuple-element.33), channel_id=1, source_target_pairs={{0,4},{4,0},{8,12},{12,8},{16,20},{20,16},{24,28},{28,24},{1,5},{5... | collective-permute-start | bytes 3145736 | tf_op jit(solution)/shard_map/ppermute | solution.py:22
  55.2 8.0 %collective-permute-start.10 = (bf16[512,128]{1,0:T(8,128)(2,1)S(1)}, bf16[512,128]{1,0:T(8,128)(2,1)S(1)}, u32[]{:S(2)}, u32[]{:S(2)}) collective-permute-start(bf16[512,128]{1,0:T(8,128)(2,1)S(1)} %get-tuple-element.29), channel_id=1, source_target_pairs={{0,8},{4,12},{8,0},{12,4},{16,24},{20,28},{24,16},{28,20},{1,9},{5... | collective-permute-start | bytes 393224 | tf_op jit(solution)/shard_map/ppermute | solution.py:22
  58.2 20.6 %collective-permute-start.16 = (bf16[2,512,128]{2,1,0:T(8,128)(2,1)S(1)}, bf16[2,512,128]{2,1,0:T(8,128)(2,1)S(1)}, u32[]{:S(2)}, u32[]{:S(2)}) collective-permute-start(bf16[2,512,128]{2,1,0:T(8,128)(2,1)S(1)} %get-tuple-element.37), channel_id=1, source_target_pairs={{0,24},{4,28},{8,16},{12,20},{16,8},{20,12},{24,0},{28,4},{1,25},{... | collective-permute-start | bytes 786440 | tf_op jit(solution)/shard_map/ppermute | solution.py:22
  59.8 19.1 %collective-permute-start.15 = (bf16[2,512,128]{2,1,0:T(8,128)(2,1)S(1)}, bf16[2,512,128]{2,1,0:T(8,128)(2,1)S(1)}, u32[]{:S(2)}, u32[]{:S(2)}) collective-permute-start(bf16[2,512,128]{2,1,0:T(8,128)(2,1)S(1)} %get-tuple-element.38), channel_id=1, source_target_pairs={{0,16},{4,20},{8,24},{12,28},{16,0},{20,4},{24,8},{28,12},{1,17},{... | collective-permute-start | bytes 786440 | tf_op jit(solution)/shard_map/ppermute | solution.py:22
  59.9 19.0 %collective-permute-start.14 = (bf16[2,512,128]{2,1,0:T(8,128)(2,1)S(1)}, bf16[2,512,128]{2,1,0:T(8,128)(2,1)S(1)}, u32[]{:S(2)}, u32[]{:S(2)}) collective-permute-start(bf16[2,512,128]{2,1,0:T(8,128)(2,1)S(1)} %get-tuple-element.39), channel_id=1, source_target_pairs={{0,8},{4,12},{8,0},{12,4},{16,24},{20,28},{24,16},{28,20},{1,9},{5... | collective-permute-start | bytes 786440 | tf_op jit(solution)/shard_map/ppermute | solution.py:22
  61.7 17.1 %collective-permute-start.11 = (bf16[512,128]{1,0:T(8,128)(2,1)S(1)}, bf16[512,128]{1,0:T(8,128)(2,1)S(1)}, u32[]{:S(2)}, u32[]{:S(2)}) collective-permute-start(bf16[512,128]{1,0:T(8,128)(2,1)S(1)} %get-tuple-element.30), channel_id=1, source_target_pairs={{0,16},{4,20},{8,24},{12,28},{16,0},{20,4},{24,8},{28,12},{1,17},{... | collective-permute-start | bytes 393224 | tf_op jit(solution)/shard_map/ppermute | solution.py:22
  63.3 15.6 %collective-permute-start.12 = (bf16[512,128]{1,0:T(8,128)(2,1)S(1)}, bf16[512,128]{1,0:T(8,128)(2,1)S(1)}, u32[]{:S(2)}, u32[]{:S(2)}) collective-permute-start(bf16[512,128]{1,0:T(8,128)(2,1)S(1)} %get-tuple-element.31), channel_id=1, source_target_pairs={{0,24},{4,28},{8,16},{12,20},{16,8},{20,12},{24,0},{28,4},{1,25},{... | collective-permute-start | bytes 393224 | tf_op jit(solution)/shard_map/ppermute | solution.py:22

commit v2 on v1

v2 whole, which is shorter than its diff:
```python
import functools
import math

import jax
import jax.numpy as jnp
from jax import lax
from jax.experimental import pallas as pl
from jax.experimental.pallas import tpu as pltpu
from jax.sharding import PartitionSpec as P

HEAD_DIM = 128
BLK = 128
WIN = 2
LINKS = 6
SPAN = WIN + LINKS
NEG_FILL = -1e30
VMEM_LIMIT = 24 * 1024 * 1024
FAR_LIMIT = 40 * 1024 * 1024
SPLIT_LIMIT = 56 * 1024 * 1024
SMALL_LIMIT = 16 * 1024 * 1024


def swapped(x, by):
    count = lax.axis_size("ctx")
    return lax.ppermute(x, "ctx", [(i, i ^ by) for i in range(count)])


def chip_column(members, s):
    chip = lax.div(lax.axis_index("ctx"), members)
    return pl.ds(pl.multiple_of((chip ^ s) * HEAD_DIM, HEAD_DIM), HEAD_DIM)


def all_started(moves, sems):
    copies = [
        pltpu.make_async_copy(source, target, sems.at[i])
        for i, (source, target) in enumerate(moves)
    ]
    for copy in copies:
        copy.start()
    return copies


def split_heads_kernel(which, members, groups, *refs):
    query, key, value, grad = refs[:4]
    outs = refs[4:-1]
    half = query.shape[0] // 2
    taken = pl.ds(which * half, half)
    moves = []
    for s in range(groups):
        column = chip_column(members, s)
        for t, (pair, ask) in enumerate(((key, query), (value, grad))):
            lanes = pl.ds(t * HEAD_DIM, HEAD_DIM)
            moves.append((pair.at[taken, column], outs[s].at[pl.ds(0, half), lanes]))
            moves.append((ask.at[taken, column], outs[s].at[pl.ds(half, half), lanes]))
    for copy in all_started(moves, refs[-1]):
        copy.wait()


def split_heads(which, arrays, members, groups):
    rows = arrays[0].shape[0]
    out = jax.ShapeDtypeStruct((rows, 2 * HEAD_DIM), jnp.bfloat16)
    return pl.pallas_call(
        functools.partial(split_heads_kernel, which, members, groups),
        out_shape=[out] * groups,
        in_specs=[pl.BlockSpec(memory_space=pl.ANY)] * len(arrays),
        out_specs=[pl.BlockSpec(memory_space=pltpu.VMEM)] * groups,
        scratch_shapes=[pltpu.SemaphoreType.DMA((4 * groups,))],
        compiler_params=pltpu.CompilerParams(vmem_limit_bytes=SPLIT_LIMIT),
        cost_estimate=pl.CostEstimate(
            flops=0, bytes_accessed=8 * groups * rows * HEAD_DIM, transcendentals=0
        ),
        name="split_late" if which else "split_early",
    )(*arrays)


def join_heads_kernel(members, groups, *refs):
    parts = refs[:groups]
    outs = refs[groups:]
    rows = outs[0].shape[0]
    for s in range(groups):
        column = chip_column(members, s)
        for n in range(rows // BLK):
            at = slice(n * BLK, (n + 1) * BLK)
            packed = rows + n // 2 * BLK
            lanes = slice(n % 2 * HEAD_DIM, (n % 2 + 1) * HEAD_DIM)
            outs[0][at, column] = parts[s][packed : packed + BLK, lanes]
            outs[1][at, column] = parts[s][at, :HEAD_DIM]
            outs[2][at, column] = parts[s][at, HEAD_DIM:]


def join_heads(parts, rows, members, groups):
    vmem = pl.BlockSpec(memory_space=pltpu.VMEM)
    out = jax.ShapeDtypeStruct((rows, groups * HEAD_DIM), jnp.bfloat16)
    return pl.pallas_call(
        functools.partial(join_heads_kernel, members, groups),
        out_shape=[out] * 3,
        in_specs=[vmem] * groups,
        out_specs=[vmem] * 3,
        compiler_params=pltpu.CompilerParams(vmem_limit_bytes=SMALL_LIMIT),
        cost_estimate=pl.CostEstimate(
            flops=0, bytes_accessed=12 * rows * groups * HEAD_DIM, transcendentals=0
        ),
        name="join_heads",
    )(*parts)


def add_kernel(members, groups, *refs):
    far = refs[:  members - 1]
    own, dq_early, dq_late = (
        refs[members - 1 + i * groups : members - 1 + (i + 1) * groups] for i in range(3)
    )
    outs = refs[members - 1 + 3 * groups :]
    rows = own[0].shape[0]
    quarter = rows // 4
    for s in range(groups):
        total = own[s][...].astype(jnp.float32)
        for part in far:
            total = total + part[s].astype(jnp.float32)
        outs[s][:rows, :HEAD_DIM] = (total[:, :HEAD_DIM] * HEAD_DIM**-0.5).astype(jnp.bfloat16)
        outs[s][:rows, HEAD_DIM:] = total[:, HEAD_DIM:].astype(jnp.bfloat16)
        outs[s][rows : rows + quarter] = dq_early[s][...]
        outs[s][rows + quarter :] = dq_late[s][...]


def add_partials(far, own, dq_early, dq_late, members, groups):
    vmem = pl.BlockSpec(memory_space=pltpu.VMEM)
    rows = own[0].shape[0]
    out = jax.ShapeDtypeStruct((rows + rows // 2, 2 * HEAD_DIM), jnp.bfloat16)
    given = [*far, *own, *dq_early, *dq_late]
    return pl.pallas_call(
        functools.partial(add_kernel, members, groups),
        out_shape=[out] * groups,
        in_specs=[vmem] * len(given),
        out_specs=[vmem] * groups,
        compiler_params=pltpu.CompilerParams(vmem_limit_bytes=SMALL_LIMIT),
        cost_estimate=pl.CostEstimate(
            flops=0, bytes_accessed=8 * groups * rows * HEAD_DIM, transcendentals=0
        ),
        name="add_partials",
    )(*given)


def dot(left, right, dims):
    return lax.dot_general(left, right, (dims, ((), ())), preferred_element_type=jnp.float32)


def attend_kernel(late, near, shards, members, groups, half, *refs):
    slots = members * groups
    halves = 2 if late else 1
    held = halves * half
    stretch = half // BLK
    links = refs[0]
    packs = [refs[1 + h * slots : 1 + (h + 1) * slots] for h in range(halves)]
    refs = refs[1 + halves * slots :]
    if late:
        sums_in = refs[0]
        refs = refs[1:]
    dq_outs = refs[:groups]
    refs = refs[groups:]
    if late:
        own_outs = refs[:groups]
        far_outs = refs[groups : groups + members - 1]
        pair_buf, ask_buf, dq_buf, sems, acc = refs[groups + members - 1 :]
    else:
        acc, pair_buf, ask_buf, dq_buf, sems = refs
    device = lax.axis_index("ctx")

    moves = []
    for h in range(halves):
        for i in range(slots):
            place = pl.ds(i * held + h * half, half)
            moves.append((packs[h][i].at[pl.ds(0, half)], pair_buf.at[place]))
            if late and h == 0:
                moves.append((sums_in.at[pl.ds(i * half, half)], acc.at[place]))
            else:
                acc[place, :] = jnp.zeros((half, 2 * HEAD_DIM), jnp.float32)
    for s in range(groups):
        place = pl.ds(s * half, half)
        moves.append((packs[-1][s].at[pl.ds(half, half)], ask_buf.at[place]))
    if near:
        for source, target in moves:
            target[...] = source[...]
    else:
        for copy in all_started(moves, sems):
            copy.wait()

    scaling = HEAD_DIM**-0.5
    causal = lax.broadcasted_iota(jnp.int32, (BLK, BLK), 0) <= lax.broadcasted_iota(
        jnp.int32, (BLK, BLK), 1
    )
    blank = jnp.zeros((BLK, HEAD_DIM), jnp.bfloat16)

    def place_of(block):
        run = lax.div(block, stretch)
        local = block - run * stretch
        owner = run
        if late:
            is_late = run >= shards
            owner = jnp.where(is_late, 2 * shards - 1 - run, run)
            local = local + jnp.where(is_late, stretch, 0)
        apart = owner ^ device
        slot = lax.rem(apart, members) * groups + lax.div(apart, members)
        return pl.multiple_of(slot * held + local * BLK, BLK)

    def step(s, _):
        asker = device ^ (s * members)
        first = (2 * shards - 1 - asker if late else asker) * stretch
        units = range(stretch)
        listed = []
        for n in units:
            block = first + n
            listed.append([block, block - 1] + [links[block, i] for i in range(LINKS)])
        places = [[place_of(jnp.maximum(j, 0)) for j in row] for row in listed]
        pairs = [jnp.concatenate([pair_buf[pl.ds(p, BLK), :] for p in row], 0) for row in places]
        wide = []
        for n in units:
            ask = ask_buf[pl.ds(pl.multiple_of(s * half + n * BLK, BLK), BLK), :]
            wide.append(
                jnp.concatenate(
                    [
                        jnp.concatenate([ask[:, :HEAD_DIM], blank], 1),
                        jnp.concatenate([blank, ask[:, HEAD_DIM:]], 1),
                    ],
                    0,
                )
            )
        both = [dot(pairs[n], wide[n], ((1,), (1,))) for n in units]
        dscore_b, terms = [], []
        for n in units:
            raw = [both[n][i * BLK : (i + 1) * BLK, :BLK] for i in range(SPAN)]
            dprob = both[n][:, BLK:].reshape(SPAN, BLK, BLK)
            raw[0] = jnp.where(causal, raw[0], NEG_FILL)
            unused = [0.0] + [jnp.where(j >= 0, 0.0, NEG_FILL) for j in listed[n][1:]]
            tops = [jnp.max(raw[i], axis=0, keepdims=True) + unused[i] for i in range(SPAN)]
            top = functools.reduce(jnp.maximum, tops)
            weight = jnp.stack(
                [
                    jnp.exp2((raw[i] - (top - unused[i])) * (scaling * math.log2(math.e)))
                    for i in range(SPAN)
                ]
            )
            share = 1.0 / jnp.sum(weight, axis=(0, 1), keepdims=True)
            delta = jnp.sum(weight * dprob, axis=(0, 1), keepdims=True) * share
            prob = weight * share
            dscore = (prob * (dprob - delta)).astype(jnp.bfloat16).reshape(SPAN * BLK, BLK)
            dscore_b.append(dscore)
            prob = prob.astype(jnp.bfloat16).reshape(SPAN * BLK, BLK)
            terms.append(dot(jnp.concatenate([dscore, prob], 1), wide[n], ((1,), (0,))))
        dq = [dot(dscore_b[n], pairs[n][:, :HEAD_DIM], ((0,), (0,))) * scaling for n in units]
        for n in units:
            lanes = slice(n % 2 * HEAD_DIM, (n % 2 + 1) * HEAD_DIM)
            packed = pl.ds(pl.multiple_of(s * (half // 2) + n // 2 * BLK, BLK), BLK)
            dq_buf[packed, lanes] = dq[n].astype(jnp.bfloat16)
            for i, p in enumerate(places[n]):
                acc[pl.ds(p, BLK), :] += terms[n][i * BLK : (i + 1) * BLK]
        return 0

    lax.fori_loop(0, groups, step, 0)

    for s in range(groups):
        dq_outs[s][...] = dq_buf[s * (half // 2) : (s + 1) * (half // 2), :]
    if late:
        for s in range(groups):
            own_outs[s][...] = acc[s * held : (s + 1) * held, :].astype(jnp.bfloat16)
        for r in range(1, members):
            for s in range(groups):
                start = (r * groups + s) * held
                far_outs[r - 1][s] = acc[start : start + held, :].astype(jnp.bfloat16)


def attend(links, packs, sums, shards, members, groups):
    late = sums is not None
    half = packs[0][0].shape[0] // 2
    slots = members * groups
    held = half * len(packs)
    blocks = groups * half // BLK
    given = [pack for part in packs for pack in part] + ([sums] if late else [])
    dq = jax.ShapeDtypeStruct((half // 2, 2 * HEAD_DIM), jnp.bfloat16)
    outs = [dq] * groups
    scratch = [
        pltpu.VMEM((slots * held, 2 * HEAD_DIM), jnp.bfloat16),
        pltpu.VMEM((groups * half, 2 * HEAD_DIM), jnp.bfloat16),
        pltpu.VMEM((groups * half // 2, 2 * HEAD_DIM), jnp.bfloat16),
        pltpu.SemaphoreType.DMA((3 * slots + groups,)),
    ]
    if late:
        outs += [jax.ShapeDtypeStruct((held, 2 * HEAD_DIM), jnp.bfloat16)] * groups
        far = jax.ShapeDtypeStruct((groups, held, 2 * HEAD_DIM), jnp.bfloat16)
        outs += [far] * (members - 1)
        scratch += [pltpu.VMEM((slots * held, 2 * HEAD_DIM), jnp.float32)]
    else:
        outs += [jax.ShapeDtypeStruct((slots * held, 2 * HEAD_DIM), jnp.float32)]
    near = slots * half <= 4096
    vmem = pl.BlockSpec(memory_space=pltpu.VMEM)
    found = pl.pallas_call(
        functools.partial(attend_kernel, late, near, shards, members, groups, half),
        out_shape=outs,
        in_specs=[pl.BlockSpec(memory_space=pltpu.SMEM)]
        + [vmem if near else pl.BlockSpec(memory_space=pl.ANY)] * len(given),
        out_specs=[vmem] * len(outs),
        scratch_shapes=scratch,
        compiler_params=pltpu.CompilerParams(vmem_limit_bytes=VMEM_LIMIT if near else FAR_LIMIT),
        cost_estimate=pl.CostEstimate(
            flops=10 * blocks * SPAN * BLK * BLK * HEAD_DIM,
            bytes_accessed=8 * slots * held * HEAD_DIM,
            transcendentals=blocks * SPAN * BLK * BLK,
        ),
        name="attend_late" if late else "attend_early",
    )(links, *given)
    if late:
        return found[:groups], found[groups : 2 * groups], found[2 * groups :]
    return found[:groups], found[groups]


def to_chips(parts, members):
    return [parts[0]] + [swapped(part, s * members) for s, part in enumerate(parts[1:], 1)]


def with_members(parts, members):
    return parts + [swapped(part, r) for r in range(1, members) for part in parts]


def per_device(query, key, value, out_grad, links):
    rows, width = query.shape
    groups = width // HEAD_DIM
    shards = lax.axis_size("ctx")
    members = shards // groups
    arrays = (query, key, value, out_grad)

    early = with_members(to_chips(split_heads(0, arrays, members, groups), members), members)
    late = with_members(to_chips(split_heads(1, arrays, members, groups), members), members)
    dq_early, sums = attend(links, [early], None, shards, members, groups)
    dq_late, own, far = attend(links, [early, late], sums, shards, members, groups)
    far = [swapped(part, r) for r, part in enumerate(far, 1)]
    parts = add_partials(far, own, dq_early, dq_late, members, groups)
    return tuple(join_heads(to_chips(parts, members), rows, members, groups))


def solution(mesh):
    return jax.shard_map(
        per_device,
        mesh=mesh,
        in_specs=(P("ctx", "head"), P("ctx", "head"), P("ctx", "head"), P("ctx", "head"), P()),
        out_specs=(P("ctx", "head"), P("ctx", "head"), P("ctx", "head")),
        check_vma=False,
    )
```

time: 80.5 us -> 73.7 us (0.916)
  Pallas kernels: 24.4 us -> 20.9 us
  waiting for transfers between devices: 35.8 us -> 34.6 us
  local copies, waits for them, and re-layouts: 2.18 us -> 1.05 us
  starting transfers between devices: 17 us -> 16.1 us
    pallas_call x3 -> x5, Pallas kernels: 23 us -> 19.5 us  [the longest x2 14.3 us: attend(): pl.pallas_call(functools.partial(attend_kernel, late, near, shards, membe...]
    ppermute x17 -> x18, waiting for transfers between devices: 35.8 us -> 34.6 us  [swapped(): return lax.ppermute(x, 'ctx', [(i, i ^ by) for i in range(count)])]
    unnamed x11 -> x9, local copies, waits for them, and re-layouts: 2.18 us -> 1.05 us
    ppermute x17 -> x18, starting transfers between devices: 17 us -> 16.1 us  [swapped(): return lax.ppermute(x, 'ctx', [(i, i ^ by) for i in range(count)])]
  transfers between devices with their start and end apart: 17 -> 18, of which waited for: 7 -> 8; matrix products, arithmetic and copies ran while one was open for 0% -> 0% of each run, Pallas kernels for 0% -> 13%
where the time goes in v2:
time: 73.7 us; the launch traced here: 73.3 us
  waiting for transfers between devices  34.6 us (47%)
  Pallas kernels  20.9 us (28%)
  starting transfers between devices  16.1 us (22%)
  local copies, waits for them, and re-layouts  1.05 us (1%)
  between operations  0.74 us (1%)
    ppermute x18, waiting for transfers between devices, swapped(): return lax.ppermute(x, 'ctx', [(i, i ^ by) for i in range(count)])  34.6 us
    ppermute x18, starting transfers between devices, swapped(): return lax.ppermute(x, 'ctx', [(i, i ^ by) for i in range(count)])  16.1 us
    pallas_call x2, Pallas kernels, attend(): pl.pallas_call(functools.partial(attend_kernel, late, near, shards, membe...  14.3 us
    pallas_call x2, Pallas kernels, split_heads(): pl.pallas_call(functools.partial(split_heads_kernel, which, members, grou...  4.81 us
  transfers between devices with their start and end apart: 18, of which 8 were waited for; matrix products, arithmetic and copies ran while one was open for 0% of the time, Pallas kernels for 13%

profile of v2, /device:TPU:0, one launch (start us, length us, event | category | flops | bytes accessed | tf_op | source)
XLA Modules:
  0.0 73.3 jit_solution(15154587431822553012)
XLA Ops:
  0.6 0.0 copy-start.2
  0.6 2.4 %split_late.1 = (bf16[512,256]{1,0:T(8,128)(2,1)}, bf16[512,256]{1,0:T(8,128)(2,1)}, bf16[512,256]{1,0:T(8,128)(2,1)}, bf16[512,256]{1,0:T(8,128)(2,1)}) custom-call(bf16[512,512]{1,0:T(8,128)(2,1)} %refs_0_.5, bf16[512,512]{1,0:T(8,128)(2,1)} %refs_1_.3, bf16[512,512]{1,0:T(8,128)(2,1)} %refs_2_.3, bf16[512,512]{1,0:T(8,128)(2,1)} %refs_3_.3), custom_call_target="tpu_custom_call" | custom-call | bytes 2097152 | tf_op jit(solution)/shard_map/split_late/pallas_call | solution.py:62
  3.1 0.0 copy-start.3
  3.1 3.0 %collective-permute-start.7 = (bf16[512,256]{1,0:T(8,128)(2,1)}, bf16[512,256]{1,0:T(8,128)(2,1)S(1)}, u32[]{:S(2)}, u32[]{:S(2)}) collective-permute-start(bf16[512,256]{1,0:T(8,128)(2,1)} %get-tuple-element.34), channel_id=1, source_target_pairs={{0,8},{4,12},{8,0},{12,4},{16,24},{20,28},{24,16},{28,20},{1,9},{5... | collective-permute-start | bytes 786440 | tf_op jit(solution)/shard_map/ppermute | solution.py:25
  6.1 1.5 %collective-permute-start.8 = (bf16[512,256]{1,0:T(8,128)(2,1)}, bf16[512,256]{1,0:T(8,128)(2,1)S(1)}, u32[]{:S(2)}, u32[]{:S(2)}) collective-permute-start(bf16[512,256]{1,0:T(8,128)(2,1)} %get-tuple-element.35), channel_id=1, source_target_pairs={{0,16},{4,20},{8,24},{12,28},{16,0},{20,4},{24,8},{28,12},{1,17},{... | collective-permute-start | bytes 786440 | tf_op jit(solution)/shard_map/ppermute | solution.py:25
  7.6 2.4 %split_early.1 = (bf16[512,256]{1,0:T(8,128)(2,1)}, bf16[512,256]{1,0:T(8,128)(2,1)}, bf16[512,256]{1,0:T(8,128)(2,1)}, bf16[512,256]{1,0:T(8,128)(2,1)}) custom-call(bf16[512,512]{1,0:T(8,128)(2,1)} %refs_0_.5, bf16[512,512]{1,0:T(8,128)(2,1)} %refs_1_.3, bf16[512,512]{1,0:T(8,128)(2,1)} %refs_2_.3, bf16[512,512]{1,0:T(8,128)(2,1)} %refs_3_.3), custom_call_target="tpu_custom_call" | custom-call | bytes 2097152 | tf_op jit(solution)/shard_map/split_early/pallas_call | solution.py:62
  10.0 0.6 collective-permute-start
  10.6 0.0 collective-permute-start.1
  10.7 2.9 %collective-permute-start.2 = (bf16[512,256]{1,0:T(8,128)(2,1)}, bf16[512,256]{1,0:T(8,128)(2,1)S(1)}, u32[]{:S(2)}, u32[]{:S(2)}) collective-permute-start(bf16[512,256]{1,0:T(8,128)(2,1)} %get-tuple-element.32), channel_id=1, source_target_pairs={{0,24},{4,28},{8,16},{12,20},{16,8},{20,12},{24,0},{28,4},{1,25},{... | collective-permute-start | bytes 786440 | tf_op jit(solution)/shard_map/ppermute | solution.py:25
  13.6 0.0 collective-permute-done.7.refs_10_
  13.6 0.0 copy-done.3
  13.6 2.9 %collective-permute-start.9 = (bf16[512,256]{1,0:T(8,128)(2,1)S(1)}, bf16[512,256]{1,0:T(8,128)(2,1)S(1)}, u32[]{:S(2)}, u32[]{:S(2)}) collective-permute-start(bf16[512,256]{1,0:T(8,128)(2,1)S(1)} %copy-done.3), channel_id=1, source_target_pairs={{0,24},{4,28},{8,16},{12,20},{16,8},{20,12},{24,0},{28,4},{1,25},{... | collective-permute-start | bytes 786440 | tf_op jit(solution)/shard_map/ppermute | solution.py:25
  16.5 0.0 collective-permute-done.8.refs_11_
  16.5 0.0 collective-permute-start.3
  16.5 3.0 %collective-permute-done.refs_2_ = bf16[512,256]{1,0:T(8,128)(2,1)S(1)} collective-permute-done((bf16[512,256]{1,0:T(8,128)(2,1)}, bf16[512,256]{1,0:T(8,128)(2,1)S(1)}, u32[]{:S(2)}, u32[]{:S(2)}) %collective-permute-start) | collective-permute-done | bytes 262176 | tf_op jit(solution)/shard_map/ppermute | solution.py:25
  19.5 0.0 collective-permute-start.4
  19.5 11.4 %collective-permute-done.1.refs_3_ = bf16[512,256]{1,0:T(8,128)(2,1)S(1)} collective-permute-done((bf16[512,256]{1,0:T(8,128)(2,1)}, bf16[512,256]{1,0:T(8,128)(2,1)S(1)}, u32[]{:S(2)}, u32[]{:S(2)}) %collective-permute-start.1) | collective-permute-done | bytes 262176 | tf_op jit(solution)/shard_map/ppermute | solution.py:25
  30.9 0.0 collective-permute-start.5
  30.9 0.0 collective-permute-done.2.refs_4_
  30.9 0.5 collective-permute-start.6
  31.5 0.0 collective-permute-done.9.refs_12_
  31.5 0.0 copy-done
  31.5 0.1 collective-permute-start.10
  31.5 0.0 collective-permute-done.3.refs_5_
  31.5 0.4 collective-permute-start.11
  32.0 0.0 collective-permute-done.4.refs_6_
  32.0 0.1 collective-permute-start.12
  32.1 0.4 collective-permute-done.5.refs_7_
  32.5 0.1 collective-permute-start.13
  32.6 0.1 copy.9.refs_0_
  32.7 0.1 collective-permute-done.6.refs_8_
  32.9 0.9 %copy-done.1 = bf16[512,256]{1,0:T(8,128)(2,1)S(1)} copy-done((bf16[512,256]{1,0:T(8,128)(2,1)S(1)}, bf16[512,256]{1,0:T(8,128)(2,1)}, u32[]{:S(2)}) %copy-start.1) | copy-done | bytes 262168
  33.8 6.8 %attend_early.1 = (bf16[128,256]{1,0:T(8,128)(2,1)S(1)}, bf16[128,256]{1,0:T(8,128)(2,1)S(1)}, bf16[128,256]{1,0:T(8,128)(2,1)S(1)}, bf16[128,256]{1,0:T(8,128)(2,1)S(1)}, f32[2048,256]{1,0:T(8,128)S(1)}) custom-call(s32[32,6]{1,0:T(8,128)S(1)} %copy.9.refs_0_, bf16[512,256]{1,0:T(8,128)(2,1)S(1)} %copy-done.1, ...), custom_call_target="tpu_custom_call" | custom-call | flops 1342177280 | bytes 2097152 | tf_op jit(solution)/shard_map/attend_early/pallas_call | solution.py:295
  40.7 0.0 collective-permute-done.10.refs_13_
  40.7 0.0 collective-permute-done.11.refs_14_
  40.7 0.0 collective-permute-done.12.refs_15_
  40.7 0.0 collective-permute-done.13.refs_16_
  40.7 7.5 %attend_late.1 = (bf16[128,256]{1,0:T(8,128)(2,1)S(1)}, bf16[128,256]{1,0:T(8,128)(2,1)S(1)}, bf16[128,256]{1,0:T(8,128)(2,1)S(1)}, bf16[128,256]{1,0:T(8,128)(2...) custom-call(s32[32,6]{1,0:T(8,128)S(1)} %copy.9.refs_0_, ...), custom_call_target="tpu_custom_call" | custom-call | flops 1342177280 | bytes 4194304 | tf_op jit(solution)/shard_map/attend_late/pallas_call | solution.py:295
  48.2 0.3 collective-permute-start.14
  48.5 2.4 %collective-permute-done.14.refs_0_ = bf16[4,512,256]{2,1,0:T(8,128)(2,1)S(1)} collective-permute-done((bf16[4,512,256]{2,1,0:T(8,128)(2,1)S(1)}, bf16[4,512,256]{2,1,0:T(8,128)(2,1)S(1)}, u32[]{:S(2)}, u32[]{:S(2)}) %collective-permute-start.14) | collective-permute-done | bytes 1048608 | tf_op jit(solution)/shard_map/ppermute | solution.py:25
  50.9 0.3 add_partials.1
  51.2 0.5 collective-permute-start.15
  51.8 1.6 %collective-permute-start.16 = (bf16[768,256]{1,0:T(8,128)(2,1)S(1)}, bf16[768,256]{1,0:T(8,128)(2,1)S(1)}, u32[]{:S(2)}, u32[]{:S(2)}) collective-permute-start(bf16[768,256]{1,0:T(8,128)(2,1)S(1)} %get-tuple-element.53), channel_id=1, source_target_pairs={{0,16},{4,20},{8,24},{12,28},{16,0},{20,4},{24,8},{28,12},{1,17},{... | collective-permute-start | bytes 1179656 | tf_op jit(solution)/shard_map/ppermute | solution.py:25
  53.4 1.4 %collective-permute-start.17 = (bf16[768,256]{1,0:T(8,128)(2,1)S(1)}, bf16[768,256]{1,0:T(8,128)(2,1)S(1)}, u32[]{:S(2)}, u32[]{:S(2)}) collective-permute-start(bf16[768,256]{1,0:T(8,128)(2,1)S(1)} %get-tuple-element.54), channel_id=1, source_target_pairs={{0,24},{4,28},{8,16},{12,20},{16,8},{20,12},{24,0},{28,4},{1,25},{... | collective-permute-start | bytes 1179656 | tf_op jit(solution)/shard_map/ppermute | solution.py:25
  54.8 8.5 %collective-permute-done.15.refs_1_ = bf16[768,256]{1,0:T(8,128)(2,1)S(1)} collective-permute-done((bf16[768,256]{1,0:T(8,128)(2,1)S(1)}, bf16[768,256]{1,0:T(8,128)(2,1)S(1)}, u32[]{:S(2)}, u32[]{:S(2)}) %collective-permute-start.15) | collective-permute-done | bytes 393248 | tf_op jit(solution)/shard_map/ppermute | solution.py:25
  63.3 7.0 %collective-permute-done.16.refs_2_ = bf16[768,256]{1,0:T(8,128)(2,1)S(1)} collective-permute-done((bf16[768,256]{1,0:T(8,128)(2,1)S(1)}, bf16[768,256]{1,0:T(8,128)(2,1)S(1)}, u32[]{:S(2)}, u32[]{:S(2)}) %collective-permute-start.16) | collective-permute-done | bytes 393248 | tf_op jit(solution)/shard_map/ppermute | solution.py:25
  70.3 1.6 %collective-permute-done.17.refs_3_ = bf16[768,256]{1,0:T(8,128)(2,1)S(1)} collective-permute-done((bf16[768,256]{1,0:T(8,128)(2,1)S(1)}, bf16[768,256]{1,0:T(8,128)(2,1)S(1)}, u32[]{:S(2)}, u32[]{:S(2)}) %collective-permute-start.17) | collective-permute-done | bytes 393248 | tf_op jit(solution)/shard_map/ppermute | solution.py:25
  71.9 1.4 %join_heads.1 = (bf16[512,512]{1,0:T(8,128)(2,1)}, bf16[512,512]{1,0:T(8,128)(2,1)}, bf16[512,512]{1,0:T(8,128)(2,1)}) custom-call(bf16[768,256]{1,0:T(8,128)(2,1)S(1)} %get-tuple-element.51.refs_0_, bf16[768,256]{1,0:T(8,128)(2,1)S(1)} %collective-permute-done.15.refs_1_, bf16[768,256]{1,0:T(8,128)(2,1)S(1)} %collective-permute-done.16.refs_2_, ...), custom_call_target="tpu_custom_call" | custom-call | bytes 3145728 | tf_op jit(solution)/shard_map/join_heads/pallas_call | solution.py:94
  (3 shorter events, 0.0 us)
Async XLA Ops:
  0.6 32.0 %copy-start.2 = (s32[32,6]{0,1:T(8,128)S(1)}, s32[32,6]{0,1:T(8,128)}, u32[]{:S(2)}) copy-start(s32[32,6]{0,1:T(8,128)} %param.9) | copy-start | bytes 2308
  3.1 10.5 %copy-start.3 = (bf16[512,256]{1,0:T(8,128)(2,1)S(1)}, bf16[512,256]{1,0:T(8,128)(2,1)}, u32[]{:S(2)}) copy-start(bf16[512,256]{1,0:T(8,128)(2,1)} %get-tuple-element.36) | copy-start | bytes 786436
  3.1 28.4 %copy-start = (bf16[512,256]{1,0:T(8,128)(2,1)S(1)}, bf16[512,256]{1,0:T(8,128)(2,1)}, u32[]{:S(2)}) copy-start(bf16[512,256]{1,0:T(8,128)(2,1)} %get-tuple-element.33.refs_9_) | copy-start | bytes 786436
  3.1 10.5 %collective-permute-start.7 = (bf16[512,256]{1,0:T(8,128)(2,1)}, bf16[512,256]{1,0:T(8,128)(2,1)S(1)}, u32[]{:S(2)}, u32[]{:S(2)}) collective-permute-start(bf16[512,256]{1,0:T(8,128)(2,1)} %get-tuple-element.34), channel_id=1, source_target_pairs={{0,8},{4,12},{8,0},{12,4},{16,24},{20,28},{24,16},{28,20},{1,9},{5... | collective-permute-start | bytes 786440 | tf_op jit(solution)/shard_map/ppermute | solution.py:25
  6.1 10.4 %collective-permute-start.8 = (bf16[512,256]{1,0:T(8,128)(2,1)}, bf16[512,256]{1,0:T(8,128)(2,1)S(1)}, u32[]{:S(2)}, u32[]{:S(2)}) collective-permute-start(bf16[512,256]{1,0:T(8,128)(2,1)} %get-tuple-element.35), channel_id=1, source_target_pairs={{0,16},{4,20},{8,24},{12,28},{16,0},{20,4},{24,8},{28,12},{1,17},{... | collective-permute-start | bytes 786440 | tf_op jit(solution)/shard_map/ppermute | solution.py:25
  10.0 9.5 %collective-permute-start = (bf16[512,256]{1,0:T(8,128)(2,1)}, bf16[512,256]{1,0:T(8,128)(2,1)S(1)}, u32[]{:S(2)}, u32[]{:S(2)}) collective-permute-start(bf16[512,256]{1,0:T(8,128)(2,1)} %get-tuple-element.30), channel_id=1, source_target_pairs={{0,8},{4,12},{8,0},{12,4},{16,24},{20,28},{24,16},{28,20},{1,9},{5... | collective-permute-start | bytes 786440 | tf_op jit(solution)/shard_map/ppermute | solution.py:25
  10.6 20.3 %collective-permute-start.1 = (bf16[512,256]{1,0:T(8,128)(2,1)}, bf16[512,256]{1,0:T(8,128)(2,1)S(1)}, u32[]{:S(2)}, u32[]{:S(2)}) collective-permute-start(bf16[512,256]{1,0:T(8,128)(2,1)} %get-tuple-element.31), channel_id=1, source_target_pairs={{0,16},{4,20},{8,24},{12,28},{16,0},{20,4},{24,8},{28,12},{1,17},{... | collective-permute-start | bytes 786440 | tf_op jit(solution)/shard_map/ppermute | solution.py:25
  10.7 20.3 %collective-permute-start.2 = (bf16[512,256]{1,0:T(8,128)(2,1)}, bf16[512,256]{1,0:T(8,128)(2,1)S(1)}, u32[]{:S(2)}, u32[]{:S(2)}) collective-permute-start(bf16[512,256]{1,0:T(8,128)(2,1)} %get-tuple-element.32), channel_id=1, source_target_pairs={{0,24},{4,28},{8,16},{12,20},{16,8},{20,12},{24,0},{28,4},{1,25},{... | collective-permute-start | bytes 786440 | tf_op jit(solution)/shard_map/ppermute | solution.py:25
  13.6 17.9 %collective-permute-start.9 = (bf16[512,256]{1,0:T(8,128)(2,1)S(1)}, bf16[512,256]{1,0:T(8,128)(2,1)S(1)}, u32[]{:S(2)}, u32[]{:S(2)}) collective-permute-start(bf16[512,256]{1,0:T(8,128)(2,1)S(1)} %copy-done.3), channel_id=1, source_target_pairs={{0,24},{4,28},{8,16},{12,20},{16,8},{20,12},{24,0},{28,4},{1,25},{... | collective-permute-start | bytes 786440 | tf_op jit(solution)/shard_map/ppermute | solution.py:25
  16.5 15.1 %collective-permute-start.3 = (bf16[512,256]{1,0:T(8,128)(2,1)}, bf16[512,256]{1,0:T(8,128)(2,1)S(1)}, u32[]{:S(2)}, u32[]{:S(2)}) collective-permute-start(bf16[512,256]{1,0:T(8,128)(2,1)} %get-tuple-element.29.refs_1_), channel_id=1, source_target_pairs={{0,4},{4,0},{8,12},{12,8},{16,20},{20,16},{24,28},{28,24},{1,5},{5... | collective-permute-start | bytes 786440 | tf_op jit(solution)/shard_map/ppermute | solution.py:25
  19.5 12.5 %collective-permute-start.4 = (bf16[512,256]{1,0:T(8,128)(2,1)S(1)}, bf16[512,256]{1,0:T(8,128)(2,1)S(1)}, u32[]{:S(2)}, u32[]{:S(2)}) collective-permute-start(bf16[512,256]{1,0:T(8,128)(2,1)S(1)} %collective-permute-done.refs_2_), channel_id=1, source_target_pairs={{0,4},{4,0},{8,12},{12,8},{16,20},{20,16},{24,28},{28,24},{1,5},{5... | collective-permute-start | bytes 786440 | tf_op jit(solution)/shard_map/ppermute | solution.py:25
  30.9 1.5 %collective-permute-start.5 = (bf16[512,256]{1,0:T(8,128)(2,1)S(1)}, bf16[512,256]{1,0:T(8,128)(2,1)S(1)}, u32[]{:S(2)}, u32[]{:S(2)}) collective-permute-start(bf16[512,256]{1,0:T(8,128)(2,1)S(1)} %collective-permute-done.1.refs_3_), channel_id=1, source_target_pairs={{0,4},{4,0},{8,12},{12,8},{16,20},{20,16},{24,28},{28,24},{1,5},{5... | collective-permute-start | bytes 786440 | tf_op jit(solution)/shard_map/ppermute | solution.py:25
  30.9 1.9 %collective-permute-start.6 = (bf16[512,256]{1,0:T(8,128)(2,1)S(1)}, bf16[512,256]{1,0:T(8,128)(2,1)S(1)}, u32[]{:S(2)}, u32[]{:S(2)}) collective-permute-start(bf16[512,256]{1,0:T(8,128)(2,1)S(1)} %collective-permute-done.2.refs_4_), channel_id=1, source_target_pairs={{0,4},{4,0},{8,12},{12,8},{16,20},{20,16},{24,28},{28,24},{1,5},{5... | collective-permute-start | bytes 786440 | tf_op jit(solution)/shard_map/ppermute | solution.py:25
  31.5 9.2 %collective-permute-start.10 = (bf16[512,256]{1,0:T(8,128)(2,1)S(1)}, bf16[512,256]{1,0:T(8,128)(2,1)S(1)}, u32[]{:S(2)}, u32[]{:S(2)}) collective-permute-start(bf16[512,256]{1,0:T(8,128)(2,1)S(1)} %copy-done), channel_id=1, source_target_pairs={{0,4},{4,0},{8,12},{12,8},{16,20},{20,16},{24,28},{28,24},{1,5},{5... | collective-permute-start | bytes 786440 | tf_op jit(solution)/shard_map/ppermute | solution.py:25
  31.5 9.1 %collective-permute-start.11 = (bf16[512,256]{1,0:T(8,128)(2,1)S(1)}, bf16[512,256]{1,0:T(8,128)(2,1)S(1)}, u32[]{:S(2)}, u32[]{:S(2)}) collective-permute-start(bf16[512,256]{1,0:T(8,128)(2,1)S(1)} %collective-permute-done.7.refs_10_), channel_id=1, source_target_pairs={{0,4},{4,0},{8,12},{12,8},{16,20},{20,16},{24,28},{28,24},{1,5},{5... | collective-permute-start | bytes 786440 | tf_op jit(solution)/shard_map/ppermute | solution.py:25
  32.0 8.7 %collective-permute-start.12 = (bf16[512,256]{1,0:T(8,128)(2,1)S(1)}, bf16[512,256]{1,0:T(8,128)(2,1)}, u32[]{:S(2)}, u32[]{:S(2)}) collective-permute-start(bf16[512,256]{1,0:T(8,128)(2,1)S(1)} %collective-permute-done.8.refs_11_), channel_id=1, source_target_pairs={{0,4},{4,0},{8,12},{12,8},{16,20},{20,16},{24,28},{28,24},{1,5},{5... | collective-permute-start | bytes 786440 | tf_op jit(solution)/shard_map/ppermute | solution.py:25
  32.5 8.2 %collective-permute-start.13 = (bf16[512,256]{1,0:T(8,128)(2,1)S(1)}, bf16[512,256]{1,0:T(8,128)(2,1)}, u32[]{:S(2)}, u32[]{:S(2)}) collective-permute-start(bf16[512,256]{1,0:T(8,128)(2,1)S(1)} %collective-permute-done.9.refs_12_), channel_id=1, source_target_pairs={{0,4},{4,0},{8,12},{12,8},{16,20},{20,16},{24,28},{28,24},{1,5},{5... | collective-permute-start | bytes 786440 | tf_op jit(solution)/shard_map/ppermute | solution.py:25
  32.9 1.0 %copy-start.1 = (bf16[512,256]{1,0:T(8,128)(2,1)S(1)}, bf16[512,256]{1,0:T(8,128)(2,1)}, u32[]{:S(2)}) copy-start(bf16[512,256]{1,0:T(8,128)(2,1)} %get-tuple-element.29.refs_1_) | copy-start | bytes 786436
  48.2 2.7 %collective-permute-start.14 = (bf16[4,512,256]{2,1,0:T(8,128)(2,1)S(1)}, bf16[4,512,256]{2,1,0:T(8,128)(2,1)S(1)}, u32[]{:S(2)}, u32[]{:S(2)}) collective-permute-start(bf16[4,512,256]{2,1,0:T(8,128)(2,1)S(1)} %get-tuple-element.38), channel_id=1, source_target_pairs={{0,4},{4,0},{8,12},{12,8},{16,20},{20,16},{24,28},{28,24},{1,5},{5... | collective-permute-start | bytes 3145736 | tf_op jit(solution)/shard_map/ppermute | solution.py:25
  51.2 12.0 %collective-permute-start.15 = (bf16[768,256]{1,0:T(8,128)(2,1)S(1)}, bf16[768,256]{1,0:T(8,128)(2,1)S(1)}, u32[]{:S(2)}, u32[]{:S(2)}) collective-permute-start(bf16[768,256]{1,0:T(8,128)(2,1)S(1)} %get-tuple-element.52), channel_id=1, source_target_pairs={{0,8},{4,12},{8,0},{12,4},{16,24},{20,28},{24,16},{28,20},{1,9},{5... | collective-permute-start | bytes 1179656 | tf_op jit(solution)/shard_map/ppermute | solution.py:25
  51.8 18.5 %collective-permute-start.16 = (bf16[768,256]{1,0:T(8,128)(2,1)S(1)}, bf16[768,256]{1,0:T(8,128)(2,1)S(1)}, u32[]{:S(2)}, u32[]{:S(2)}) collective-permute-start(bf16[768,256]{1,0:T(8,128)(2,1)S(1)} %get-tuple-element.53), channel_id=1, source_target_pairs={{0,16},{4,20},{8,24},{12,28},{16,0},{20,4},{24,8},{28,12},{1,17},{... | collective-permute-start | bytes 1179656 | tf_op jit(solution)/shard_map/ppermute | solution.py:25
  53.4 18.6 %collective-permute-start.17 = (bf16[768,256]{1,0:T(8,128)(2,1)S(1)}, bf16[768,256]{1,0:T(8,128)(2,1)S(1)}, u32[]{:S(2)}, u32[]{:S(2)}) collective-permute-start(bf16[768,256]{1,0:T(8,128)(2,1)S(1)} %get-tuple-element.54), channel_id=1, source_target_pairs={{0,24},{4,28},{8,16},{12,20},{16,8},{20,12},{24,0},{28,4},{1,25},{... | collective-permute-start | bytes 1179656 | tf_op jit(solution)/shard_map/ppermute | solution.py:25

commit v3 on v2

v3 whole, which is shorter than its diff:
```python
import functools
import math

import jax
import jax.numpy as jnp
from jax import lax
from jax.experimental import pallas as pl
from jax.experimental.pallas import tpu as pltpu
from jax.sharding import PartitionSpec as P

HEAD_DIM = 128
BLK = 128
WIN = 2
LINKS = 6
SPAN = WIN + LINKS
NEG_FILL = -1e30
SPLIT_LIMIT = 56 * 1024 * 1024
SMALL_LIMIT = 16 * 1024 * 1024


def swapped(x, by):
    count = lax.axis_size("ctx")
    return lax.ppermute(x, "ctx", [(i, i ^ by) for i in range(count)])


def chip_column(members, s):
    chip = lax.div(lax.axis_index("ctx"), members)
    return pl.ds(pl.multiple_of((chip ^ s) * HEAD_DIM, HEAD_DIM), HEAD_DIM)


def all_started(moves, sems):
    copies = [
        pltpu.make_async_copy(source, target, sems.at[i])
        for i, (source, target) in enumerate(moves)
    ]
    for copy in copies:
        copy.start()
    return copies


def split_heads_kernel(which, members, groups, *refs):
    query, key, value, grad = refs[:4]
    outs = refs[-1 - groups : -1]
    half = query.shape[0] // 2
    taken = pl.ds(which * half, half)
    moves = []
    for s in range(groups):
        column = chip_column(members, s)
        for t, (pair, ask) in enumerate(((key, query), (value, grad))):
            lanes = pl.ds(t * HEAD_DIM, HEAD_DIM)
            moves.append((pair.at[taken, column], outs[s].at[pl.ds(0, half), lanes]))
            moves.append((ask.at[taken, column], outs[s].at[pl.ds(half, half), lanes]))
    for copy in all_started(moves, refs[-1]):
        copy.wait()


def split_heads(which, arrays, after, members, groups):
    rows = arrays[0].shape[0]
    out = jax.ShapeDtypeStruct((rows, 2 * HEAD_DIM), jnp.bfloat16)
    return pl.pallas_call(
        functools.partial(split_heads_kernel, which, members, groups),
        out_shape=[out] * groups,
        in_specs=[pl.BlockSpec(memory_space=pl.ANY)] * (len(arrays) + len(after)),
        out_specs=[pl.BlockSpec(memory_space=pltpu.VMEM)] * groups,
        scratch_shapes=[pltpu.SemaphoreType.DMA((4 * groups,))],
        compiler_params=pltpu.CompilerParams(vmem_limit_bytes=SPLIT_LIMIT),
        cost_estimate=pl.CostEstimate(
            flops=0, bytes_accessed=8 * groups * rows * HEAD_DIM, transcendentals=0
        ),
        name="split_late" if which else "split_early",
    )(*arrays, *after)


def pairs_kernel(groups, *refs):
    out = refs[-1]
    for s in range(groups):
        out[s] = refs[s][: out.shape[1], :]


def only_pairs(packs, after, groups):
    half = packs[0].shape[0] // 2
    vmem = pl.BlockSpec(memory_space=pltpu.VMEM)
    return pl.pallas_call(
        functools.partial(pairs_kernel, groups),
        out_shape=jax.ShapeDtypeStruct((groups, half, 2 * HEAD_DIM), jnp.bfloat16),
        in_specs=[vmem] * groups + [pl.BlockSpec(memory_space=pl.ANY)] * len(after),
        out_specs=vmem,
        compiler_params=pltpu.CompilerParams(vmem_limit_bytes=SMALL_LIMIT),
        cost_estimate=pl.CostEstimate(
            flops=0, bytes_accessed=8 * groups * half * HEAD_DIM, transcendentals=0
        ),
        name="only_pairs",
    )(*packs, *after)


def join_heads_kernel(members, groups, *refs):
    pairs = refs[:groups]
    dqs = refs[groups : 2 * groups]
    outs = refs[2 * groups :]
    for s in range(groups):
        column = chip_column(members, s)
        outs[1][:, column] = pairs[s][:, :HEAD_DIM]
        outs[2][:, column] = pairs[s][:, HEAD_DIM:]
        for n in range(outs[0].shape[0] // BLK):
            packed = slice(n // 2 * BLK, (n // 2 + 1) * BLK)
            lanes = slice(n % 2 * HEAD_DIM, (n % 2 + 1) * HEAD_DIM)
            outs[0][n * BLK : (n + 1) * BLK, column] = dqs[s][packed, lanes]


def join_heads(dqs, pairs, members, groups):
    rows = pairs[0].shape[0]
    vmem = pl.BlockSpec(memory_space=pltpu.VMEM)
    out = jax.ShapeDtypeStruct((rows, groups * HEAD_DIM), jnp.bfloat16)
    return pl.pallas_call(
        functools.partial(join_heads_kernel, members, groups),
        out_shape=[out] * 3,
        in_specs=[vmem] * (2 * groups),
        out_specs=[vmem] * 3,
        compiler_params=pltpu.CompilerParams(vmem_limit_bytes=SMALL_LIMIT),
        cost_estimate=pl.CostEstimate(
            flops=0, bytes_accessed=12 * rows * groups * HEAD_DIM, transcendentals=0
        ),
        name="join_heads",
    )(*pairs, *dqs)


def add_kernel(members, groups, *refs):
    far = refs[: members - 1]
    own = refs[members - 1 : members - 1 + groups]
    outs = refs[members - 1 + groups :]
    for s in range(groups):
        total = own[s][...].astype(jnp.float32)
        for part in far:
            total = total + part[s].astype(jnp.float32)
        outs[s][:, :HEAD_DIM] = (total[:, :HEAD_DIM] * HEAD_DIM**-0.5).astype(jnp.bfloat16)
        outs[s][:, HEAD_DIM:] = total[:, HEAD_DIM:].astype(jnp.bfloat16)


def add_partials(far, own, members, groups):
    vmem = pl.BlockSpec(memory_space=pltpu.VMEM)
    out = jax.ShapeDtypeStruct(own[0].shape, jnp.bfloat16)
    return pl.pallas_call(
        functools.partial(add_kernel, members, groups),
        out_shape=[out] * groups,
        in_specs=[vmem] * (members - 1 + groups),
        out_specs=[vmem] * groups,
        compiler_params=pltpu.CompilerParams(vmem_limit_bytes=SMALL_LIMIT),
        cost_estimate=pl.CostEstimate(
            flops=0, bytes_accessed=8 * groups * own[0].size, transcendentals=0
        ),
        name="add_partials",
    )(*far, *own)


def dot(left, right, dims):
    return lax.dot_general(left, right, (dims, ((), ())), preferred_element_type=jnp.float32)


def attend_kernel(late, near, shards, members, groups, half, *refs):
    slots = members * groups
    rows = 2 * half
    stretch = half // BLK
    links = refs[0]
    refs = refs[1:]
    if late:
        packs = [*refs[:groups]]
        for part in refs[groups : groups + members - 1]:
            packs += [part.at[s] for s in range(groups)]
        dq_early = refs[groups + members - 1 : 2 * groups + members - 1]
        refs = refs[2 * groups + members + 1 :]
        dq_outs = refs[:groups]
        own_outs = refs[groups : 2 * groups]
        far_outs = refs[2 * groups : 2 * groups + members - 1]
        refs = refs[2 * groups + members - 1 :]
    else:
        packs = refs[:slots]
        dq_outs = refs[slots : slots + groups]
        refs = refs[slots + groups :]
    pair_buf, acc, ask_buf, dq_buf, sems = refs
    device = lax.axis_index("ctx")

    moves = []
    for i in range(slots):
        place = pl.ds(i * rows + (half if late else 0), half)
        moves.append((packs[i].at[pl.ds(0, half)], pair_buf.at[place]))
    for s in range(groups):
        moves.append((packs[s].at[pl.ds(half, half)], ask_buf.at[pl.ds(s * half, half)]))
    if near:
        for source, target in moves:
            target[...] = source[...]
    else:
        copies = all_started(moves, sems)
    if not late:
        acc[...] = jnp.zeros_like(acc)
    if not near:
        for copy in copies:
            copy.wait()

    scaling = HEAD_DIM**-0.5
    causal = lax.broadcasted_iota(jnp.int32, (BLK, BLK), 0) <= lax.broadcasted_iota(
        jnp.int32, (BLK, BLK), 1
    )
    blank = jnp.zeros((BLK, HEAD_DIM), jnp.bfloat16)

    def place_of(block):
        run = lax.div(block, stretch)
        local = block - run * stretch
        owner = run
        if late:
            is_late = run >= shards
            owner = jnp.where(is_late, 2 * shards - 1 - run, run)
            local = local + jnp.where(is_late, stretch, 0)
        apart = owner ^ device
        slot = lax.rem(apart, members) * groups + lax.div(apart, members)
        return pl.multiple_of(slot * rows + local * BLK, BLK)

    def step(s, _):
        asker = device ^ (s * members)
        first = (2 * shards - 1 - asker if late else asker) * stretch
        units = range(stretch)
        listed = []
        for n in units:
            block = first + n
            listed.append([block, block - 1] + [links[block, i] for i in range(LINKS)])
        places = [[place_of(jnp.maximum(j, 0)) for j in row] for row in listed]
        pairs = [jnp.concatenate([pair_buf[pl.ds(p, BLK), :] for p in row], 0) for row in places]
        wide = []
        for n in units:
            ask = ask_buf[pl.ds(pl.multiple_of(s * half + n * BLK, BLK), BLK), :]
            wide.append(
                jnp.concatenate(
                    [
                        jnp.concatenate([ask[:, :HEAD_DIM], blank], 1),
                        jnp.concatenate([blank, ask[:, HEAD_DIM:]], 1),
                    ],
                    0,
                )
            )
        both = [dot(pairs[n], wide[n], ((1,), (1,))) for n in units]
        dscore_b, terms = [], []
        for n in units:
            raw = [both[n][i * BLK : (i + 1) * BLK, :BLK] for i in range(SPAN)]
            dprob = both[n][:, BLK:].reshape(SPAN, BLK, BLK)
            raw[0] = jnp.where(causal, raw[0], NEG_FILL)
            unused = [0.0] + [jnp.where(j >= 0, 0.0, NEG_FILL) for j in listed[n][1:]]
            tops = [jnp.max(raw[i], axis=0, keepdims=True) + unused[i] for i in range(SPAN)]
            top = functools.reduce(jnp.maximum, tops)
            weight = jnp.stack(
                [
                    jnp.exp2((raw[i] - (top - unused[i])) * (scaling * math.log2(math.e)))
                    for i in range(SPAN)
                ]
            )
            share = 1.0 / jnp.sum(weight, axis=(0, 1), keepdims=True)
            delta = jnp.sum(weight * dprob, axis=(0, 1), keepdims=True) * share
            prob = weight * share
            dscore = (prob * (dprob - delta)).astype(jnp.bfloat16).reshape(SPAN * BLK, BLK)
            dscore_b.append(dscore)
            prob = prob.astype(jnp.bfloat16).reshape(SPAN * BLK, BLK)
            terms.append(dot(jnp.concatenate([dscore, prob], 1), wide[n], ((1,), (0,))))
        dq = [dot(dscore_b[n], pairs[n][:, :HEAD_DIM], ((0,), (0,))) * scaling for n in units]
        for n in units:
            lanes = slice(n % 2 * HEAD_DIM, (n % 2 + 1) * HEAD_DIM)
            packed = pl.ds(pl.multiple_of(s * (half // 2) + n // 2 * BLK, BLK), BLK)
            dq_buf[packed, lanes] = dq[n].astype(jnp.bfloat16)
            for i, p in enumerate(places[n]):
                acc[pl.ds(p, BLK), :] += terms[n][i * BLK : (i + 1) * BLK]
        return 0

    lax.fori_loop(0, groups, step, 0)

    quarter = half // 2
    for s in range(groups):
        if late:
            dq_outs[s][:quarter] = dq_early[s][...]
        dq_outs[s][-quarter:] = dq_buf[s * quarter : (s + 1) * quarter, :]
    if late:
        for s in range(groups):
            own_outs[s][...] = acc[s * rows : (s + 1) * rows, :].astype(jnp.bfloat16)
        for r in range(1, members):
            for s in range(groups):
                start = (r * groups + s) * rows
                far_outs[r - 1][s] = acc[start : start + rows, :].astype(jnp.bfloat16)


def attend(links, packs, dq_early, buffers, shards, members, groups):
    late = len(buffers) > 0
    half = packs[0].shape[0] // 2
    rows = 2 * half
    slots = members * groups
    blocks = groups * half // BLK
    near = slots * rows <= 4096

    def shape(*dims, dtype=jnp.bfloat16):
        return jax.ShapeDtypeStruct((*dims, 2 * HEAD_DIM), dtype)

    outs = [shape(half if late else half // 2)] * groups
    if late:
        outs += [shape(rows)] * groups + [shape(groups, rows)] * (members - 1)
    outs += [shape(slots * rows), shape(slots * rows, dtype=jnp.float32)]
    vmem = pl.BlockSpec(memory_space=pltpu.VMEM)
    read = vmem if near else pl.BlockSpec(memory_space=pl.ANY)
    given = [*packs, *dq_early, *buffers]
    found = pl.pallas_call(
        functools.partial(attend_kernel, late, near, shards, members, groups, half),
        out_shape=outs,
        in_specs=[pl.BlockSpec(memory_space=pltpu.SMEM)]
        + [read] * len(packs)
        + [vmem] * (len(dq_early) + len(buffers)),
        out_specs=[vmem] * len(outs),
        input_output_aliases={len(given) - 1: len(outs) - 2, len(given): len(outs) - 1}
        if late
        else {},
        scratch_shapes=[
            pltpu.VMEM((groups * half, 2 * HEAD_DIM), jnp.bfloat16),
            pltpu.VMEM((groups * half // 2, 2 * HEAD_DIM), jnp.bfloat16),
            pltpu.SemaphoreType.DMA((slots + groups,)),
        ],
        compiler_params=pltpu.CompilerParams(vmem_limit_bytes=SMALL_LIMIT),
        cost_estimate=pl.CostEstimate(
            flops=10 * blocks * SPAN * BLK * BLK * HEAD_DIM if late else 0,
            bytes_accessed=8 * slots * rows * HEAD_DIM if late else 0,
            transcendentals=blocks * SPAN * BLK * BLK if late else 0,
        ),
        name="attend_late" if late else "attend_early",
    )(links, *given)
    if late:
        return found[:groups], found[groups : 2 * groups], found[2 * groups : -2]
    return found[:groups], found[-2:]


def to_chips(parts, members):
    return [parts[0]] + [swapped(part, s * members) for s, part in enumerate(parts[1:], 1)]


def with_members(parts, members):
    return parts + [swapped(part, r) for r in range(1, members) for part in parts]


def per_device(query, key, value, out_grad, links):
    rows, width = query.shape
    groups = width // HEAD_DIM
    shards = lax.axis_size("ctx")
    members = shards // groups
    arrays = (query, key, value, out_grad)

    early = split_heads(0, arrays, [], members, groups)
    late = split_heads(1, arrays, early[:1], members, groups)
    early = with_members(to_chips(early, members), members)
    late = to_chips(late, members)
    dq_early, buffers = attend(links, early, [], [], shards, members, groups)
    lent = only_pairs(late, dq_early[:1], groups)
    late = late + [swapped(lent, r) for r in range(1, members)]
    dqs, own, far = attend(links, late, dq_early, buffers, shards, members, groups)
    far = [swapped(part, r) for r, part in enumerate(far, 1)]
    dqs = to_chips(dqs, members)
    pairs = to_chips(add_partials(far, own, members, groups), members)
    return tuple(join_heads(dqs, pairs, members, groups))


def solution(mesh):
    return jax.shard_map(
        per_device,
        mesh=mesh,
        in_specs=(P("ctx", "head"), P("ctx", "head"), P("ctx", "head"), P("ctx", "head"), P()),
        out_specs=(P("ctx", "head"), P("ctx", "head"), P("ctx", "head")),
        check_vma=False,
    )
```

time: 73.7 us -> 69.4 us (0.942)
  waiting for transfers between devices: 34.6 us -> 29.2 us
  local copies, waits for them, and re-layouts: 1.05 us -> 1.99 us
  starting transfers between devices: 16.1 us -> 17 us
  Pallas kernels: 20.9 us -> 20.1 us
    ppermute x18, waiting for transfers between devices: 34.6 us -> 29.2 us  [swapped(): return lax.ppermute(x, 'ctx', [(i, i ^ by) for i in range(count)])]
    unnamed x9 -> x7, local copies, waits for them, and re-layouts: 1.05 us -> 1.99 us
    ppermute x18, starting transfers between devices: 16.1 us -> 17 us  [swapped(): return lax.ppermute(x, 'ctx', [(i, i ^ by) for i in range(count)])]
  transfers between devices with their start and end apart: 18 -> 18, of which waited for: 8 -> 6; matrix products, arithmetic and copies ran while one was open for 0% -> 0% of each run, Pallas kernels for 13% -> 14%
where the time goes in v3:
time: 69.4 us; the launch traced here: 69 us
  waiting for transfers between devices  29.2 us (42%)
  Pallas kernels  20.1 us (29%)
  starting transfers between devices  17 us (24%)
  local copies, waits for them, and re-layouts  1.99 us (3%)
  between operations  0.73 us (1%)
    ppermute x18, waiting for transfers between devices, swapped(): return lax.ppermute(x, 'ctx', [(i, i ^ by) for i in range(count)])  29.2 us
    ppermute x18, starting transfers between devices, swapped(): return lax.ppermute(x, 'ctx', [(i, i ^ by) for i in range(count)])  17 us
    pallas_call x2, Pallas kernels, attend(): pl.pallas_call(functools.partial(attend_kernel, late, near, shards, membe...  13.6 us
    pallas_call x2, Pallas kernels, split_heads(): pl.pallas_call(functools.partial(split_heads_kernel, which, members, grou...  4.75 us
    unnamed x7, local copies, waits for them, and re-layouts  1.99 us
    pallas_call x1, Pallas kernels, join_heads(): pl.pallas_call(functools.partial(join_heads_kernel, members, groups), out...  1.42 us
  transfers between devices with their start and end apart: 18, of which 6 were waited for; matrix products, arithmetic and copies ran while one was open for 0% of the time, Pallas kernels for 14%

profile of v3, /device:TPU:0, one launch (start us, length us, event | category | flops | bytes accessed | tf_op | source)
XLA Modules:
  0.0 69.0 jit_solution(2690647621880524700)
XLA Ops:
  0.6 0.0 copy-start.2
  0.6 2.4 %split_early.1 = (bf16[512,256]{1,0:T(8,128)(2,1)}, bf16[512,256]{1,0:T(8,128)(2,1)}, bf16[512,256]{1,0:T(8,128)(2,1)}, bf16[512,256]{1,0:T(8,128)(2,1)}) custom-call(bf16[512,512]{1,0:T(8,128)(2,1)} %refs_0_.5, bf16[512,512]{1,0:T(8,128)(2,1)} %refs_1_.3, bf16[512,512]{1,0:T(8,128)(2,1)} %refs_2_.3, bf16[512,512]{1,0:T(8,128)(2,1)} %refs_3_.3), custom_call_target="tpu_custom_call" | custom-call | bytes 2097152 | tf_op jit(solution)/shard_map/split_early/pallas_call | solution.py:60
  3.0 3.0 %collective-permute-start.3 = (bf16[512,256]{1,0:T(8,128)(2,1)}, bf16[512,256]{1,0:T(8,128)(2,1)S(1)}, u32[]{:S(2)}, u32[]{:S(2)}) collective-permute-start(bf16[512,256]{1,0:T(8,128)(2,1)} %get-tuple-element.35), channel_id=1, source_target_pairs={{0,8},{4,12},{8,0},{12,4},{16,24},{20,28},{24,16},{28,20},{1,9},{5... | collective-permute-start | bytes 786440 | tf_op jit(solution)/shard_map/ppermute | solution.py:23
  6.0 1.5 %collective-permute-start.4 = (bf16[512,256]{1,0:T(8,128)(2,1)}, bf16[512,256]{1,0:T(8,128)(2,1)S(1)}, u32[]{:S(2)}, u32[]{:S(2)}) collective-permute-start(bf16[512,256]{1,0:T(8,128)(2,1)} %get-tuple-element.36), channel_id=1, source_target_pairs={{0,16},{4,20},{8,24},{12,28},{16,0},{20,4},{24,8},{28,12},{1,17},{... | collective-permute-start | bytes 786440 | tf_op jit(solution)/shard_map/ppermute | solution.py:23
  7.6 0.0 collective-permute-start.5
  7.6 0.0 collective-permute-start.6
  7.6 5.8 %collective-permute-done.3.refs_2_ = bf16[512,256]{1,0:T(8,128)(2,1)S(1)} collective-permute-done((bf16[512,256]{1,0:T(8,128)(2,1)}, bf16[512,256]{1,0:T(8,128)(2,1)S(1)}, u32[]{:S(2)}, u32[]{:S(2)}) %collective-permute-start.3) | collective-permute-done | bytes 262176 | tf_op jit(solution)/shard_map/ppermute | solution.py:23
  13.4 0.0 collective-permute-start.7
  13.4 2.4 %split_late.1 = (bf16[512,256]{1,0:T(8,128)(2,1)}, bf16[512,256]{1,0:T(8,128)(2,1)}, bf16[512,256]{1,0:T(8,128)(2,1)}, bf16[512,256]{1,0:T(8,128)(2,1)}) custom-call(bf16[512,512]{1,0:T(8,128)(2,1)} %refs_0_.5, bf16[512,512]{1,0:T(8,128)(2,1)} %refs_1_.3, bf16[512,512]{1,0:T(8,128)(2,1)} %refs_2_.3, bf16[512,512]{1,0:T(8,128)(2,1)} %refs_3_.3, ...), custom_call_target="tpu_custom_call" | custom-call | bytes 2097152 | tf_op jit(solution)/shard_map/split_late/pallas_call | solution.py:60
  15.8 2.1 %collective-permute-start = (bf16[512,256]{1,0:T(8,128)(2,1)}, bf16[512,256]{1,0:T(8,128)(2,1)S(1)}, u32[]{:S(2)}, u32[]{:S(2)}) collective-permute-start(bf16[512,256]{1,0:T(8,128)(2,1)} %get-tuple-element.32), channel_id=1, source_target_pairs={{0,8},{4,12},{8,0},{12,4},{16,24},{20,28},{24,16},{28,20},{1,9},{5... | collective-permute-start | bytes 786440 | tf_op jit(solution)/shard_map/ppermute | solution.py:23
  17.9 1.7 %collective-permute-done.4.refs_3_ = bf16[512,256]{1,0:T(8,128)(2,1)S(1)} collective-permute-done((bf16[512,256]{1,0:T(8,128)(2,1)}, bf16[512,256]{1,0:T(8,128)(2,1)S(1)}, u32[]{:S(2)}, u32[]{:S(2)}) %collective-permute-start.4) | collective-permute-done | bytes 262176 | tf_op jit(solution)/shard_map/ppermute | solution.py:23
  19.6 0.0 collective-permute-start.8
  19.6 0.0 collective-permute-done.5.refs_4_
  19.6 0.5 collective-permute-start.9
  20.1 0.0 collective-permute-done.6.refs_5_
  20.1 1.5 %collective-permute-start.1 = (bf16[512,256]{1,0:T(8,128)(2,1)}, bf16[512,256]{1,0:T(8,128)(2,1)S(1)}, u32[]{:S(2)}, u32[]{:S(2)}) collective-permute-start(bf16[512,256]{1,0:T(8,128)(2,1)} %get-tuple-element.33), channel_id=1, source_target_pairs={{0,16},{4,20},{8,24},{12,28},{16,0},{20,4},{24,8},{28,12},{1,17},{... | collective-permute-start | bytes 786440 | tf_op jit(solution)/shard_map/ppermute | solution.py:23
  21.7 0.0 collective-permute-done.7.refs_6_
  21.7 0.7 collective-permute-start.2
  22.3 0.0 copy-done.2
  22.3 0.1 copy.11.refs_0_
  22.4 0.0 collective-permute-done.8.refs_7_
  22.4 0.0 collective-permute-done.9.refs_8_
  22.4 0.0 copy-start.1
  22.4 0.9 %copy-done.1 = bf16[512,256]{1,0:T(8,128)(2,1)S(1)} copy-done((bf16[512,256]{1,0:T(8,128)(2,1)S(1)}, bf16[512,256]{1,0:T(8,128)(2,1)}, u32[]{:S(2)}) %copy-start.1) | copy-done | bytes 262168
  23.4 6.8 %attend_early.1 = (bf16[128,256]{1,0:T(8,128)(2,1)S(1)}, bf16[128,256]{1,0:T(8,128)(2,1)S(1)}, bf16[128,256]{1,0:T(8,128)(2,1)S(1)}, bf16[128,256]{1,0:T(8,128)(...) custom-call(s32[32,6]{1,0:T(8,128)S(1)} %copy.11.refs_0_, bf16[512,256]{1,0:T(8,128)(2,1)S(1)} %copy-done.1, ...), custom_call_target="tpu_custom_call" | custom-call | tf_op jit(solution)/shard_map/attend_early/pallas_call | solution.py:304
  30.2 0.0 collective-permute-done.refs_1_.refs_2_
  30.2 4.0 %collective-permute-done.1.refs_2_.refs_3_ = bf16[512,256]{1,0:T(8,128)(2,1)S(1)} collective-permute-done((bf16[512,256]{1,0:T(8,128)(2,1)}, bf16[512,256]{1,0:T(8,128)(2,1)S(1)}, u32[]{:S(2)}, u32[]{:S(2)}) %collective-permute-start.1) | collective-permute-done | bytes 262176 | tf_op jit(solution)/shard_map/ppermute | solution.py:23
  34.3 0.0 collective-permute-done.2.refs_3_.refs_4_
  34.3 0.9 %copy-done = bf16[512,256]{1,0:T(8,128)(2,1)S(1)} copy-done((bf16[512,256]{1,0:T(8,128)(2,1)S(1)}, bf16[512,256]{1,0:T(8,128)(2,1)}, u32[]{:S(2)}) %copy-start) | copy-done | bytes 262168
  35.2 0.1 collective-permute-start.10
  35.3 1.9 %collective-permute-done.10.refs_5_ = bf16[4,256,256]{2,1,0:T(8,128)(2,1)S(1)} collective-permute-done((bf16[4,256,256]{2,1,0:T(8,128)(2,1)S(1)}, bf16[4,256,256]{2,1,0:T(8,128)(2,1)S(1)}, u32[]{:S(2)}, u32[]{:S(2)}) %collective-permute-start.10) | collective-permute-done | bytes 524320 | tf_op jit(solution)/shard_map/ppermute | solution.py:23
  37.2 6.8 %attend_late.1 = (bf16[256,256]{1,0:T(8,128)(2,1)S(1)}, bf16[256,256]{1,0:T(8,128)(2,1)S(1)}, bf16[256,256]{1,0:T(8,128)(2,1)S(1)}, bf16[256,256]{1,0:T(8,128)(2...) custom-call(s32[32,6]{1,0:T(8,128)S(1)} %copy.11.refs_0_, ...), custom_call_target="tpu_custom_call", output_to_operand_aliasing={{9}: (10, {}), {10}: (11, {})} | custom-call | flops 1342177280 | bytes 4194304 | tf_op jit(solution)/shard_map/attend_late/pallas_call | solution.py:304
  44.0 0.2 collective-permute-start.11
  44.2 1.2 %collective-permute-start.15 = (bf16[256,256]{1,0:T(8,128)(2,1)S(1)}, bf16[256,256]{1,0:T(8,128)(2,1)S(1)}, u32[]{:S(2)}, u32[]{:S(2)}) collective-permute-start(bf16[256,256]{1,0:T(8,128)(2,1)S(1)} %get-tuple-element.54), channel_id=1, source_target_pairs={{0,8},{4,12},{8,0},{12,4},{16,24},{20,28},{24,16},{28,20},{1,9},{5... | collective-permute-start | bytes 393224 | tf_op jit(solution)/shard_map/ppermute | solution.py:23
  45.4 1.3 %collective-permute-done.11.refs_0_ = bf16[4,512,256]{2,1,0:T(8,128)(2,1)S(1)} collective-permute-done((bf16[4,512,256]{2,1,0:T(8,128)(2,1)S(1)}, bf16[4,512,256]{2,1,0:T(8,128)(2,1)S(1)}, u32[]{:S(2)}, u32[]{:S(2)}) %collective-permute-start.11) | collective-permute-done | bytes 1048608 | tf_op jit(solution)/shard_map/ppermute | solution.py:23
  46.7 0.3 add_partials.1
  47.0 1.2 %collective-permute-start.12 = (bf16[512,256]{1,0:T(8,128)(2,1)S(1)}, bf16[512,256]{1,0:T(8,128)(2,1)S(1)}, u32[]{:S(2)}, u32[]{:S(2)}) collective-permute-start(bf16[512,256]{1,0:T(8,128)(2,1)S(1)} %get-tuple-element.50), channel_id=1, source_target_pairs={{0,8},{4,12},{8,0},{12,4},{16,24},{20,28},{24,16},{28,20},{1,9},{5... | collective-permute-start | bytes 786440 | tf_op jit(solution)/shard_map/ppermute | solution.py:23
  48.3 0.9 %collective-permute-start.13 = (bf16[512,256]{1,0:T(8,128)(2,1)S(1)}, bf16[512,256]{1,0:T(8,128)(2,1)S(1)}, u32[]{:S(2)}, u32[]{:S(2)}) collective-permute-start(bf16[512,256]{1,0:T(8,128)(2,1)S(1)} %get-tuple-element.51), channel_id=1, source_target_pairs={{0,16},{4,20},{8,24},{12,28},{16,0},{20,4},{24,8},{28,12},{1,17},{... | collective-permute-start | bytes 786440 | tf_op jit(solution)/shard_map/ppermute | solution.py:23
  49.2 1.4 %collective-permute-start.14 = (bf16[512,256]{1,0:T(8,128)(2,1)S(1)}, bf16[512,256]{1,0:T(8,128)(2,1)S(1)}, u32[]{:S(2)}, u32[]{:S(2)}) collective-permute-start(bf16[512,256]{1,0:T(8,128)(2,1)S(1)} %get-tuple-element.52), channel_id=1, source_target_pairs={{0,24},{4,28},{8,16},{12,20},{16,8},{20,12},{24,0},{28,4},{1,25},{... | collective-permute-start | bytes 786440 | tf_op jit(solution)/shard_map/ppermute | solution.py:23
  50.6 1.5 %collective-permute-start.16 = (bf16[256,256]{1,0:T(8,128)(2,1)S(1)}, bf16[256,256]{1,0:T(8,128)(2,1)S(1)}, u32[]{:S(2)}, u32[]{:S(2)}) collective-permute-start(bf16[256,256]{1,0:T(8,128)(2,1)S(1)} %get-tuple-element.55), channel_id=1, source_target_pairs={{0,16},{4,20},{8,24},{12,28},{16,0},{20,4},{24,8},{28,12},{1,17},{... | collective-permute-start | bytes 393224 | tf_op jit(solution)/shard_map/ppermute | solution.py:23
  52.1 0.0 collective-permute-done.15.refs_5_
  52.1 1.1 %collective-permute-start.17 = (bf16[256,256]{1,0:T(8,128)(2,1)S(1)}, bf16[256,256]{1,0:T(8,128)(2,1)S(1)}, u32[]{:S(2)}, u32[]{:S(2)}) collective-permute-start(bf16[256,256]{1,0:T(8,128)(2,1)S(1)} %get-tuple-element.56), channel_id=1, source_target_pairs={{0,24},{4,28},{8,16},{12,20},{16,8},{20,12},{24,0},{28,4},{1,25},{... | collective-permute-start | bytes 393224 | tf_op jit(solution)/shard_map/ppermute | solution.py:23
  53.2 14.4 %collective-permute-done.16.refs_6_ = bf16[256,256]{1,0:T(8,128)(2,1)S(1)} collective-permute-done((bf16[256,256]{1,0:T(8,128)(2,1)S(1)}, bf16[256,256]{1,0:T(8,128)(2,1)S(1)}, u32[]{:S(2)}, u32[]{:S(2)}) %collective-permute-start.16) | collective-permute-done | bytes 131104 | tf_op jit(solution)/shard_map/ppermute | solution.py:23
  67.6 0.0 collective-permute-done.17.refs_7_
  67.6 0.0 collective-permute-done.12.refs_1_
  67.6 0.0 collective-permute-done.13.refs_2_
  67.6 0.0 collective-permute-done.14.refs_3_
  67.6 1.4 %join_heads.1 = (bf16[512,512]{1,0:T(8,128)(2,1)}, bf16[512,512]{1,0:T(8,128)(2,1)}, bf16[512,512]{1,0:T(8,128)(2,1)}) custom-call(bf16[512,256]{1,0:T(8,128)(2,1)S(1)} %get-tuple-element.49.refs_0_, bf16[512,256]{1,0:T(8,128)(2,1)S(1)} %collective-permute-done.12.refs_1_, bf16[512,256]{1,0:T(8,128)(2,1)S(1)} %collective-permute-done.13.refs_2_, ...), custom_call_target="tpu_custom_call" | custom-call | bytes 3145728 | tf_op jit(solution)/shard_map/join_heads/pallas_call | solution.py:114
  (2 shorter events, 0.0 us)
Async XLA Ops:
  0.6 21.7 %copy-start.2 = (s32[32,6]{0,1:T(8,128)S(1)}, s32[32,6]{0,1:T(8,128)}, u32[]{:S(2)}) copy-start(s32[32,6]{0,1:T(8,128)} %param.9) | copy-start | bytes 2308
  3.0 10.3 %collective-permute-start.3 = (bf16[512,256]{1,0:T(8,128)(2,1)}, bf16[512,256]{1,0:T(8,128)(2,1)S(1)}, u32[]{:S(2)}, u32[]{:S(2)}) collective-permute-start(bf16[512,256]{1,0:T(8,128)(2,1)} %get-tuple-element.35), channel_id=1, source_target_pairs={{0,8},{4,12},{8,0},{12,4},{16,24},{20,28},{24,16},{28,20},{1,9},{5... | collective-permute-start | bytes 786440 | tf_op jit(solution)/shard_map/ppermute | solution.py:23
  6.0 13.6 %collective-permute-start.4 = (bf16[512,256]{1,0:T(8,128)(2,1)}, bf16[512,256]{1,0:T(8,128)(2,1)S(1)}, u32[]{:S(2)}, u32[]{:S(2)}) collective-permute-start(bf16[512,256]{1,0:T(8,128)(2,1)} %get-tuple-element.36), channel_id=1, source_target_pairs={{0,16},{4,20},{8,24},{12,28},{16,0},{20,4},{24,8},{28,12},{1,17},{... | collective-permute-start | bytes 786440 | tf_op jit(solution)/shard_map/ppermute | solution.py:23
  7.6 12.1 %collective-permute-start.5 = (bf16[512,256]{1,0:T(8,128)(2,1)}, bf16[512,256]{1,0:T(8,128)(2,1)S(1)}, u32[]{:S(2)}, u32[]{:S(2)}) collective-permute-start(bf16[512,256]{1,0:T(8,128)(2,1)} %get-tuple-element.37), channel_id=1, source_target_pairs={{0,24},{4,28},{8,16},{12,20},{16,8},{20,12},{24,0},{28,4},{1,25},{... | collective-permute-start | bytes 786440 | tf_op jit(solution)/shard_map/ppermute | solution.py:23
  7.6 12.6 %collective-permute-start.6 = (bf16[512,256]{1,0:T(8,128)(2,1)}, bf16[512,256]{1,0:T(8,128)(2,1)S(1)}, u32[]{:S(2)}, u32[]{:S(2)}) collective-permute-start(bf16[512,256]{1,0:T(8,128)(2,1)} %get-tuple-element.30.refs_4_.refs_1_), channel_id=1, source_target_pairs={{0,4},{4,0},{8,12},{12,8},{16,20},{20,16},{24,28},{28,24},{1,5},{5... | collective-permute-start | bytes 786440 | tf_op jit(solution)/shard_map/ppermute | solution.py:23
  13.4 8.3 %collective-permute-start.7 = (bf16[512,256]{1,0:T(8,128)(2,1)S(1)}, bf16[512,256]{1,0:T(8,128)(2,1)S(1)}, u32[]{:S(2)}, u32[]{:S(2)}) collective-permute-start(bf16[512,256]{1,0:T(8,128)(2,1)S(1)} %collective-permute-done.3.refs_2_), channel_id=1, source_target_pairs={{0,4},{4,0},{8,12},{12,8},{16,20},{20,16},{24,28},{28,24},{1,5},{5... | collective-permute-start | bytes 786440 | tf_op jit(solution)/shard_map/ppermute | solution.py:23
  15.8 14.5 %collective-permute-start = (bf16[512,256]{1,0:T(8,128)(2,1)}, bf16[512,256]{1,0:T(8,128)(2,1)S(1)}, u32[]{:S(2)}, u32[]{:S(2)}) collective-permute-start(bf16[512,256]{1,0:T(8,128)(2,1)} %get-tuple-element.32), channel_id=1, source_target_pairs={{0,8},{4,12},{8,0},{12,4},{16,24},{20,28},{24,16},{28,20},{1,9},{5... | collective-permute-start | bytes 786440 | tf_op jit(solution)/shard_map/ppermute | solution.py:23
  19.6 2.8 %collective-permute-start.8 = (bf16[512,256]{1,0:T(8,128)(2,1)S(1)}, bf16[512,256]{1,0:T(8,128)(2,1)S(1)}, u32[]{:S(2)}, u32[]{:S(2)}) collective-permute-start(bf16[512,256]{1,0:T(8,128)(2,1)S(1)} %collective-permute-done.4.refs_3_), channel_id=1, source_target_pairs={{0,4},{4,0},{8,12},{12,8},{16,20},{20,16},{24,28},{28,24},{1,5},{5... | collective-permute-start | bytes 786440 | tf_op jit(solution)/shard_map/ppermute | solution.py:23
  19.6 2.8 %collective-permute-start.9 = (bf16[512,256]{1,0:T(8,128)(2,1)S(1)}, bf16[512,256]{1,0:T(8,128)(2,1)S(1)}, u32[]{:S(2)}, u32[]{:S(2)}) collective-permute-start(bf16[512,256]{1,0:T(8,128)(2,1)S(1)} %collective-permute-done.5.refs_4_), channel_id=1, source_target_pairs={{0,4},{4,0},{8,12},{12,8},{16,20},{20,16},{24,28},{28,24},{1,5},{5... | collective-permute-start | bytes 786440 | tf_op jit(solution)/shard_map/ppermute | solution.py:23
  20.1 14.1 %collective-permute-start.1 = (bf16[512,256]{1,0:T(8,128)(2,1)}, bf16[512,256]{1,0:T(8,128)(2,1)S(1)}, u32[]{:S(2)}, u32[]{:S(2)}) collective-permute-start(bf16[512,256]{1,0:T(8,128)(2,1)} %get-tuple-element.33), channel_id=1, source_target_pairs={{0,16},{4,20},{8,24},{12,28},{16,0},{20,4},{24,8},{28,12},{1,17},{... | collective-permute-start | bytes 786440 | tf_op jit(solution)/shard_map/ppermute | solution.py:23
  21.7 12.6 %collective-permute-start.2 = (bf16[512,256]{1,0:T(8,128)(2,1)}, bf16[512,256]{1,0:T(8,128)(2,1)S(1)}, u32[]{:S(2)}, u32[]{:S(2)}) collective-permute-start(bf16[512,256]{1,0:T(8,128)(2,1)} %get-tuple-element.34), channel_id=1, source_target_pairs={{0,24},{4,28},{8,16},{12,20},{16,8},{20,12},{24,0},{28,4},{1,25},{... | collective-permute-start | bytes 786440 | tf_op jit(solution)/shard_map/ppermute | solution.py:23
  22.4 1.0 %copy-start.1 = (bf16[512,256]{1,0:T(8,128)(2,1)S(1)}, bf16[512,256]{1,0:T(8,128)(2,1)}, u32[]{:S(2)}) copy-start(bf16[512,256]{1,0:T(8,128)(2,1)} %get-tuple-element.30.refs_4_.refs_1_) | copy-start | bytes 786436
  34.3 1.0 %copy-start = (bf16[512,256]{1,0:T(8,128)(2,1)S(1)}, bf16[512,256]{1,0:T(8,128)(2,1)}, u32[]{:S(2)}) copy-start(bf16[512,256]{1,0:T(8,128)(2,1)} %get-tuple-element.31.refs_0_.refs_1_) | copy-start | bytes 786436
  35.2 2.0 %collective-permute-start.10 = (bf16[4,256,256]{2,1,0:T(8,128)(2,1)S(1)}, bf16[4,256,256]{2,1,0:T(8,128)(2,1)S(1)}, u32[]{:S(2)}, u32[]{:S(2)}) collective-permute-start(bf16[4,256,256]{2,1,0:T(8,128)(2,1)S(1)} %only_pairs.1), channel_id=1, source_target_pairs={{0,4},{4,0},{8,12},{12,8},{16,20},{20,16},{24,28},{28,24},{1,5},{5... | collective-permute-start | bytes 1572872 | tf_op jit(solution)/shard_map/ppermute | solution.py:23
  44.0 2.7 %collective-permute-start.11 = (bf16[4,512,256]{2,1,0:T(8,128)(2,1)S(1)}, bf16[4,512,256]{2,1,0:T(8,128)(2,1)S(1)}, u32[]{:S(2)}, u32[]{:S(2)}) collective-permute-start(bf16[4,512,256]{2,1,0:T(8,128)(2,1)S(1)} %get-tuple-element.44), channel_id=1, source_target_pairs={{0,4},{4,0},{8,12},{12,8},{16,20},{20,16},{24,28},{28,24},{1,5},{5... | collective-permute-start | bytes 3145736 | tf_op jit(solution)/shard_map/ppermute | solution.py:23
  44.2 7.9 %collective-permute-start.15 = (bf16[256,256]{1,0:T(8,128)(2,1)S(1)}, bf16[256,256]{1,0:T(8,128)(2,1)S(1)}, u32[]{:S(2)}, u32[]{:S(2)}) collective-permute-start(bf16[256,256]{1,0:T(8,128)(2,1)S(1)} %get-tuple-element.54), channel_id=1, source_target_pairs={{0,8},{4,12},{8,0},{12,4},{16,24},{20,28},{24,16},{28,20},{1,9},{5... | collective-permute-start | bytes 393224 | tf_op jit(solution)/shard_map/ppermute | solution.py:23
  47.0 20.6 %collective-permute-start.12 = (bf16[512,256]{1,0:T(8,128)(2,1)S(1)}, bf16[512,256]{1,0:T(8,128)(2,1)S(1)}, u32[]{:S(2)}, u32[]{:S(2)}) collective-permute-start(bf16[512,256]{1,0:T(8,128)(2,1)S(1)} %get-tuple-element.50), channel_id=1, source_target_pairs={{0,8},{4,12},{8,0},{12,4},{16,24},{20,28},{24,16},{28,20},{1,9},{5... | collective-permute-start | bytes 786440 | tf_op jit(solution)/shard_map/ppermute | solution.py:23
  48.3 19.3 %collective-permute-start.13 = (bf16[512,256]{1,0:T(8,128)(2,1)S(1)}, bf16[512,256]{1,0:T(8,128)(2,1)S(1)}, u32[]{:S(2)}, u32[]{:S(2)}) collective-permute-start(bf16[512,256]{1,0:T(8,128)(2,1)S(1)} %get-tuple-element.51), channel_id=1, source_target_pairs={{0,16},{4,20},{8,24},{12,28},{16,0},{20,4},{24,8},{28,12},{1,17},{... | collective-permute-start | bytes 786440 | tf_op jit(solution)/shard_map/ppermute | solution.py:23
  49.2 18.4 %collective-permute-start.14 = (bf16[512,256]{1,0:T(8,128)(2,1)S(1)}, bf16[512,256]{1,0:T(8,128)(2,1)S(1)}, u32[]{:S(2)}, u32[]{:S(2)}) collective-permute-start(bf16[512,256]{1,0:T(8,128)(2,1)S(1)} %get-tuple-element.52), channel_id=1, source_target_pairs={{0,24},{4,28},{8,16},{12,20},{16,8},{20,12},{24,0},{28,4},{1,25},{... | collective-permute-start | bytes 786440 | tf_op jit(solution)/shard_map/ppermute | solution.py:23
  50.6 17.0 %collective-permute-start.16 = (bf16[256,256]{1,0:T(8,128)(2,1)S(1)}, bf16[256,256]{1,0:T(8,128)(2,1)S(1)}, u32[]{:S(2)}, u32[]{:S(2)}) collective-permute-start(bf16[256,256]{1,0:T(8,128)(2,1)S(1)} %get-tuple-element.55), channel_id=1, source_target_pairs={{0,16},{4,20},{8,24},{12,28},{16,0},{20,4},{24,8},{28,12},{1,17},{... | collective-permute-start | bytes 393224 | tf_op jit(solution)/shard_map/ppermute | solution.py:23
  52.1 15.5 %collective-permute-start.17 = (bf16[256,256]{1,0:T(8,128)(2,1)S(1)}, bf16[256,256]{1,0:T(8,128)(2,1)S(1)}, u32[]{:S(2)}, u32[]{:S(2)}) collective-permute-start(bf16[256,256]{1,0:T(8,128)(2,1)S(1)} %get-tuple-element.56), channel_id=1, source_target_pairs={{0,24},{4,28},{8,16},{12,20},{16,8},{20,12},{24,0},{28,4},{1,25},{... | collective-permute-start | bytes 393224 | tf_op jit(solution)/shard_map/ppermute | solution.py:23

commit v4 on v3

--- a/solution.py
+++ b/solution.py
@@ -14,6 +14,7 @@
 LINKS = 6
 SPAN = WIN + LINKS
 NEG_FILL = -1e30
+LATE_PAD = 16
 SPLIT_LIMIT = 56 * 1024 * 1024
 SMALL_LIMIT = 16 * 1024 * 1024
 
@@ -23,9 +24,13 @@
     return lax.ppermute(x, "ctx", [(i, i ^ by) for i in range(count)])
 
 
-def chip_column(members, s):
+def apart(s, groups):
+    return lax.rem(groups - s, groups)
+
+
+def chip_column(members, groups, s):
     chip = lax.div(lax.axis_index("ctx"), members)
-    return pl.ds(pl.multiple_of((chip ^ s) * HEAD_DIM, HEAD_DIM), HEAD_DIM)
+    return pl.ds(pl.multiple_of((chip ^ (-s % groups)) * HEAD_DIM, HEAD_DIM), HEAD_DIM)
 
 
 def all_started(moves, sems):
@@ -38,53 +43,87 @@
     return copies
 
 
-def split_heads_kernel(which, members, groups, *refs):
-    query, key, value, grad = refs[:4]
-    outs = refs[-1 - groups : -1]
-    half = query.shape[0] // 2
-    taken = pl.ds(which * half, half)
-    moves = []
-    for s in range(groups):
-        column = chip_column(members, s)
-        for t, (pair, ask) in enumerate(((key, query), (value, grad))):
-            lanes = pl.ds(t * HEAD_DIM, HEAD_DIM)
-            moves.append((pair.at[taken, column], outs[s].at[pl.ds(0, half), lanes]))
-            moves.append((ask.at[taken, column], outs[s].at[pl.ds(half, half), lanes]))
-    for copy in all_started(moves, refs[-1]):
+def fill_pack(out, held, at, column):
+    query, key, value, grad = held
+    half = at.stop - at.start
+    for t, (pair, ask) in enumerate(((key, query), (value, grad))):
+        lanes = slice(t * HEAD_DIM, (t + 1) * HEAD_DIM)
+        out[:half, lanes] = pair[at, column]
+        out[half : 2 * half, lanes] = ask[at, column]
+
+
+def split_first_kernel(members, groups, *refs):
+    held, sems = refs[4 + groups - 1 : -1], refs[-1]
+    half = held[0].shape[0]
+    for copy in all_started(
+        [(array.at[pl.ds(0, half)], buf) for array, buf in zip(refs[:4], held)], sems
+    ):
         copy.wait()
-
-
-def split_heads(which, arrays, after, members, groups):
-    rows = arrays[0].shape[0]
+    for s in range(1, groups):
+        column = chip_column(members, groups, s)
+        fill_pack(refs[4 + s - 1], held, slice(0, half), column)
+
+
+def split_rest_kernel(members, groups, *refs):
+    held = refs[:4]
+    own, late = refs[4], refs[5:]
+    rows = held[0].shape[0]
+    half = rows // 2
+    fill_pack(own, held, slice(0, half), chip_column(members, groups, 0))
+    for s in range(groups):
+        fill_pack(late[s], held, slice(half, rows), chip_column(members, groups, s))
+        late[s][rows:, :] = jnp.zeros_like(late[s][rows:, :])
+
+
+def split_heads(arrays, members, groups):
+    rows, width = arrays[0].shape
+    half = rows // 2
     out = jax.ShapeDtypeStruct((rows, 2 * HEAD_DIM), jnp.bfloat16)
-    return pl.pallas_call(
-        functools.partial(split_heads_kernel, which, members, groups),
-        out_shape=[out] * groups,
-        in_specs=[pl.BlockSpec(memory_space=pl.ANY)] * (len(arrays) + len(after)),
-        out_specs=[pl.BlockSpec(memory_space=pltpu.VMEM)] * groups,
-        scratch_shapes=[pltpu.SemaphoreType.DMA((4 * groups,))],
+    longer = jax.ShapeDtypeStruct((rows + LATE_PAD, 2 * HEAD_DIM), jnp.bfloat16)
+    vmem = pl.BlockSpec(memory_space=pltpu.VMEM)
+    early = pl.pallas_call(
+        functools.partial(split_first_kernel, members, groups),
+        out_shape=[out] * (groups - 1),
+        in_specs=[pl.BlockSpec(memory_space=pl.ANY)] * 4,
+        out_specs=[vmem] * (groups - 1),
+        scratch_shapes=[pltpu.VMEM((half, width), array.dtype) for array in arrays]
+        + [pltpu.SemaphoreType.DMA((4,))],
         compiler_params=pltpu.CompilerParams(vmem_limit_bytes=SPLIT_LIMIT),
         cost_estimate=pl.CostEstimate(
-            flops=0, bytes_accessed=8 * groups * rows * HEAD_DIM, transcendentals=0
-        ),
-        name="split_late" if which else "split_early",
-    )(*arrays, *after)
+            flops=0, bytes_accessed=16 * half * width, transcendentals=0
+        ),
+        name="split_first",
+    )(*arrays)
+    own, *late = pl.pallas_call(
+        functools.partial(split_rest_kernel, members, groups),
+        out_shape=[out] + [longer] * groups,
+        in_specs=[vmem] * 4,
+        out_specs=[vmem] * (groups + 1),
+        compiler_params=pltpu.CompilerParams(vmem_limit_bytes=SMALL_LIMIT),
+        cost_estimate=pl.CostEstimate(
+            flops=0, bytes_accessed=16 * half * width, transcendentals=0
+        ),
+        name="split_rest",
+    )(*arrays)
+    return [own, *early], late
 
 
 def pairs_kernel(groups, *refs):
-    out = refs[-1]
-    for s in range(groups):
-        out[s] = refs[s][: out.shape[1], :]
-
-
-def only_pairs(packs, after, groups):
-    half = packs[0].shape[0] // 2
+    outs = refs[-(groups // 2) :]
+    for s in range(groups):
+        out = outs[s // 2]
+        out[s % 2] = refs[s][: out.shape[1], :]
+
+
+def only_pairs(packs, half, after, groups):
+    hbm = pl.BlockSpec(memory_space=pl.ANY)
     vmem = pl.BlockSpec(memory_space=pltpu.VMEM)
+    outs = groups // 2
     return pl.pallas_call(
         functools.partial(pairs_kernel, groups),
-        out_shape=jax.ShapeDtypeStruct((groups, half, 2 * HEAD_DIM), jnp.bfloat16),
-        in_specs=[vmem] * groups + [pl.BlockSpec(memory_space=pl.ANY)] * len(after),
-        out_specs=vmem,
+        out_shape=[jax.ShapeDtypeStruct((2, half, 2 * HEAD_DIM), jnp.bfloat16)] * outs,
+        in_specs=[vmem] * groups + [hbm] * len(after),
+        out_specs=[vmem] * outs,
         compiler_params=pltpu.CompilerParams(vmem_limit_bytes=SMALL_LIMIT),
         cost_estimate=pl.CostEstimate(
             flops=0, bytes_accessed=8 * groups * half * HEAD_DIM, transcendentals=0
@@ -93,35 +132,52 @@
     )(*packs, *after)
 
 
-def join_heads_kernel(members, groups, *refs):
-    pairs = refs[:groups]
-    dqs = refs[groups : 2 * groups]
-    outs = refs[2 * groups :]
-    for s in range(groups):
-        column = chip_column(members, s)
-        outs[1][:, column] = pairs[s][:, :HEAD_DIM]
-        outs[2][:, column] = pairs[s][:, HEAD_DIM:]
-        for n in range(outs[0].shape[0] // BLK):
+def join_queries_kernel(members, groups, *refs):
+    out, token = refs[-2:]
+    token[...] = jnp.zeros_like(token)
+    for s in range(groups):
+        column = chip_column(members, groups, s)
+        for n in range(out.shape[0] // BLK):
             packed = slice(n // 2 * BLK, (n // 2 + 1) * BLK)
             lanes = slice(n % 2 * HEAD_DIM, (n % 2 + 1) * HEAD_DIM)
-            outs[0][n * BLK : (n + 1) * BLK, column] = dqs[s][packed, lanes]
+            out[n * BLK : (n + 1) * BLK, column] = refs[s][packed, lanes]
+
+
+def join_pairs_kernel(members, groups, *refs):
+    outs = refs[-2:]
+    for s in range(groups):
+        column = chip_column(members, groups, s)
+        outs[0][:, column] = refs[s][:, :HEAD_DIM]
+        outs[1][:, column] = refs[s][:, HEAD_DIM:]
 
 
 def join_heads(dqs, pairs, members, groups):
     rows = pairs[0].shape[0]
     vmem = pl.BlockSpec(memory_space=pltpu.VMEM)
     out = jax.ShapeDtypeStruct((rows, groups * HEAD_DIM), jnp.bfloat16)
-    return pl.pallas_call(
-        functools.partial(join_heads_kernel, members, groups),
-        out_shape=[out] * 3,
-        in_specs=[vmem] * (2 * groups),
-        out_specs=[vmem] * 3,
-        compiler_params=pltpu.CompilerParams(vmem_limit_bytes=SMALL_LIMIT),
-        cost_estimate=pl.CostEstimate(
-            flops=0, bytes_accessed=12 * rows * groups * HEAD_DIM, transcendentals=0
-        ),
-        name="join_heads",
-    )(*pairs, *dqs)
+    token = jax.ShapeDtypeStruct((8, HEAD_DIM), jnp.float32)
+    bytes_out = 2 * rows * groups * HEAD_DIM
+    query_grad, token = pl.pallas_call(
+        functools.partial(join_queries_kernel, members, groups),
+        out_shape=[out, token],
+        in_specs=[vmem] * groups,
+        out_specs=[vmem] * 2,
+        compiler_params=pltpu.CompilerParams(vmem_limit_bytes=SMALL_LIMIT),
+        cost_estimate=pl.CostEstimate(
+            flops=0, bytes_accessed=200 * bytes_out, transcendentals=0
+        ),
+        name="join_queries",
+    )(*dqs)
+    key_grad, value_grad = pl.pallas_call(
+        functools.partial(join_pairs_kernel, members, groups),
+        out_shape=[out] * 2,
+        in_specs=[vmem] * (groups + 1),
+        out_specs=[vmem] * 2,
+        compiler_params=pltpu.CompilerParams(vmem_limit_bytes=SMALL_LIMIT),
+        cost_estimate=pl.CostEstimate(flops=0, bytes_accessed=4 * bytes_out, transcendentals=0),
+        name="join_pairs",
+    )(*pairs, token)
+    return query_grad, key_grad, value_grad
 
 
 def add_kernel(members, groups, *refs):
@@ -161,40 +217,39 @@
     rows = 2 * half
     stretch = half // BLK
     links = refs[0]
-    refs = refs[1:]
+    packs = [*refs[1 : 1 + groups]]
+    lent = (members - 1) * (groups // 2)
+    for part in refs[1 + groups : 1 + groups + lent]:
+        packs += [part.at[n] for n in range(2)]
+    refs = refs[1 + groups + lent :]
     if late:
-        packs = [*refs[:groups]]
-        for part in refs[groups : groups + members - 1]:
-            packs += [part.at[s] for s in range(groups)]
-        dq_early = refs[groups + members - 1 : 2 * groups + members - 1]
-        refs = refs[2 * groups + members + 1 :]
+        dq_early = refs[:groups]
+        refs = refs[groups + 2 :]
         dq_outs = refs[:groups]
         own_outs = refs[groups : 2 * groups]
         far_outs = refs[2 * groups : 2 * groups + members - 1]
         refs = refs[2 * groups + members - 1 :]
     else:
-        packs = refs[:slots]
-        dq_outs = refs[slots : slots + groups]
-        refs = refs[slots + groups :]
+        dq_outs = refs[:groups]
+        refs = refs[groups:]
     pair_buf, acc, ask_buf, dq_buf, sems = refs
     device = lax.axis_index("ctx")
 
     moves = []
-    for i in range(slots):
-        place = pl.ds(i * rows + (half if late else 0), half)
-        moves.append((packs[i].at[pl.ds(0, half)], pair_buf.at[place]))
     for s in range(groups):
         moves.append((packs[s].at[pl.ds(half, half)], ask_buf.at[pl.ds(s * half, half)]))
-    if near:
-        for source, target in moves:
-            target[...] = source[...]
-    else:
-        copies = all_started(moves, sems)
+        for r in range(members):
+            i = r * groups + s
+            place = pl.ds(i * rows + (half if late else 0), half)
+            moves.append((packs[i].at[pl.ds(0, half)], pair_buf.at[place]))
+    by_copy = 0 if near else len(moves)
+    copies = all_started(moves[:by_copy], sems)
+    for source, target in moves[by_copy:]:
+        target[...] = source[...]
     if not late:
         acc[...] = jnp.zeros_like(acc)
-    if not near:
-        for copy in copies:
-            copy.wait()
+    for copy in copies:
+        copy.wait()
 
     scaling = HEAD_DIM**-0.5
     causal = lax.broadcasted_iota(jnp.int32, (BLK, BLK), 0) <= lax.broadcasted_iota(
@@ -210,12 +265,12 @@
             is_late = run >= shards
             owner = jnp.where(is_late, 2 * shards - 1 - run, run)
             local = local + jnp.where(is_late, stretch, 0)
-        apart = owner ^ device
-        slot = lax.rem(apart, members) * groups + lax.div(apart, members)
+        bits = owner ^ device
+        slot = lax.rem(bits, members) * groups + apart(lax.div(bits, members), groups)
         return pl.multiple_of(slot * rows + local * BLK, BLK)
 
     def step(s, _):
-        asker = device ^ (s * members)
+        asker = device ^ (apart(s, groups) * members)
         first = (2 * shards - 1 - asker if late else asker) * stretch
         units = range(stretch)
         listed = []
@@ -283,10 +338,9 @@
                 far_outs[r - 1][s] = acc[start : start + rows, :].astype(jnp.bfloat16)
 
 
-def attend(links, packs, dq_early, buffers, shards, members, groups):
+def attend(links, packs, dq_early, buffers, rows, shards, members, groups):
     late = len(buffers) > 0
-    half = packs[0].shape[0] // 2
-    rows = 2 * half
+    half = rows // 2
     slots = members * groups
     blocks = groups * half // BLK
     near = slots * rows <= 4096
@@ -330,11 +384,12 @@
 
 
 def to_chips(parts, members):
-    return [parts[0]] + [swapped(part, s * members) for s, part in enumerate(parts[1:], 1)]
+    groups = len(parts)
+    return [swapped(part, -s % groups * members) if s else part for s, part in enumerate(parts)]
 
 
 def with_members(parts, members):
-    return parts + [swapped(part, r) for r in range(1, members) for part in parts]
+    return [swapped(part, r) for r in range(1, members) for part in parts]
 
 
 def per_device(query, key, value, out_grad, links):
@@ -344,18 +399,17 @@
     members = shards // groups
     arrays = (query, key, value, out_grad)
 
-    early = split_heads(0, arrays, [], members, groups)
-    late = split_heads(1, arrays, early[:1], members, groups)
-    early = with_members(to_chips(early, members), members)
+    early, late = split_heads(arrays, members, groups)
+    early = to_chips(early, members)
     late = to_chips(late, members)
-    dq_early, buffers = attend(links, early, [], [], shards, members, groups)
-    lent = only_pairs(late, dq_early[:1], groups)
-    late = late + [swapped(lent, r) for r in range(1, members)]
-    dqs, own, far = attend(links, late, dq_early, buffers, shards, members, groups)
+    early = early + with_members(only_pairs(early, rows // 2, [], groups), members)
+    dq_early, buffers = attend(links, early, [], [], rows, shards, members, groups)
+    late = late + with_members(only_pairs(late, rows // 2, dq_early[:1], groups), members)
+    dqs, own, far = attend(links, late, dq_early, buffers, rows, shards, members, groups)
     far = [swapped(part, r) for r, part in enumerate(far, 1)]
     dqs = to_chips(dqs, members)
     pairs = to_chips(add_partials(far, own, members, groups), members)
-    return tuple(join_heads(dqs, pairs, members, groups))
+    return join_heads(dqs, pairs, members, groups)
 
 
 def solution(mesh):

time: 69.4 us -> 64.6 us (0.931)
  the two profiles are of different devices: /device:TPU:0 before, /device:TPU:31 now
where the time goes in v4:
time: 64.6 us; the launch traced here: 64.3 us
  waiting for transfers between devices  24.2 us (37%)
  Pallas kernels  19.3 us (30%)
  starting transfers between devices  15.9 us (25%)
  local copies, waits for them, and re-layouts  4.26 us (7%)
  between operations  0.73 us (1%)
    ppermute x17, waiting for transfers between devices, swapped(): return lax.ppermute(x, 'ctx', [(i, i ^ by) for i in range(count)])  24.2 us
    ppermute x17, starting transfers between devices, swapped(): return lax.ppermute(x, 'ctx', [(i, i ^ by) for i in range(count)])  15.9 us
    pallas_call x2, Pallas kernels, attend(): pl.pallas_call(functools.partial(attend_kernel, late, near, shards, membe...  13.6 us
    unnamed x11, local copies, waits for them, and re-layouts  4.26 us
    pallas_call x1, Pallas kernels, split_heads(): pl.pallas_call(functools.partial(split_first_kernel, members, groups), ou...  2.24 us
  transfers between devices with their start and end apart: 17, of which 8 were waited for; matrix products, arithmetic and copies ran while one was open for 0% of the time, Pallas kernels for 14%

profile of v4, /device:TPU:31, one launch (start us, length us, event | category | flops | bytes accessed | tf_op | source)
XLA Modules:
  0.0 64.3 jit_solution(6853749341240701557)
XLA Ops:
  0.6 0.0 copy-start.4
  0.6 2.2 %split_first.1 = (bf16[512,256]{1,0:T(8,128)(2,1)}, bf16[512,256]{1,0:T(8,128)(2,1)}, bf16[512,256]{1,0:T(8,128)(2,1)}) custom-call(bf16[512,512]{1,0:T(8,128)(2,1)} %refs_0_.5, bf16[512,512]{1,0:T(8,128)(2,1)} %refs_1_.3, bf16[512,512]{1,0:T(8,128)(2,1)} %refs_2_.3, bf16[512,512]{1,0:T(8,128)(2,1)} %refs_3_.3), custom_call_target="tpu_custom_call" | custom-call | bytes 2097152 | tf_op jit(solution)/shard_map/split_first/pallas_call | solution.py:84
  2.9 0.3 collective-permute-start.3
  3.1 1.2 %collective-permute-start.4 = (bf16[512,256]{1,0:T(8,128)(2,1)}, bf16[512,256]{1,0:T(8,128)(2,1)S(1)}, u32[]{:S(2)}, u32[]{:S(2)}) collective-permute-start(bf16[512,256]{1,0:T(8,128)(2,1)} %get-tuple-element.44), channel_id=1, source_target_pairs={{0,16},{4,20},{8,24},{12,28},{16,0},{20,4},{24,8},{28,12},{1,17},{... | collective-permute-start | bytes 786440 | tf_op jit(solution)/shard_map/ppermute | solution.py:24
  4.4 1.2 %collective-permute-start.5 = (bf16[512,256]{1,0:T(8,128)(2,1)}, bf16[512,256]{1,0:T(8,128)(2,1)S(1)}, u32[]{:S(2)}, u32[]{:S(2)}) collective-permute-start(bf16[512,256]{1,0:T(8,128)(2,1)} %get-tuple-element.45), channel_id=1, source_target_pairs={{0,8},{4,12},{8,0},{12,4},{16,24},{20,28},{24,16},{28,20},{1,9},{5... | collective-permute-start | bytes 786440 | tf_op jit(solution)/shard_map/ppermute | solution.py:24
  5.6 1.0 %copy-done = bf16[512,512]{1,0:T(8,128)(2,1)S(1)} copy-done((bf16[512,512]{1,0:T(8,128)(2,1)S(1)}, bf16[512,512]{1,0:T(8,128)(2,1)}, u32[]{:S(2)}) %copy-start) | copy-done | bytes 524312
  6.6 1.0 %copy-done.1 = bf16[512,512]{1,0:T(8,128)(2,1)S(1)} copy-done((bf16[512,512]{1,0:T(8,128)(2,1)S(1)}, bf16[512,512]{1,0:T(8,128)(2,1)}, u32[]{:S(2)}) %copy-start.1) | copy-done | bytes 524312
  7.7 1.0 %copy-done.2 = bf16[512,512]{1,0:T(8,128)(2,1)S(1)} copy-done((bf16[512,512]{1,0:T(8,128)(2,1)S(1)}, bf16[512,512]{1,0:T(8,128)(2,1)}, u32[]{:S(2)}) %copy-start.2) | copy-done | bytes 524312
  8.7 1.0 %copy-done.3 = bf16[512,512]{1,0:T(8,128)(2,1)S(1)} copy-done((bf16[512,512]{1,0:T(8,128)(2,1)S(1)}, bf16[512,512]{1,0:T(8,128)(2,1)}, u32[]{:S(2)}) %copy-start.3) | copy-done | bytes 524312
  9.8 0.2 split_rest.1
  10.0 0.3 collective-permute-start
  10.3 1.2 %collective-permute-start.1 = (bf16[528,256]{1,0:T(8,128)(2,1)S(1)}, bf16[528,256]{1,0:T(8,128)(2,1)S(1)}, u32[]{:S(2)}, u32[]{:S(2)}) collective-permute-start(bf16[528,256]{1,0:T(8,128)(2,1)S(1)} %get-tuple-element.40), channel_id=1, source_target_pairs={{0,16},{4,20},{8,24},{12,28},{16,0},{20,4},{24,8},{28,12},{1,17},{... | collective-permute-start | bytes 811016 | tf_op jit(solution)/shard_map/ppermute | solution.py:24
  11.5 0.0 collective-permute-done.3.refs_1_.refs_2_
  11.5 1.2 %collective-permute-start.2 = (bf16[528,256]{1,0:T(8,128)(2,1)S(1)}, bf16[528,256]{1,0:T(8,128)(2,1)S(1)}, u32[]{:S(2)}, u32[]{:S(2)}) collective-permute-start(bf16[528,256]{1,0:T(8,128)(2,1)S(1)} %get-tuple-element.41), channel_id=1, source_target_pairs={{0,8},{4,12},{8,0},{12,4},{16,24},{20,28},{24,16},{28,20},{1,9},{5... | collective-permute-start | bytes 811016 | tf_op jit(solution)/shard_map/ppermute | solution.py:24
  12.7 3.8 %collective-permute-done.4.refs_2_.refs_3_ = bf16[512,256]{1,0:T(8,128)(2,1)S(1)} collective-permute-done((bf16[512,256]{1,0:T(8,128)(2,1)}, bf16[512,256]{1,0:T(8,128)(2,1)S(1)}, u32[]{:S(2)}, u32[]{:S(2)}) %collective-permute-start.4) | collective-permute-done | bytes 262176 | tf_op jit(solution)/shard_map/ppermute | solution.py:24
  16.5 0.0 collective-permute-done.5.refs_3_.refs_4_
  16.5 0.8 %only_pairs.2 = (bf16[2,256,256]{2,1,0:T(8,128)(2,1)}, bf16[2,256,256]{2,1,0:T(8,128)(2,1)}) custom-call(bf16[512,256]{1,0:T(8,128)(2,1)S(1)} %get-tuple-element.42.refs_0_.refs_1_, bf16[512,256]{1,0:T(8,128)(2,1)S(1)} %collective-permute-done.3.refs_1_.refs_2_, bf16[512,256]{1,0:T(8,128)(2,1)S(1)} %collective-permute-done.4.refs_2_.refs_3_, ...), custom_call_target="tpu_custom_call" | custom-call | bytes 1048576 | tf_op jit(solution)/shard_map/only_pairs/pallas_call | solution.py:122
  17.4 6.7 %collective-permute-start.6 = (bf16[2,256,256]{2,1,0:T(8,128)(2,1)}, bf16[2,256,256]{2,1,0:T(8,128)(2,1)S(1)}, u32[]{:S(2)}, u32[]{:S(2)}) collective-permute-start(bf16[2,256,256]{2,1,0:T(8,128)(2,1)} %get-tuple-element.46), channel_id=1, source_target_pairs={{0,4},{4,0},{8,12},{12,8},{16,20},{20,16},{24,28},{28,24},{1,5},{5... | collective-permute-start | bytes 786440 | tf_op jit(solution)/shard_map/ppermute | solution.py:24
  24.1 0.0 collective-permute-start.7
  24.1 0.1 copy.11.refs_0_
  24.2 1.3 %collective-permute-done.6.refs_5_ = bf16[2,256,256]{2,1,0:T(8,128)(2,1)S(1)} collective-permute-done((bf16[2,256,256]{2,1,0:T(8,128)(2,1)}, bf16[2,256,256]{2,1,0:T(8,128)(2,1)S(1)}, u32[]{:S(2)}, u32[]{:S(2)}) %collective-permute-start.6) | collective-permute-done | bytes 262176 | tf_op jit(solution)/shard_map/ppermute | solution.py:24
  25.4 0.4 collective-permute-done.7.refs_6_
  25.8 6.8 %attend_early.1 = (bf16[128,256]{1,0:T(8,128)(2,1)S(1)}, bf16[128,256]{1,0:T(8,128)(2,1)S(1)}, bf16[128,256]{1,0:T(8,128)(2,1)S(1)}, bf16[128,256]{1,0:T(8,128)(...) custom-call(s32[32,6]{1,0:T(8,128)S(1)} %copy.11.refs_0_, ...), custom_call_target="tpu_custom_call" | custom-call | tf_op jit(solution)/shard_map/attend_early/pallas_call | solution.py:358
  32.6 0.0 collective-permute-done.refs_1_.refs_2_
  32.6 0.0 collective-permute-done.1.refs_2_.refs_3_
  32.7 0.0 collective-permute-done.2.refs_3_.refs_4_
  32.7 0.4 collective-permute-start.8
  33.1 0.1 collective-permute-start.9
  33.3 1.0 %collective-permute-done.8.refs_5_ = bf16[2,256,256]{2,1,0:T(8,128)(2,1)S(1)} collective-permute-done((bf16[2,256,256]{2,1,0:T(8,128)(2,1)S(1)}, bf16[2,256,256]{2,1,0:T(8,128)(2,1)S(1)}, u32[]{:S(2)}, u32[]{:S(2)}) %collective-permute-start.8) | collective-permute-done | bytes 262176 | tf_op jit(solution)/shard_map/ppermute | solution.py:24
  34.3 0.4 collective-permute-done.9.refs_6_
  34.7 6.8 %attend_late.1 = (bf16[256,256]{1,0:T(8,128)(2,1)S(1)}, bf16[256,256]{1,0:T(8,128)(2,1)S(1)}, bf16[256,256]{1,0:T(8,128)(2,1)S(1)}, bf16[256,256]{1,0:T(8,128)(2...) custom-call(s32[32,6]{1,0:T(8,128)S(1)} %copy.11.refs_0_, ...), custom_call_target="tpu_custom_call", output_to_operand_aliasing={{9}: (11, {}), {10}: (12, {})} | custom-call | flops 1342177280 | bytes 4194304 | tf_op jit(solution)/shard_map/attend_late/pallas_call | solution.py:358
  41.4 0.4 collective-permute-start.13
  41.9 0.0 collective-permute-start.10
  41.9 2.3 %collective-permute-done.13.refs_0_ = bf16[4,512,256]{2,1,0:T(8,128)(2,1)S(1)} collective-permute-done((bf16[4,512,256]{2,1,0:T(8,128)(2,1)S(1)}, bf16[4,512,256]{2,1,0:T(8,128)(2,1)S(1)}, u32[]{:S(2)}, u32[]{:S(2)}) %collective-permute-start.13) | collective-permute-done | bytes 1048608 | tf_op jit(solution)/shard_map/ppermute | solution.py:24
  44.2 0.3 add_partials.1
  44.5 0.1 collective-permute-start.14
  44.6 0.0 collective-permute-start.15
  44.7 2.6 %collective-permute-start.16 = (bf16[512,256]{1,0:T(8,128)(2,1)S(1)}, bf16[512,256]{1,0:T(8,128)(2,1)S(1)}, u32[]{:S(2)}, u32[]{:S(2)}) collective-permute-start(bf16[512,256]{1,0:T(8,128)(2,1)S(1)} %get-tuple-element.69), channel_id=1, source_target_pairs={{0,8},{4,12},{8,0},{12,4},{16,24},{20,28},{24,16},{28,20},{1,9},{5... | collective-permute-start | bytes 786440 | tf_op jit(solution)/shard_map/ppermute | solution.py:24
  47.2 0.0 collective-permute-start.11
  47.2 0.5 collective-permute-done.10.refs_1_
  47.8 0.0 collective-permute-start.12
  47.8 14.5 %collective-permute-done.11.refs_2_ = bf16[256,256]{1,0:T(8,128)(2,1)S(1)} collective-permute-done((bf16[256,256]{1,0:T(8,128)(2,1)S(1)}, bf16[256,256]{1,0:T(8,128)(2,1)S(1)}, u32[]{:S(2)}, u32[]{:S(2)}) %collective-permute-start.11) | collective-permute-done | bytes 131104 | tf_op jit(solution)/shard_map/ppermute | solution.py:24
  62.3 0.0 collective-permute-done.12.refs_3_
  62.3 0.9 %join_queries.1 = (bf16[512,512]{1,0:T(8,128)(2,1)}, f32[8,128]{1,0:T(8,128)S(1)}) custom-call(bf16[256,256]{1,0:T(8,128)(2,1)S(1)} %get-tuple-element.56.refs_0_, bf16[256,256]{1,0:T(8,128)(2,1)S(1)} %collective-permute-done.10.refs_1_, bf16[256,256]{1,0:T(8,128)(2,1)S(1)} %collective-permute-done.11.refs_2_, ...), custom_call_target="tpu_custom_call" | custom-call | bytes 104857600 | tf_op jit(solution)/shard_map/join_queries/pallas_call | solution.py:160
  63.1 0.0 collective-permute-done.14.refs_1_
  63.2 0.0 collective-permute-done.15.refs_2_
  63.2 0.0 collective-permute-done.16.refs_3_
  63.2 1.2 %join_pairs.1 = (bf16[512,512]{1,0:T(8,128)(2,1)}, bf16[512,512]{1,0:T(8,128)(2,1)}) custom-call(bf16[512,256]{1,0:T(8,128)(2,1)S(1)} %get-tuple-element.66.refs_0_, bf16[512,256]{1,0:T(8,128)(2,1)S(1)} %collective-permute-done.14.refs_1_, bf16[512,256]{1,0:T(8,128)(2,1)S(1)} %collective-permute-done.15.refs_2_, ...), custom_call_target="tpu_custom_call" | custom-call | bytes 2097152 | tf_op jit(solution)/shard_map/join_pairs/pallas_call | solution.py:171
  (6 shorter events, 0.0 us)
Async XLA Ops:
  0.6 23.4 %copy-start.4 = (s32[32,6]{0,1:T(8,128)S(1)}, s32[32,6]{0,1:T(8,128)}, u32[]{:S(2)}) copy-start(s32[32,6]{0,1:T(8,128)} %param.9) | copy-start | bytes 2308
  2.9 8.6 %collective-permute-start.3 = (bf16[512,256]{1,0:T(8,128)(2,1)}, bf16[512,256]{1,0:T(8,128)(2,1)S(1)}, u32[]{:S(2)}, u32[]{:S(2)}) collective-permute-start(bf16[512,256]{1,0:T(8,128)(2,1)} %get-tuple-element.43), channel_id=1, source_target_pairs={{0,24},{4,28},{8,16},{12,20},{16,8},{20,12},{24,0},{28,4},{1,25},{... | collective-permute-start | bytes 786440 | tf_op jit(solution)/shard_map/ppermute | solution.py:24
  3.1 13.4 %collective-permute-start.4 = (bf16[512,256]{1,0:T(8,128)(2,1)}, bf16[512,256]{1,0:T(8,128)(2,1)S(1)}, u32[]{:S(2)}, u32[]{:S(2)}) collective-permute-start(bf16[512,256]{1,0:T(8,128)(2,1)} %get-tuple-element.44), channel_id=1, source_target_pairs={{0,16},{4,20},{8,24},{12,28},{16,0},{20,4},{24,8},{28,12},{1,17},{... | collective-permute-start | bytes 786440 | tf_op jit(solution)/shard_map/ppermute | solution.py:24
  4.4 12.2 %collective-permute-start.5 = (bf16[512,256]{1,0:T(8,128)(2,1)}, bf16[512,256]{1,0:T(8,128)(2,1)S(1)}, u32[]{:S(2)}, u32[]{:S(2)}) collective-permute-start(bf16[512,256]{1,0:T(8,128)(2,1)} %get-tuple-element.45), channel_id=1, source_target_pairs={{0,8},{4,12},{8,0},{12,4},{16,24},{20,28},{24,16},{28,20},{1,9},{5... | collective-permute-start | bytes 786440 | tf_op jit(solution)/shard_map/ppermute | solution.py:24
  5.6 1.0 %copy-start = (bf16[512,512]{1,0:T(8,128)(2,1)S(1)}, bf16[512,512]{1,0:T(8,128)(2,1)}, u32[]{:S(2)}) copy-start(bf16[512,512]{1,0:T(8,128)(2,1)} %refs_0_.5) | copy-start | bytes 1572868
  6.6 1.0 %copy-start.1 = (bf16[512,512]{1,0:T(8,128)(2,1)S(1)}, bf16[512,512]{1,0:T(8,128)(2,1)}, u32[]{:S(2)}) copy-start(bf16[512,512]{1,0:T(8,128)(2,1)} %refs_1_.3) | copy-start | bytes 1572868
  7.7 1.0 %copy-start.2 = (bf16[512,512]{1,0:T(8,128)(2,1)S(1)}, bf16[512,512]{1,0:T(8,128)(2,1)}, u32[]{:S(2)}) copy-start(bf16[512,512]{1,0:T(8,128)(2,1)} %refs_2_.3) | copy-start | bytes 1572868
  8.7 1.0 %copy-start.3 = (bf16[512,512]{1,0:T(8,128)(2,1)S(1)}, bf16[512,512]{1,0:T(8,128)(2,1)}, u32[]{:S(2)}) copy-start(bf16[512,512]{1,0:T(8,128)(2,1)} %refs_3_.3) | copy-start | bytes 1572868
  10.0 22.6 %collective-permute-start = (bf16[528,256]{1,0:T(8,128)(2,1)S(1)}, bf16[528,256]{1,0:T(8,128)(2,1)S(1)}, u32[]{:S(2)}, u32[]{:S(2)}) collective-permute-start(bf16[528,256]{1,0:T(8,128)(2,1)S(1)} %get-tuple-element.39), channel_id=1, source_target_pairs={{0,24},{4,28},{8,16},{12,20},{16,8},{20,12},{24,0},{28,4},{1,25},{... | collective-permute-start | bytes 811016 | tf_op jit(solution)/shard_map/ppermute | solution.py:24
  10.3 22.4 %collective-permute-start.1 = (bf16[528,256]{1,0:T(8,128)(2,1)S(1)}, bf16[528,256]{1,0:T(8,128)(2,1)S(1)}, u32[]{:S(2)}, u32[]{:S(2)}) collective-permute-start(bf16[528,256]{1,0:T(8,128)(2,1)S(1)} %get-tuple-element.40), channel_id=1, source_target_pairs={{0,16},{4,20},{8,24},{12,28},{16,0},{20,4},{24,8},{28,12},{1,17},{... | collective-permute-start | bytes 811016 | tf_op jit(solution)/shard_map/ppermute | solution.py:24
  11.5 21.1 %collective-permute-start.2 = (bf16[528,256]{1,0:T(8,128)(2,1)S(1)}, bf16[528,256]{1,0:T(8,128)(2,1)S(1)}, u32[]{:S(2)}, u32[]{:S(2)}) collective-permute-start(bf16[528,256]{1,0:T(8,128)(2,1)S(1)} %get-tuple-element.41), channel_id=1, source_target_pairs={{0,8},{4,12},{8,0},{12,4},{16,24},{20,28},{24,16},{28,20},{1,9},{5... | collective-permute-start | bytes 811016 | tf_op jit(solution)/shard_map/ppermute | solution.py:24
  17.4 8.1 %collective-permute-start.6 = (bf16[2,256,256]{2,1,0:T(8,128)(2,1)}, bf16[2,256,256]{2,1,0:T(8,128)(2,1)S(1)}, u32[]{:S(2)}, u32[]{:S(2)}) collective-permute-start(bf16[2,256,256]{2,1,0:T(8,128)(2,1)} %get-tuple-element.46), channel_id=1, source_target_pairs={{0,4},{4,0},{8,12},{12,8},{16,20},{20,16},{24,28},{28,24},{1,5},{5... | collective-permute-start | bytes 786440 | tf_op jit(solution)/shard_map/ppermute | solution.py:24
  24.1 1.7 %collective-permute-start.7 = (bf16[2,256,256]{2,1,0:T(8,128)(2,1)}, bf16[2,256,256]{2,1,0:T(8,128)(2,1)S(1)}, u32[]{:S(2)}, u32[]{:S(2)}) collective-permute-start(bf16[2,256,256]{2,1,0:T(8,128)(2,1)} %get-tuple-element.47), channel_id=1, source_target_pairs={{0,4},{4,0},{8,12},{12,8},{16,20},{20,16},{24,28},{28,24},{1,5},{5... | collective-permute-start | bytes 786440 | tf_op jit(solution)/shard_map/ppermute | solution.py:24
  32.7 1.6 %collective-permute-start.8 = (bf16[2,256,256]{2,1,0:T(8,128)(2,1)S(1)}, bf16[2,256,256]{2,1,0:T(8,128)(2,1)S(1)}, u32[]{:S(2)}, u32[]{:S(2)}) collective-permute-start(bf16[2,256,256]{2,1,0:T(8,128)(2,1)S(1)} %get-tuple-element.49), channel_id=1, source_target_pairs={{0,4},{4,0},{8,12},{12,8},{16,20},{20,16},{24,28},{28,24},{1,5},{5... | collective-permute-start | bytes 786440 | tf_op jit(solution)/shard_map/ppermute | solution.py:24
  33.1 1.5 %collective-permute-start.9 = (bf16[2,256,256]{2,1,0:T(8,128)(2,1)S(1)}, bf16[2,256,256]{2,1,0:T(8,128)(2,1)S(1)}, u32[]{:S(2)}, u32[]{:S(2)}) collective-permute-start(bf16[2,256,256]{2,1,0:T(8,128)(2,1)S(1)} %get-tuple-element.50), channel_id=1, source_target_pairs={{0,4},{4,0},{8,12},{12,8},{16,20},{20,16},{24,28},{28,24},{1,5},{5... | collective-permute-start | bytes 786440 | tf_op jit(solution)/shard_map/ppermute | solution.py:24
  41.4 2.7 %collective-permute-start.13 = (bf16[4,512,256]{2,1,0:T(8,128)(2,1)S(1)}, bf16[4,512,256]{2,1,0:T(8,128)(2,1)S(1)}, u32[]{:S(2)}, u32[]{:S(2)}) collective-permute-start(bf16[4,512,256]{2,1,0:T(8,128)(2,1)S(1)} %get-tuple-element.61), channel_id=1, source_target_pairs={{0,4},{4,0},{8,12},{12,8},{16,20},{20,16},{24,28},{28,24},{1,5},{5... | collective-permute-start | bytes 3145736 | tf_op jit(solution)/shard_map/ppermute | solution.py:24
  41.9 5.9 %collective-permute-start.10 = (bf16[256,256]{1,0:T(8,128)(2,1)S(1)}, bf16[256,256]{1,0:T(8,128)(2,1)S(1)}, u32[]{:S(2)}, u32[]{:S(2)}) collective-permute-start(bf16[256,256]{1,0:T(8,128)(2,1)S(1)} %get-tuple-element.57), channel_id=1, source_target_pairs={{0,24},{4,28},{8,16},{12,20},{16,8},{20,12},{24,0},{28,4},{1,25},{... | collective-permute-start | bytes 393224 | tf_op jit(solution)/shard_map/ppermute | solution.py:24
  44.5 18.7 %collective-permute-start.14 = (bf16[512,256]{1,0:T(8,128)(2,1)S(1)}, bf16[512,256]{1,0:T(8,128)(2,1)S(1)}, u32[]{:S(2)}, u32[]{:S(2)}) collective-permute-start(bf16[512,256]{1,0:T(8,128)(2,1)S(1)} %get-tuple-element.67), channel_id=1, source_target_pairs={{0,24},{4,28},{8,16},{12,20},{16,8},{20,12},{24,0},{28,4},{1,25},{... | collective-permute-start | bytes 786440 | tf_op jit(solution)/shard_map/ppermute | solution.py:24
  44.6 18.5 %collective-permute-start.15 = (bf16[512,256]{1,0:T(8,128)(2,1)S(1)}, bf16[512,256]{1,0:T(8,128)(2,1)S(1)}, u32[]{:S(2)}, u32[]{:S(2)}) collective-permute-start(bf16[512,256]{1,0:T(8,128)(2,1)S(1)} %get-tuple-element.68), channel_id=1, source_target_pairs={{0,16},{4,20},{8,24},{12,28},{16,0},{20,4},{24,8},{28,12},{1,17},{... | collective-permute-start | bytes 786440 | tf_op jit(solution)/shard_map/ppermute | solution.py:24
  44.7 18.5 %collective-permute-start.16 = (bf16[512,256]{1,0:T(8,128)(2,1)S(1)}, bf16[512,256]{1,0:T(8,128)(2,1)S(1)}, u32[]{:S(2)}, u32[]{:S(2)}) collective-permute-start(bf16[512,256]{1,0:T(8,128)(2,1)S(1)} %get-tuple-element.69), channel_id=1, source_target_pairs={{0,8},{4,12},{8,0},{12,4},{16,24},{20,28},{24,16},{28,20},{1,9},{5... | collective-permute-start | bytes 786440 | tf_op jit(solution)/shard_map/ppermute | solution.py:24
  47.2 15.0 %collective-permute-start.11 = (bf16[256,256]{1,0:T(8,128)(2,1)S(1)}, bf16[256,256]{1,0:T(8,128)(2,1)S(1)}, u32[]{:S(2)}, u32[]{:S(2)}) collective-permute-start(bf16[256,256]{1,0:T(8,128)(2,1)S(1)} %get-tuple-element.58), channel_id=1, source_target_pairs={{0,16},{4,20},{8,24},{12,28},{16,0},{20,4},{24,8},{28,12},{1,17},{... | collective-permute-start | bytes 393224 | tf_op jit(solution)/shard_map/ppermute | solution.py:24
  47.8 14.5 %collective-permute-start.12 = (bf16[256,256]{1,0:T(8,128)(2,1)S(1)}, bf16[256,256]{1,0:T(8,128)(2,1)S(1)}, u32[]{:S(2)}, u32[]{:S(2)}) collective-permute-start(bf16[256,256]{1,0:T(8,128)(2,1)S(1)} %get-tuple-element.59), channel_id=1, source_target_pairs={{0,8},{4,12},{8,0},{12,4},{16,24},{20,28},{24,16},{28,20},{1,9},{5... | collective-permute-start | bytes 393224 | tf_op jit(solution)/shard_map/ppermute | solution.py:24

commit v5 on v4

--- a/solution.py
+++ b/solution.py
@@ -1,5 +1,4 @@
 import functools
-import math
 
 import jax
 import jax.numpy as jnp
@@ -145,14 +144,17 @@
 
 def join_pairs_kernel(members, groups, *refs):
     outs = refs[-2:]
-    for s in range(groups):
-        column = chip_column(members, groups, s)
-        outs[0][:, column] = refs[s][:, :HEAD_DIM]
-        outs[1][:, column] = refs[s][:, HEAD_DIM:]
+    half = refs[0].shape[0]
+    for h in range(2):
+        at = slice(h * half, (h + 1) * half)
+        for s in range(groups):
+            column = chip_column(members, groups, s)
+            outs[0][at, column] = refs[h * groups + s][:, :HEAD_DIM]
+            outs[1][at, column] = refs[h * groups + s][:, HEAD_DIM:]
 
 
 def join_heads(dqs, pairs, members, groups):
-    rows = pairs[0].shape[0]
+    rows = 2 * pairs[0].shape[0]
     vmem = pl.BlockSpec(memory_space=pltpu.VMEM)
     out = jax.ShapeDtypeStruct((rows, groups * HEAD_DIM), jnp.bfloat16)
     token = jax.ShapeDtypeStruct((8, HEAD_DIM), jnp.float32)
@@ -171,7 +173,7 @@
     key_grad, value_grad = pl.pallas_call(
         functools.partial(join_pairs_kernel, members, groups),
         out_shape=[out] * 2,
-        in_specs=[vmem] * (groups + 1),
+        in_specs=[vmem] * (2 * groups + 1),
         out_specs=[vmem] * 2,
         compiler_params=pltpu.CompilerParams(vmem_limit_bytes=SMALL_LIMIT),
         cost_estimate=pl.CostEstimate(flops=0, bytes_accessed=4 * bytes_out, transcendentals=0),
@@ -184,28 +186,34 @@
     far = refs[: members - 1]
     own = refs[members - 1 : members - 1 + groups]
     outs = refs[members - 1 + groups :]
-    for s in range(groups):
-        total = own[s][...].astype(jnp.float32)
-        for part in far:
-            total = total + part[s].astype(jnp.float32)
-        outs[s][:, :HEAD_DIM] = (total[:, :HEAD_DIM] * HEAD_DIM**-0.5).astype(jnp.bfloat16)
-        outs[s][:, HEAD_DIM:] = total[:, HEAD_DIM:].astype(jnp.bfloat16)
+    half = outs[0].shape[0]
+    for h in range(2):
+        at = slice(h * half, (h + 1) * half)
+        for s in range(groups):
+            total = own[s][at, :].astype(jnp.float32)
+            for part in far:
+                total = total + part[s, at, :].astype(jnp.float32)
+            out = outs[h * groups + s]
+            out[:, :HEAD_DIM] = (total[:, :HEAD_DIM] * HEAD_DIM**-0.5).astype(jnp.bfloat16)
+            out[:, HEAD_DIM:] = total[:, HEAD_DIM:].astype(jnp.bfloat16)
 
 
 def add_partials(far, own, members, groups):
     vmem = pl.BlockSpec(memory_space=pltpu.VMEM)
-    out = jax.ShapeDtypeStruct(own[0].shape, jnp.bfloat16)
-    return pl.pallas_call(
+    rows = own[0].shape[0]
+    out = jax.ShapeDtypeStruct((rows // 2, 2 * HEAD_DIM), jnp.bfloat16)
+    found = pl.pallas_call(
         functools.partial(add_kernel, members, groups),
-        out_shape=[out] * groups,
+        out_shape=[out] * (2 * groups),
         in_specs=[vmem] * (members - 1 + groups),
-        out_specs=[vmem] * groups,
+        out_specs=[vmem] * (2 * groups),
         compiler_params=pltpu.CompilerParams(vmem_limit_bytes=SMALL_LIMIT),
         cost_estimate=pl.CostEstimate(
             flops=0, bytes_accessed=8 * groups * own[0].size, transcendentals=0
         ),
         name="add_partials",
     )(*far, *own)
+    return found[:groups], found[groups:]
 
 
 def dot(left, right, dims):
@@ -255,7 +263,6 @@
     causal = lax.broadcasted_iota(jnp.int32, (BLK, BLK), 0) <= lax.broadcasted_iota(
         jnp.int32, (BLK, BLK), 1
     )
-    blank = jnp.zeros((BLK, HEAD_DIM), jnp.bfloat16)
 
     def place_of(block):
         run = lax.div(block, stretch)
@@ -279,30 +286,22 @@
             listed.append([block, block - 1] + [links[block, i] for i in range(LINKS)])
         places = [[place_of(jnp.maximum(j, 0)) for j in row] for row in listed]
         pairs = [jnp.concatenate([pair_buf[pl.ds(p, BLK), :] for p in row], 0) for row in places]
-        wide = []
-        for n in units:
-            ask = ask_buf[pl.ds(pl.multiple_of(s * half + n * BLK, BLK), BLK), :]
-            wide.append(
-                jnp.concatenate(
-                    [
-                        jnp.concatenate([ask[:, :HEAD_DIM], blank], 1),
-                        jnp.concatenate([blank, ask[:, HEAD_DIM:]], 1),
-                    ],
-                    0,
-                )
-            )
-        both = [dot(pairs[n], wide[n], ((1,), (1,))) for n in units]
+        asks = [
+            ask_buf[pl.ds(pl.multiple_of(s * half + n * BLK, BLK), BLK), :] for n in units
+        ]
+        raws = [dot(pairs[n][:, :HEAD_DIM], asks[n][:, :HEAD_DIM], ((1,), (1,))) for n in units]
+        dprobs = [dot(pairs[n][:, HEAD_DIM:], asks[n][:, HEAD_DIM:], ((1,), (1,))) for n in units]
         dscore_b, terms = [], []
         for n in units:
-            raw = [both[n][i * BLK : (i + 1) * BLK, :BLK] for i in range(SPAN)]
-            dprob = both[n][:, BLK:].reshape(SPAN, BLK, BLK)
+            raw = [raws[n][i * BLK : (i + 1) * BLK] for i in range(SPAN)]
+            dprob = dprobs[n].reshape(SPAN, BLK, BLK)
             raw[0] = jnp.where(causal, raw[0], NEG_FILL)
             unused = [0.0] + [jnp.where(j >= 0, 0.0, NEG_FILL) for j in listed[n][1:]]
             tops = [jnp.max(raw[i], axis=0, keepdims=True) + unused[i] for i in range(SPAN)]
             top = functools.reduce(jnp.maximum, tops)
             weight = jnp.stack(
                 [
-                    jnp.exp2((raw[i] - (top - unused[i])) * (scaling * math.log2(math.e)))
+                    jnp.exp((raw[i] - (top - unused[i])) * scaling)
                     for i in range(SPAN)
                 ]
             )
@@ -312,7 +311,9 @@
             dscore = (prob * (dprob - delta)).astype(jnp.bfloat16).reshape(SPAN * BLK, BLK)
             dscore_b.append(dscore)
             prob = prob.astype(jnp.bfloat16).reshape(SPAN * BLK, BLK)
-            terms.append(dot(jnp.concatenate([dscore, prob], 1), wide[n], ((1,), (0,))))
+            dk = dot(dscore, asks[n][:, :HEAD_DIM], ((1,), (0,)))
+            dv = dot(prob, asks[n][:, HEAD_DIM:], ((1,), (0,)))
+            terms.append(jnp.concatenate([dk, dv], 1))
         dq = [dot(dscore_b[n], pairs[n][:, :HEAD_DIM], ((0,), (0,))) * scaling for n in units]
         for n in units:
             lanes = slice(n % 2 * HEAD_DIM, (n % 2 + 1) * HEAD_DIM)
@@ -322,13 +323,16 @@
                 acc[pl.ds(p, BLK), :] += terms[n][i * BLK : (i + 1) * BLK]
         return 0
 
-    lax.fori_loop(0, groups, step, 0)
+    lax.fori_loop(0, groups, step, 0, unroll=2)
 
     quarter = half // 2
     for s in range(groups):
         if late:
             dq_outs[s][:quarter] = dq_early[s][...]
-        dq_outs[s][-quarter:] = dq_buf[s * quarter : (s + 1) * quarter, :]
+        start = quarter if late else 0
+        dq_outs[s][start : start + quarter] = dq_buf[s * quarter : (s + 1) * quarter, :]
+        if late:
+            dq_outs[s][half:] = jnp.zeros_like(dq_outs[s][half:])
     if late:
         for s in range(groups):
             own_outs[s][...] = acc[s * rows : (s + 1) * rows, :].astype(jnp.bfloat16)
@@ -348,7 +352,7 @@
     def shape(*dims, dtype=jnp.bfloat16):
         return jax.ShapeDtypeStruct((*dims, 2 * HEAD_DIM), dtype)
 
-    outs = [shape(half if late else half // 2)] * groups
+    outs = [shape(half + LATE_PAD if late else half // 2)] * groups
     if late:
         outs += [shape(rows)] * groups + [shape(groups, rows)] * (members - 1)
     outs += [shape(slots * rows), shape(slots * rows, dtype=jnp.float32)]
@@ -408,7 +412,8 @@
     dqs, own, far = attend(links, late, dq_early, buffers, rows, shards, members, groups)
     far = [swapped(part, r) for r, part in enumerate(far, 1)]
     dqs = to_chips(dqs, members)
-    pairs = to_chips(add_partials(far, own, members, groups), members)
+    pairs = add_partials(far, own, members, groups)
+    pairs = to_chips(pairs[0], members) + to_chips(pairs[1], members)
     return join_heads(dqs, pairs, members, groups)
 
 

time: 64.6 us -> 62.1 us (0.961)
  the two profiles are of different devices: /device:TPU:31 before, /device:TPU:0 now
where the time goes in v5:
time: 62.1 us; the launch traced here: 61.2 us
  starting transfers between devices  22.5 us (36%)
  Pallas kernels  17.3 us (28%)
  waiting for transfers between devices  16.5 us (27%)
  local copies, waits for them, and re-layouts  4.26 us (7%)
  between operations  0.72 us (1%)
    ppermute x20, starting transfers between devices, swapped(): return lax.ppermute(x, 'ctx', [(i, i ^ by) for i in range(count)])  22.5 us
    ppermute x20, waiting for transfers between devices, swapped(): return lax.ppermute(x, 'ctx', [(i, i ^ by) for i in range(count)])  16.5 us
    pallas_call x2, Pallas kernels, attend(): pl.pallas_call(functools.partial(attend_kernel, late, near, shards, membe...  11.6 us
    unnamed x11, local copies, waits for them, and re-layouts  4.26 us
    pallas_call x1, Pallas kernels, split_heads(): pl.pallas_call(functools.partial(split_first_kernel, members, groups), ou...  2.24 us
  transfers between devices with their start and end apart: 20, of which 13 were waited for; matrix products, arithmetic and copies ran while one was open for 0% of the time, Pallas kernels for 13%

profile of v5, /device:TPU:0, one launch (start us, length us, event | category | flops | bytes accessed | tf_op | source)
XLA Modules:
  0.0 61.2 jit_solution(2547109841538512177)
XLA Ops:
  0.6 2.2 %split_first.1 = (bf16[512,256]{1,0:T(8,128)(2,1)}, bf16[512,256]{1,0:T(8,128)(2,1)}, bf16[512,256]{1,0:T(8,128)(2,1)}) custom-call(bf16[512,512]{1,0:T(8,128)(2,1)} %refs_0_.5, bf16[512,512]{1,0:T(8,128)(2,1)} %refs_1_.3, bf16[512,512]{1,0:T(8,128)(2,1)} %refs_2_.3, bf16[512,512]{1,0:T(8,128)(2,1)} %refs_3_.3), custom_call_target="tpu_custom_call" | custom-call | bytes 2097152 | tf_op jit(solution)/shard_map/split_first/pallas_call | solution.py:83
  2.9 4.0 %collective-permute-start.3 = (bf16[512,256]{1,0:T(8,128)(2,1)}, bf16[512,256]{1,0:T(8,128)(2,1)S(1)}, u32[]{:S(2)}, u32[]{:S(2)}) collective-permute-start(bf16[512,256]{1,0:T(8,128)(2,1)} %get-tuple-element.47), channel_id=1, source_target_pairs={{0,24},{4,28},{8,16},{12,20},{16,8},{20,12},{24,0},{28,4},{1,25},{... | collective-permute-start | bytes 786440 | tf_op jit(solution)/shard_map/ppermute | solution.py:23
  6.8 0.5 collective-permute-start.4
  7.3 0.1 collective-permute-start.5
  7.5 1.0 %copy-done = bf16[512,512]{1,0:T(8,128)(2,1)S(1)} copy-done((bf16[512,512]{1,0:T(8,128)(2,1)S(1)}, bf16[512,512]{1,0:T(8,128)(2,1)}, u32[]{:S(2)}) %copy-start) | copy-done | bytes 524312
  8.5 1.0 %copy-done.1 = bf16[512,512]{1,0:T(8,128)(2,1)S(1)} copy-done((bf16[512,512]{1,0:T(8,128)(2,1)S(1)}, bf16[512,512]{1,0:T(8,128)(2,1)}, u32[]{:S(2)}) %copy-start.1) | copy-done | bytes 524312
  9.6 1.0 %copy-done.2 = bf16[512,512]{1,0:T(8,128)(2,1)S(1)} copy-done((bf16[512,512]{1,0:T(8,128)(2,1)S(1)}, bf16[512,512]{1,0:T(8,128)(2,1)}, u32[]{:S(2)}) %copy-start.2) | copy-done | bytes 524312
  10.6 1.0 %copy-done.3 = bf16[512,512]{1,0:T(8,128)(2,1)S(1)} copy-done((bf16[512,512]{1,0:T(8,128)(2,1)S(1)}, bf16[512,512]{1,0:T(8,128)(2,1)}, u32[]{:S(2)}) %copy-start.3) | copy-done | bytes 524312
  11.7 0.2 split_rest.1
  11.9 2.9 %collective-permute-start = (bf16[528,256]{1,0:T(8,128)(2,1)S(1)}, bf16[528,256]{1,0:T(8,128)(2,1)S(1)}, u32[]{:S(2)}, u32[]{:S(2)}) collective-permute-start(bf16[528,256]{1,0:T(8,128)(2,1)S(1)} %get-tuple-element.43), channel_id=1, source_target_pairs={{0,24},{4,28},{8,16},{12,20},{16,8},{20,12},{24,0},{28,4},{1,25},{... | collective-permute-start | bytes 811016 | tf_op jit(solution)/shard_map/ppermute | solution.py:23
  14.8 0.5 collective-permute-start.1
  15.3 0.9 %collective-permute-start.2 = (bf16[528,256]{1,0:T(8,128)(2,1)S(1)}, bf16[528,256]{1,0:T(8,128)(2,1)S(1)}, u32[]{:S(2)}, u32[]{:S(2)}) collective-permute-start(bf16[528,256]{1,0:T(8,128)(2,1)S(1)} %get-tuple-element.45), channel_id=1, source_target_pairs={{0,8},{4,12},{8,0},{12,4},{16,24},{20,28},{24,16},{28,20},{1,9},{5... | collective-permute-start | bytes 811016 | tf_op jit(solution)/shard_map/ppermute | solution.py:23
  16.2 3.7 %collective-permute-done.4.refs_2_.refs_3_ = bf16[512,256]{1,0:T(8,128)(2,1)S(1)} collective-permute-done((bf16[512,256]{1,0:T(8,128)(2,1)}, bf16[512,256]{1,0:T(8,128)(2,1)S(1)}, u32[]{:S(2)}, u32[]{:S(2)}) %collective-permute-start.4) | collective-permute-done | bytes 262176 | tf_op jit(solution)/shard_map/ppermute | solution.py:23
  19.9 0.5 collective-permute-done.5.refs_3_.refs_4_
  20.4 0.8 %only_pairs.2 = (bf16[2,256,256]{2,1,0:T(8,128)(2,1)}, bf16[2,256,256]{2,1,0:T(8,128)(2,1)}) custom-call(bf16[512,256]{1,0:T(8,128)(2,1)S(1)} %get-tuple-element.46.refs_0_.refs_1_, bf16[512,256]{1,0:T(8,128)(2,1)S(1)} %collective-permute-done.3.refs_1_.refs_2_, bf16[512,256]{1,0:T(8,128)(2,1)S(1)} %collective-permute-done.4.refs_2_.refs_3_, ...), custom_call_target="tpu_custom_call" | custom-call | bytes 1048576 | tf_op jit(solution)/shard_map/only_pairs/pallas_call | solution.py:121
  21.2 0.0 collective-permute-start.6
  21.2 0.5 collective-permute-start.7
  21.8 0.1 copy.11.refs_0_
  21.8 1.1 %collective-permute-done.6.refs_5_ = bf16[2,256,256]{2,1,0:T(8,128)(2,1)S(1)} collective-permute-done((bf16[2,256,256]{2,1,0:T(8,128)(2,1)}, bf16[2,256,256]{2,1,0:T(8,128)(2,1)S(1)}, u32[]{:S(2)}, u32[]{:S(2)}) %collective-permute-start.6) | collective-permute-done | bytes 262176 | tf_op jit(solution)/shard_map/ppermute | solution.py:23
  23.0 0.4 collective-permute-done.7.refs_6_
  23.4 5.8 %attend_early.1 = (bf16[128,256]{1,0:T(8,128)(2,1)S(1)}, bf16[128,256]{1,0:T(8,128)(2,1)S(1)}, bf16[128,256]{1,0:T(8,128)(2,1)S(1)}, bf16[128,256]{1,0:T(8,128)(...) custom-call(s32[32,6]{1,0:T(8,128)S(1)} %copy.11.refs_0_, ...), custom_call_target="tpu_custom_call" | custom-call | tf_op jit(solution)/shard_map/attend_early/pallas_call | solution.py:362
  29.1 0.0 collective-permute-done.refs_1_.refs_2_
  29.1 1.4 %collective-permute-done.1.refs_2_.refs_3_ = bf16[528,256]{1,0:T(8,128)(2,1)S(1)} collective-permute-done((bf16[528,256]{1,0:T(8,128)(2,1)S(1)}, bf16[528,256]{1,0:T(8,128)(2,1)S(1)}, u32[]{:S(2)}, u32[]{:S(2)}) %collective-permute-start.1) | collective-permute-done | bytes 270368 | tf_op jit(solution)/shard_map/ppermute | solution.py:23
  30.6 0.3 collective-permute-done.2.refs_3_.refs_4_
  30.9 0.1 collective-permute-start.8
  31.0 0.5 collective-permute-start.9
  31.5 1.0 %collective-permute-done.8.refs_5_ = bf16[2,256,256]{2,1,0:T(8,128)(2,1)S(1)} collective-permute-done((bf16[2,256,256]{2,1,0:T(8,128)(2,1)S(1)}, bf16[2,256,256]{2,1,0:T(8,128)(2,1)S(1)}, u32[]{:S(2)}, u32[]{:S(2)}) %collective-permute-start.8) | collective-permute-done | bytes 262176 | tf_op jit(solution)/shard_map/ppermute | solution.py:23
  32.5 0.4 collective-permute-done.9.refs_6_
  32.9 5.8 %attend_late.1 = (bf16[272,256]{1,0:T(8,128)(2,1)S(1)}, bf16[272,256]{1,0:T(8,128)(2,1)S(1)}, bf16[272,256]{1,0:T(8,128)(2,1)S(1)}, bf16[272,256]{1,0:T(8,128)(2...) custom-call(s32[32,6]{1,0:T(8,128)S(1)} %copy.11.refs_0_, ...), custom_call_target="tpu_custom_call", output_to_operand_aliasing={{9}: (11, {}), {10}: (12, {})} | custom-call | flops 1342177280 | bytes 4194304 | tf_op jit(solution)/shard_map/attend_late/pallas_call | solution.py:362
  38.8 0.2 collective-permute-start.13
  39.0 1.5 %collective-permute-start.10 = (bf16[272,256]{1,0:T(8,128)(2,1)S(1)}, bf16[272,256]{1,0:T(8,128)(2,1)S(1)}, u32[]{:S(2)}, u32[]{:S(2)}) collective-permute-start(bf16[272,256]{1,0:T(8,128)(2,1)S(1)} %get-tuple-element.61), channel_id=1, source_target_pairs={{0,24},{4,28},{8,16},{12,20},{16,8},{20,12},{24,0},{28,4},{1,25},{... | collective-permute-start | bytes 417800 | tf_op jit(solution)/shard_map/ppermute | solution.py:23
  40.5 1.5 %collective-permute-start.11 = (bf16[272,256]{1,0:T(8,128)(2,1)S(1)}, bf16[272,256]{1,0:T(8,128)(2,1)S(1)}, u32[]{:S(2)}, u32[]{:S(2)}) collective-permute-start(bf16[272,256]{1,0:T(8,128)(2,1)S(1)} %get-tuple-element.62), channel_id=1, source_target_pairs={{0,16},{4,20},{8,24},{12,28},{16,0},{20,4},{24,8},{28,12},{1,17},{... | collective-permute-start | bytes 417800 | tf_op jit(solution)/shard_map/ppermute | solution.py:23
  41.9 0.5 collective-permute-start.12
  42.5 0.3 add_partials.1
  42.8 1.5 %collective-permute-start.14 = (bf16[256,256]{1,0:T(8,128)(2,1)S(1)}, bf16[256,256]{1,0:T(8,128)(2,1)S(1)}, u32[]{:S(2)}, u32[]{:S(2)}) collective-permute-start(bf16[256,256]{1,0:T(8,128)(2,1)S(1)} %get-tuple-element.71), channel_id=1, source_target_pairs={{0,24},{4,28},{8,16},{12,20},{16,8},{20,12},{24,0},{28,4},{1,25},{... | collective-permute-start | bytes 393224 | tf_op jit(solution)/shard_map/ppermute | solution.py:23
  44.3 1.5 %collective-permute-start.15 = (bf16[256,256]{1,0:T(8,128)(2,1)S(1)}, bf16[256,256]{1,0:T(8,128)(2,1)S(1)}, u32[]{:S(2)}, u32[]{:S(2)}) collective-permute-start(bf16[256,256]{1,0:T(8,128)(2,1)S(1)} %get-tuple-element.72), channel_id=1, source_target_pairs={{0,16},{4,20},{8,24},{12,28},{16,0},{20,4},{24,8},{28,12},{1,17},{... | collective-permute-start | bytes 393224 | tf_op jit(solution)/shard_map/ppermute | solution.py:23
  45.8 0.6 %collective-permute-done.10.refs_1_ = bf16[272,256]{1,0:T(8,128)(2,1)S(1)} collective-permute-done((bf16[272,256]{1,0:T(8,128)(2,1)S(1)}, bf16[272,256]{1,0:T(8,128)(2,1)S(1)}, u32[]{:S(2)}, u32[]{:S(2)}) %collective-permute-start.10) | collective-permute-done | bytes 139296 | tf_op jit(solution)/shard_map/ppermute | solution.py:23
  46.4 1.5 %collective-permute-start.16 = (bf16[256,256]{1,0:T(8,128)(2,1)S(1)}, bf16[256,256]{1,0:T(8,128)(2,1)S(1)}, u32[]{:S(2)}, u32[]{:S(2)}) collective-permute-start(bf16[256,256]{1,0:T(8,128)(2,1)S(1)} %get-tuple-element.73), channel_id=1, source_target_pairs={{0,8},{4,12},{8,0},{12,4},{16,24},{20,28},{24,16},{28,20},{1,9},{5... | collective-permute-start | bytes 393224 | tf_op jit(solution)/shard_map/ppermute | solution.py:23
  47.9 1.6 %collective-permute-done.11.refs_2_ = bf16[272,256]{1,0:T(8,128)(2,1)S(1)} collective-permute-done((bf16[272,256]{1,0:T(8,128)(2,1)S(1)}, bf16[272,256]{1,0:T(8,128)(2,1)S(1)}, u32[]{:S(2)}, u32[]{:S(2)}) %collective-permute-start.11) | collective-permute-done | bytes 139296 | tf_op jit(solution)/shard_map/ppermute | solution.py:23
  49.5 1.5 %collective-permute-start.17 = (bf16[256,256]{1,0:T(8,128)(2,1)S(1)}, bf16[256,256]{1,0:T(8,128)(2,1)S(1)}, u32[]{:S(2)}, u32[]{:S(2)}) collective-permute-start(bf16[256,256]{1,0:T(8,128)(2,1)S(1)} %get-tuple-element.75), channel_id=1, source_target_pairs={{0,24},{4,28},{8,16},{12,20},{16,8},{20,12},{24,0},{28,4},{1,25},{... | collective-permute-start | bytes 393224 | tf_op jit(solution)/shard_map/ppermute | solution.py:23
  50.9 1.5 %collective-permute-start.18 = (bf16[256,256]{1,0:T(8,128)(2,1)S(1)}, bf16[256,256]{1,0:T(8,128)(2,1)S(1)}, u32[]{:S(2)}, u32[]{:S(2)}) collective-permute-start(bf16[256,256]{1,0:T(8,128)(2,1)S(1)} %get-tuple-element.76), channel_id=1, source_target_pairs={{0,16},{4,20},{8,24},{12,28},{16,0},{20,4},{24,8},{28,12},{1,17},{... | collective-permute-start | bytes 393224 | tf_op jit(solution)/shard_map/ppermute | solution.py:23
  52.4 1.3 %collective-permute-start.19 = (bf16[256,256]{1,0:T(8,128)(2,1)S(1)}, bf16[256,256]{1,0:T(8,128)(2,1)S(1)}, u32[]{:S(2)}, u32[]{:S(2)}) collective-permute-start(bf16[256,256]{1,0:T(8,128)(2,1)S(1)} %get-tuple-element.77), channel_id=1, source_target_pairs={{0,8},{4,12},{8,0},{12,4},{16,24},{20,28},{24,16},{28,20},{1,9},{5... | collective-permute-start | bytes 393224 | tf_op jit(solution)/shard_map/ppermute | solution.py:23
  53.7 0.9 %join_queries.1 = (bf16[512,512]{1,0:T(8,128)(2,1)}, f32[8,128]{1,0:T(8,128)S(1)}) custom-call(bf16[272,256]{1,0:T(8,128)(2,1)S(1)} %get-tuple-element.60.refs_0_, bf16[272,256]{1,0:T(8,128)(2,1)S(1)} %collective-permute-done.10.refs_1_, bf16[272,256]{1,0:T(8,128)(2,1)S(1)} %collective-permute-done.11.refs_2_, ...), custom_call_target="tpu_custom_call" | custom-call | bytes 104857600 | tf_op jit(solution)/shard_map/join_queries/pallas_call | solution.py:162
  54.6 0.4 collective-permute-done.15.refs_2_
  55.1 2.9 %collective-permute-done.17.refs_5_ = bf16[256,256]{1,0:T(8,128)(2,1)S(1)} collective-permute-done((bf16[256,256]{1,0:T(8,128)(2,1)S(1)}, bf16[256,256]{1,0:T(8,128)(2,1)S(1)}, u32[]{:S(2)}, u32[]{:S(2)}) %collective-permute-start.17) | collective-permute-done | bytes 131104 | tf_op jit(solution)/shard_map/ppermute | solution.py:23
  57.9 2.1 %collective-permute-done.18.refs_6_ = bf16[256,256]{1,0:T(8,128)(2,1)S(1)} collective-permute-done((bf16[256,256]{1,0:T(8,128)(2,1)S(1)}, bf16[256,256]{1,0:T(8,128)(2,1)S(1)}, u32[]{:S(2)}, u32[]{:S(2)}) %collective-permute-start.18) | collective-permute-done | bytes 131104 | tf_op jit(solution)/shard_map/ppermute | solution.py:23
  60.0 0.0 collective-permute-done.19.refs_7_
  60.1 1.2 %join_pairs.1 = (bf16[512,512]{1,0:T(8,128)(2,1)}, bf16[512,512]{1,0:T(8,128)(2,1)}) custom-call(bf16[256,256]{1,0:T(8,128)(2,1)S(1)} %get-tuple-element.70.refs_0_, bf16[256,256]{1,0:T(8,128)(2,1)S(1)} %collective-permute-done.14.refs_1_, bf16[256,256]{1,0:T(8,128)(2,1)S(1)} %collective-permute-done.15.refs_2_, ...), custom_call_target="tpu_custom_call" | custom-call | bytes 2097152 | tf_op jit(solution)/shard_map/join_pairs/pallas_call | solution.py:173
  (12 shorter events, 0.1 us)
Async XLA Ops:
  0.6 21.1 %copy-start.4 = (s32[32,6]{0,1:T(8,128)S(1)}, s32[32,6]{0,1:T(8,128)}, u32[]{:S(2)}) copy-start(s32[32,6]{0,1:T(8,128)} %param.9) | copy-start | bytes 2308
  2.9 12.4 %collective-permute-start.3 = (bf16[512,256]{1,0:T(8,128)(2,1)}, bf16[512,256]{1,0:T(8,128)(2,1)S(1)}, u32[]{:S(2)}, u32[]{:S(2)}) collective-permute-start(bf16[512,256]{1,0:T(8,128)(2,1)} %get-tuple-element.47), channel_id=1, source_target_pairs={{0,24},{4,28},{8,16},{12,20},{16,8},{20,12},{24,0},{28,4},{1,25},{... | collective-permute-start | bytes 786440 | tf_op jit(solution)/shard_map/ppermute | solution.py:23
  6.8 13.1 %collective-permute-start.4 = (bf16[512,256]{1,0:T(8,128)(2,1)}, bf16[512,256]{1,0:T(8,128)(2,1)S(1)}, u32[]{:S(2)}, u32[]{:S(2)}) collective-permute-start(bf16[512,256]{1,0:T(8,128)(2,1)} %get-tuple-element.48), channel_id=1, source_target_pairs={{0,16},{4,20},{8,24},{12,28},{16,0},{20,4},{24,8},{28,12},{1,17},{... | collective-permute-start | bytes 786440 | tf_op jit(solution)/shard_map/ppermute | solution.py:23
  7.3 13.1 %collective-permute-start.5 = (bf16[512,256]{1,0:T(8,128)(2,1)}, bf16[512,256]{1,0:T(8,128)(2,1)S(1)}, u32[]{:S(2)}, u32[]{:S(2)}) collective-permute-start(bf16[512,256]{1,0:T(8,128)(2,1)} %get-tuple-element.49), channel_id=1, source_target_pairs={{0,8},{4,12},{8,0},{12,4},{16,24},{20,28},{24,16},{28,20},{1,9},{5... | collective-permute-start | bytes 786440 | tf_op jit(solution)/shard_map/ppermute | solution.py:23
  7.5 1.0 %copy-start = (bf16[512,512]{1,0:T(8,128)(2,1)S(1)}, bf16[512,512]{1,0:T(8,128)(2,1)}, u32[]{:S(2)}) copy-start(bf16[512,512]{1,0:T(8,128)(2,1)} %refs_0_.5) | copy-start | bytes 1572868
  8.5 1.0 %copy-start.1 = (bf16[512,512]{1,0:T(8,128)(2,1)S(1)}, bf16[512,512]{1,0:T(8,128)(2,1)}, u32[]{:S(2)}) copy-start(bf16[512,512]{1,0:T(8,128)(2,1)} %refs_1_.3) | copy-start | bytes 1572868
  9.6 1.0 %copy-start.2 = (bf16[512,512]{1,0:T(8,128)(2,1)S(1)}, bf16[512,512]{1,0:T(8,128)(2,1)}, u32[]{:S(2)}) copy-start(bf16[512,512]{1,0:T(8,128)(2,1)} %refs_2_.3) | copy-start | bytes 1572868
  10.6 1.0 %copy-start.3 = (bf16[512,512]{1,0:T(8,128)(2,1)S(1)}, bf16[512,512]{1,0:T(8,128)(2,1)}, u32[]{:S(2)}) copy-start(bf16[512,512]{1,0:T(8,128)(2,1)} %refs_3_.3) | copy-start | bytes 1572868
  11.9 17.2 %collective-permute-start = (bf16[528,256]{1,0:T(8,128)(2,1)S(1)}, bf16[528,256]{1,0:T(8,128)(2,1)S(1)}, u32[]{:S(2)}, u32[]{:S(2)}) collective-permute-start(bf16[528,256]{1,0:T(8,128)(2,1)S(1)} %get-tuple-element.43), channel_id=1, source_target_pairs={{0,24},{4,28},{8,16},{12,20},{16,8},{20,12},{24,0},{28,4},{1,25},{... | collective-permute-start | bytes 811016 | tf_op jit(solution)/shard_map/ppermute | solution.py:23
  14.8 15.8 %collective-permute-start.1 = (bf16[528,256]{1,0:T(8,128)(2,1)S(1)}, bf16[528,256]{1,0:T(8,128)(2,1)S(1)}, u32[]{:S(2)}, u32[]{:S(2)}) collective-permute-start(bf16[528,256]{1,0:T(8,128)(2,1)S(1)} %get-tuple-element.44), channel_id=1, source_target_pairs={{0,16},{4,20},{8,24},{12,28},{16,0},{20,4},{24,8},{28,12},{1,17},{... | collective-permute-start | bytes 811016 | tf_op jit(solution)/shard_map/ppermute | solution.py:23
  15.3 15.6 %collective-permute-start.2 = (bf16[528,256]{1,0:T(8,128)(2,1)S(1)}, bf16[528,256]{1,0:T(8,128)(2,1)S(1)}, u32[]{:S(2)}, u32[]{:S(2)}) collective-permute-start(bf16[528,256]{1,0:T(8,128)(2,1)S(1)} %get-tuple-element.45), channel_id=1, source_target_pairs={{0,8},{4,12},{8,0},{12,4},{16,24},{20,28},{24,16},{28,20},{1,9},{5... | collective-permute-start | bytes 811016 | tf_op jit(solution)/shard_map/ppermute | solution.py:23
  21.2 1.7 %collective-permute-start.6 = (bf16[2,256,256]{2,1,0:T(8,128)(2,1)}, bf16[2,256,256]{2,1,0:T(8,128)(2,1)S(1)}, u32[]{:S(2)}, u32[]{:S(2)}) collective-permute-start(bf16[2,256,256]{2,1,0:T(8,128)(2,1)} %get-tuple-element.50), channel_id=1, source_target_pairs={{0,4},{4,0},{8,12},{12,8},{16,20},{20,16},{24,28},{28,24},{1,5},{5... | collective-permute-start | bytes 786440 | tf_op jit(solution)/shard_map/ppermute | solution.py:23
  21.2 2.1 %collective-permute-start.7 = (bf16[2,256,256]{2,1,0:T(8,128)(2,1)}, bf16[2,256,256]{2,1,0:T(8,128)(2,1)S(1)}, u32[]{:S(2)}, u32[]{:S(2)}) collective-permute-start(bf16[2,256,256]{2,1,0:T(8,128)(2,1)} %get-tuple-element.51), channel_id=1, source_target_pairs={{0,4},{4,0},{8,12},{12,8},{16,20},{20,16},{24,28},{28,24},{1,5},{5... | collective-permute-start | bytes 786440 | tf_op jit(solution)/shard_map/ppermute | solution.py:23
  30.9 1.6 %collective-permute-start.8 = (bf16[2,256,256]{2,1,0:T(8,128)(2,1)S(1)}, bf16[2,256,256]{2,1,0:T(8,128)(2,1)S(1)}, u32[]{:S(2)}, u32[]{:S(2)}) collective-permute-start(bf16[2,256,256]{2,1,0:T(8,128)(2,1)S(1)} %get-tuple-element.53), channel_id=1, source_target_pairs={{0,4},{4,0},{8,12},{12,8},{16,20},{20,16},{24,28},{28,24},{1,5},{5... | collective-permute-start | bytes 786440 | tf_op jit(solution)/shard_map/ppermute | solution.py:23
  31.0 1.9 %collective-permute-start.9 = (bf16[2,256,256]{2,1,0:T(8,128)(2,1)S(1)}, bf16[2,256,256]{2,1,0:T(8,128)(2,1)S(1)}, u32[]{:S(2)}, u32[]{:S(2)}) collective-permute-start(bf16[2,256,256]{2,1,0:T(8,128)(2,1)S(1)} %get-tuple-element.54), channel_id=1, source_target_pairs={{0,4},{4,0},{8,12},{12,8},{16,20},{20,16},{24,28},{28,24},{1,5},{5... | collective-permute-start | bytes 786440 | tf_op jit(solution)/shard_map/ppermute | solution.py:23
  38.8 3.7 %collective-permute-start.13 = (bf16[4,512,256]{2,1,0:T(8,128)(2,1)S(1)}, bf16[4,512,256]{2,1,0:T(8,128)(2,1)S(1)}, u32[]{:S(2)}, u32[]{:S(2)}) collective-permute-start(bf16[4,512,256]{2,1,0:T(8,128)(2,1)S(1)} %get-tuple-element.65), channel_id=1, source_target_pairs={{0,4},{4,0},{8,12},{12,8},{16,20},{20,16},{24,28},{28,24},{1,5},{5... | collective-permute-start | bytes 3145736 | tf_op jit(solution)/shard_map/ppermute | solution.py:23
  39.0 7.4 %collective-permute-start.10 = (bf16[272,256]{1,0:T(8,128)(2,1)S(1)}, bf16[272,256]{1,0:T(8,128)(2,1)S(1)}, u32[]{:S(2)}, u32[]{:S(2)}) collective-permute-start(bf16[272,256]{1,0:T(8,128)(2,1)S(1)} %get-tuple-element.61), channel_id=1, source_target_pairs={{0,24},{4,28},{8,16},{12,20},{16,8},{20,12},{24,0},{28,4},{1,25},{... | collective-permute-start | bytes 417800 | tf_op jit(solution)/shard_map/ppermute | solution.py:23
  40.5 9.0 %collective-permute-start.11 = (bf16[272,256]{1,0:T(8,128)(2,1)S(1)}, bf16[272,256]{1,0:T(8,128)(2,1)S(1)}, u32[]{:S(2)}, u32[]{:S(2)}) collective-permute-start(bf16[272,256]{1,0:T(8,128)(2,1)S(1)} %get-tuple-element.62), channel_id=1, source_target_pairs={{0,16},{4,20},{8,24},{12,28},{16,0},{20,4},{24,8},{28,12},{1,17},{... | collective-permute-start | bytes 417800 | tf_op jit(solution)/shard_map/ppermute | solution.py:23
  41.9 9.0 %collective-permute-start.12 = (bf16[272,256]{1,0:T(8,128)(2,1)S(1)}, bf16[272,256]{1,0:T(8,128)(2,1)S(1)}, u32[]{:S(2)}, u32[]{:S(2)}) collective-permute-start(bf16[272,256]{1,0:T(8,128)(2,1)S(1)} %get-tuple-element.63), channel_id=1, source_target_pairs={{0,8},{4,12},{8,0},{12,4},{16,24},{20,28},{24,16},{28,20},{1,9},{5... | collective-permute-start | bytes 417800 | tf_op jit(solution)/shard_map/ppermute | solution.py:23
  42.8 9.6 %collective-permute-start.14 = (bf16[256,256]{1,0:T(8,128)(2,1)S(1)}, bf16[256,256]{1,0:T(8,128)(2,1)S(1)}, u32[]{:S(2)}, u32[]{:S(2)}) collective-permute-start(bf16[256,256]{1,0:T(8,128)(2,1)S(1)} %get-tuple-element.71), channel_id=1, source_target_pairs={{0,24},{4,28},{8,16},{12,20},{16,8},{20,12},{24,0},{28,4},{1,25},{... | collective-permute-start | bytes 393224 | tf_op jit(solution)/shard_map/ppermute | solution.py:23
  44.3 10.7 %collective-permute-start.15 = (bf16[256,256]{1,0:T(8,128)(2,1)S(1)}, bf16[256,256]{1,0:T(8,128)(2,1)S(1)}, u32[]{:S(2)}, u32[]{:S(2)}) collective-permute-start(bf16[256,256]{1,0:T(8,128)(2,1)S(1)} %get-tuple-element.72), channel_id=1, source_target_pairs={{0,16},{4,20},{8,24},{12,28},{16,0},{20,4},{24,8},{28,12},{1,17},{... | collective-permute-start | bytes 393224 | tf_op jit(solution)/shard_map/ppermute | solution.py:23
  46.4 8.6 %collective-permute-start.16 = (bf16[256,256]{1,0:T(8,128)(2,1)S(1)}, bf16[256,256]{1,0:T(8,128)(2,1)S(1)}, u32[]{:S(2)}, u32[]{:S(2)}) collective-permute-start(bf16[256,256]{1,0:T(8,128)(2,1)S(1)} %get-tuple-element.73), channel_id=1, source_target_pairs={{0,8},{4,12},{8,0},{12,4},{16,24},{20,28},{24,16},{28,20},{1,9},{5... | collective-permute-start | bytes 393224 | tf_op jit(solution)/shard_map/ppermute | solution.py:23
  49.5 8.5 %collective-permute-start.17 = (bf16[256,256]{1,0:T(8,128)(2,1)S(1)}, bf16[256,256]{1,0:T(8,128)(2,1)S(1)}, u32[]{:S(2)}, u32[]{:S(2)}) collective-permute-start(bf16[256,256]{1,0:T(8,128)(2,1)S(1)} %get-tuple-element.75), channel_id=1, source_target_pairs={{0,24},{4,28},{8,16},{12,20},{16,8},{20,12},{24,0},{28,4},{1,25},{... | collective-permute-start | bytes 393224 | tf_op jit(solution)/shard_map/ppermute | solution.py:23
  50.9 9.1 %collective-permute-start.18 = (bf16[256,256]{1,0:T(8,128)(2,1)S(1)}, bf16[256,256]{1,0:T(8,128)(2,1)S(1)}, u32[]{:S(2)}, u32[]{:S(2)}) collective-permute-start(bf16[256,256]{1,0:T(8,128)(2,1)S(1)} %get-tuple-element.76), channel_id=1, source_target_pairs={{0,16},{4,20},{8,24},{12,28},{16,0},{20,4},{24,8},{28,12},{1,17},{... | collective-permute-start | bytes 393224 | tf_op jit(solution)/shard_map/ppermute | solution.py:23
  52.4 7.7 %collective-permute-start.19 = (bf16[256,256]{1,0:T(8,128)(2,1)S(1)}, bf16[256,256]{1,0:T(8,128)(2,1)S(1)}, u32[]{:S(2)}, u32[]{:S(2)}) collective-permute-start(bf16[256,256]{1,0:T(8,128)(2,1)S(1)} %get-tuple-element.77), channel_id=1, source_target_pairs={{0,8},{4,12},{8,0},{12,4},{16,24},{20,28},{24,16},{28,20},{1,9},{5... | collective-permute-start | bytes 393224 | tf_op jit(solution)/shard_map/ppermute | solution.py:23

commit v6 on v5

--- a/solution.py
+++ b/solution.py
@@ -51,16 +51,37 @@
         out[half : 2 * half, lanes] = ask[at, column]
 
 
-def split_first_kernel(members, groups, *refs):
-    held, sems = refs[4 + groups - 1 : -1], refs[-1]
-    half = held[0].shape[0]
-    for copy in all_started(
-        [(array.at[pl.ds(0, half)], buf) for array, buf in zip(refs[:4], held)], sems
-    ):
+def split_early_kernel(members, groups, wanted, *refs):
+    outs = refs[-1 - len(wanted) : -1]
+    half = outs[0].shape[0] // 2
+    rows = pl.ds(0, half)
+    query, key, value, grad = refs[:4]
+    moves = []
+    for s, out in zip(wanted, outs):
+        column = chip_column(members, groups, s)
+        for t, (pair, ask) in enumerate(((key, query), (value, grad))):
+            lanes = pl.ds(t * HEAD_DIM, HEAD_DIM)
+            moves.append((pair.at[rows, column], out.at[rows, lanes]))
+            moves.append((ask.at[rows, column], out.at[pl.ds(half, half), lanes]))
+    for copy in all_started(moves, refs[-1]):
         copy.wait()
-    for s in range(1, groups):
-        column = chip_column(members, groups, s)
-        fill_pack(refs[4 + s - 1], held, slice(0, half), column)
+
+
+def split_early(wanted, arrays, after, members, groups):
+    rows = arrays[0].shape[0]
+    out = jax.ShapeDtypeStruct((rows, 2 * HEAD_DIM), jnp.bfloat16)
+    return pl.pallas_call(
+        functools.partial(split_early_kernel, members, groups, wanted),
+        out_shape=[out] * len(wanted),
+        in_specs=[pl.BlockSpec(memory_space=pl.ANY)] * (len(arrays) + len(after)),
+        out_specs=[pl.BlockSpec(memory_space=pltpu.VMEM)] * len(wanted),
+        scratch_shapes=[pltpu.SemaphoreType.DMA((4 * len(wanted),))],
+        compiler_params=pltpu.CompilerParams(vmem_limit_bytes=SPLIT_LIMIT),
+        cost_estimate=pl.CostEstimate(
+            flops=0, bytes_accessed=8 * rows * HEAD_DIM * len(wanted), transcendentals=0
+        ),
+        name="split_early",
+    )(*arrays, *after)
 
 
 def split_rest_kernel(members, groups, *refs):
@@ -76,23 +97,11 @@
 
 def split_heads(arrays, members, groups):
     rows, width = arrays[0].shape
-    half = rows // 2
     out = jax.ShapeDtypeStruct((rows, 2 * HEAD_DIM), jnp.bfloat16)
     longer = jax.ShapeDtypeStruct((rows + LATE_PAD, 2 * HEAD_DIM), jnp.bfloat16)
     vmem = pl.BlockSpec(memory_space=pltpu.VMEM)
-    early = pl.pallas_call(
-        functools.partial(split_first_kernel, members, groups),
-        out_shape=[out] * (groups - 1),
-        in_specs=[pl.BlockSpec(memory_space=pl.ANY)] * 4,
-        out_specs=[vmem] * (groups - 1),
-        scratch_shapes=[pltpu.VMEM((half, width), array.dtype) for array in arrays]
-        + [pltpu.SemaphoreType.DMA((4,))],
-        compiler_params=pltpu.CompilerParams(vmem_limit_bytes=SPLIT_LIMIT),
-        cost_estimate=pl.CostEstimate(
-            flops=0, bytes_accessed=16 * half * width, transcendentals=0
-        ),
-        name="split_first",
-    )(*arrays)
+    early = split_early((1,), arrays, [], members, groups)
+    early += split_early(tuple(range(2, groups)), arrays, early, members, groups)
     own, *late = pl.pallas_call(
         functools.partial(split_rest_kernel, members, groups),
         out_shape=[out] + [longer] * groups,
@@ -100,7 +109,7 @@
         out_specs=[vmem] * (groups + 1),
         compiler_params=pltpu.CompilerParams(vmem_limit_bytes=SMALL_LIMIT),
         cost_estimate=pl.CostEstimate(
-            flops=0, bytes_accessed=16 * half * width, transcendentals=0
+            flops=0, bytes_accessed=8 * rows * width, transcendentals=0
         ),
         name="split_rest",
     )(*arrays)
@@ -143,14 +152,21 @@
 
 
 def join_pairs_kernel(members, groups, *refs):
-    outs = refs[-2:]
+    outs, held, sems = refs[-5:-3], refs[-3:-1], refs[-1]
     half = refs[0].shape[0]
+    copies = []
     for h in range(2):
-        at = slice(h * half, (h + 1) * half)
-        for s in range(groups):
-            column = chip_column(members, groups, s)
-            outs[0][at, column] = refs[h * groups + s][:, :HEAD_DIM]
-            outs[1][at, column] = refs[h * groups + s][:, HEAD_DIM:]
+        at = pl.ds(h * half, half)
+        for t in range(2):
+            lanes = slice(t * HEAD_DIM, (t + 1) * HEAD_DIM)
+            for s in range(groups):
+                column = chip_column(members, groups, s)
+                held[t][at, column] = refs[h * groups + s][:, lanes]
+            copy = pltpu.make_async_copy(held[t].at[at], outs[t].at[at], sems.at[2 * h + t])
+            copy.start()
+            copies.append(copy)
+    for copy in copies:
+        copy.wait()
 
 
 def join_heads(dqs, pairs, members, groups):
@@ -174,7 +190,8 @@
         functools.partial(join_pairs_kernel, members, groups),
         out_shape=[out] * 2,
         in_specs=[vmem] * (2 * groups + 1),
-        out_specs=[vmem] * 2,
+        out_specs=[pl.BlockSpec(memory_space=pl.ANY)] * 2,
+        scratch_shapes=[pltpu.VMEM(out.shape, out.dtype)] * 2 + [pltpu.SemaphoreType.DMA((4,))],
         compiler_params=pltpu.CompilerParams(vmem_limit_bytes=SMALL_LIMIT),
         cost_estimate=pl.CostEstimate(flops=0, bytes_accessed=4 * bytes_out, transcendentals=0),
         name="join_pairs",
@@ -331,8 +348,6 @@
             dq_outs[s][:quarter] = dq_early[s][...]
         start = quarter if late else 0
         dq_outs[s][start : start + quarter] = dq_buf[s * quarter : (s + 1) * quarter, :]
-        if late:
-            dq_outs[s][half:] = jnp.zeros_like(dq_outs[s][half:])
     if late:
         for s in range(groups):
             own_outs[s][...] = acc[s * rows : (s + 1) * rows, :].astype(jnp.bfloat16)
@@ -352,7 +367,7 @@
     def shape(*dims, dtype=jnp.bfloat16):
         return jax.ShapeDtypeStruct((*dims, 2 * HEAD_DIM), dtype)
 
-    outs = [shape(half + LATE_PAD if late else half // 2)] * groups
+    outs = [shape(half if late else half // 2)] * groups
     if late:
         outs += [shape(rows)] * groups + [shape(groups, rows)] * (members - 1)
     outs += [shape(slots * rows), shape(slots * rows, dtype=jnp.float32)]

time: 62.1 us -> 60.7 us (0.977); the launches traced: 61.2 us -> 60.5 us
  local copies, waits for them, and re-layouts: 4.26 us -> 0.12 us
  Pallas kernels: 17.3 us -> 18.7 us
  starting transfers between devices: 22.5 us -> 23.7 us
    unnamed x11, local copies, waits for them, and re-layouts: 4.26 us -> 0.12 us
    pallas_call x1 -> x2, Pallas kernels: 2.24 us -> 3.76 us  [split_early(): pl.pallas_call(functools.partial(split_early_kernel, members, groups, wan...]
    ppermute x20, starting transfers between devices: 22.5 us -> 23.7 us  [swapped(): return lax.ppermute(x, 'ctx', [(i, i ^ by) for i in range(count)])]
    ppermute x20, waiting for transfers between devices: 16.5 us -> 17.1 us  [swapped(): return lax.ppermute(x, 'ctx', [(i, i ^ by) for i in range(count)])]
  transfers between devices with their start and end apart: 20 -> 20, of which waited for: 13 -> 15; matrix products, arithmetic and copies ran while one was open for 0% -> 0% of each run, Pallas kernels for 13% -> 16%
where the time goes in v6:
time: 60.7 us; the launch traced here: 60.5 us
  starting transfers between devices  23.7 us (39%)
  Pallas kernels  18.7 us (31%)
  waiting for transfers between devices  17.1 us (28%)
  between operations  0.76 us (1%)
    ppermute x20, starting transfers between devices, swapped(): return lax.ppermute(x, 'ctx', [(i, i ^ by) for i in range(count)])  23.7 us
    ppermute x20, waiting for transfers between devices, swapped(): return lax.ppermute(x, 'ctx', [(i, i ^ by) for i in range(count)])  17.1 us
    pallas_call x2, Pallas kernels, attend(): pl.pallas_call(functools.partial(attend_kernel, late, near, shards, membe...  11.6 us
    pallas_call x2, Pallas kernels, split_early(): pl.pallas_call(functools.partial(split_early_kernel, members, groups, wan...  3.76 us
  transfers between devices with their start and end apart: 20, of which 15 were waited for; matrix products, arithmetic and copies ran while one was open for 0% of the time, Pallas kernels for 16%

profile of v6, /device:TPU:0, one launch (start us, length us, event | category | flops | bytes accessed | tf_op | source)
XLA Modules:
  0.0 60.5 jit_solution(15660461746817625758)
XLA Ops:
  0.6 0.0 copy-start.3
  0.6 0.0 copy-start.2
  0.7 0.0 copy-start.1
  0.7 0.0 copy-start
  0.7 1.8 %split_early.2.refs_4_ = bf16[512,256]{1,0:T(8,128)(2,1)} custom-call(bf16[512,512]{1,0:T(8,128)(2,1)} %refs_0_.7, bf16[512,512]{1,0:T(8,128)(2,1)} %refs_1_.5, bf16[512,512]{1,0:T(8,128)(2,1)} %refs_2_.5, bf16[512,512]{1,0:T(8,128)(2,1)} %refs_3_.5), custom_call_target="tpu_custom_call" | custom-call | bytes 524288 | tf_op jit(solution)/shard_map/split_early/pallas_call | solution.py:73
  2.5 4.0 %collective-permute-start.3 = (bf16[512,256]{1,0:T(8,128)(2,1)}, bf16[512,256]{1,0:T(8,128)(2,1)S(1)}, u32[]{:S(2)}, u32[]{:S(2)}) collective-permute-start(bf16[512,256]{1,0:T(8,128)(2,1)} %split_early.2.refs_4_), channel_id=1, source_target_pairs={{0,24},{4,28},{8,16},{12,20},{16,8},{20,12},{24,0},{28,4},{1,25},{... | collective-permute-start | bytes 786440 | tf_op jit(solution)/shard_map/ppermute | solution.py:23
  6.5 1.9 %split_early.3 = (bf16[512,256]{1,0:T(8,128)(2,1)}, bf16[512,256]{1,0:T(8,128)(2,1)}) custom-call(bf16[512,512]{1,0:T(8,128)(2,1)} %refs_0_.7, bf16[512,512]{1,0:T(8,128)(2,1)} %refs_1_.5, bf16[512,512]{1,0:T(8,128)(2,1)} %refs_2_.5, bf16[512,512]{1,0:T(8,128)(2,1)} %refs_3_.5, bf16[512,256]{1,0:T(8,128)(2,1)} %split_early.2.refs_4_), custom_call_target="tpu_custom_call" | custom-call | bytes 1048576 | tf_op jit(solution)/shard_map/split_early/pallas_call | solution.py:73
  8.4 0.6 collective-permute-start.4
  9.0 0.1 collective-permute-start.5
  9.1 0.2 split_rest.1
  9.4 2.9 %collective-permute-start = (bf16[528,256]{1,0:T(8,128)(2,1)S(1)}, bf16[528,256]{1,0:T(8,128)(2,1)S(1)}, u32[]{:S(2)}, u32[]{:S(2)}) collective-permute-start(bf16[528,256]{1,0:T(8,128)(2,1)S(1)} %get-tuple-element.42), channel_id=1, source_target_pairs={{0,24},{4,28},{8,16},{12,20},{16,8},{20,12},{24,0},{28,4},{1,25},{... | collective-permute-start | bytes 811016 | tf_op jit(solution)/shard_map/ppermute | solution.py:23
  12.3 0.5 collective-permute-start.1
  12.8 1.0 %collective-permute-done.3.refs_1_.refs_2_ = bf16[512,256]{1,0:T(8,128)(2,1)S(1)} collective-permute-done((bf16[512,256]{1,0:T(8,128)(2,1)}, bf16[512,256]{1,0:T(8,128)(2,1)S(1)}, u32[]{:S(2)}, u32[]{:S(2)}) %collective-permute-start.3) | collective-permute-done | bytes 262176 | tf_op jit(solution)/shard_map/ppermute | solution.py:23
  13.8 2.0 %collective-permute-start.2 = (bf16[528,256]{1,0:T(8,128)(2,1)S(1)}, bf16[528,256]{1,0:T(8,128)(2,1)S(1)}, u32[]{:S(2)}, u32[]{:S(2)}) collective-permute-start(bf16[528,256]{1,0:T(8,128)(2,1)S(1)} %get-tuple-element.44), channel_id=1, source_target_pairs={{0,8},{4,12},{8,0},{12,4},{16,24},{20,28},{24,16},{28,20},{1,9},{5... | collective-permute-start | bytes 811016 | tf_op jit(solution)/shard_map/ppermute | solution.py:23
  15.9 3.7 %collective-permute-done.4.refs_2_.refs_3_ = bf16[512,256]{1,0:T(8,128)(2,1)S(1)} collective-permute-done((bf16[512,256]{1,0:T(8,128)(2,1)}, bf16[512,256]{1,0:T(8,128)(2,1)S(1)}, u32[]{:S(2)}, u32[]{:S(2)}) %collective-permute-start.4) | collective-permute-done | bytes 262176 | tf_op jit(solution)/shard_map/ppermute | solution.py:23
  19.5 0.5 collective-permute-done.5.refs_3_.refs_4_
  20.1 0.8 %only_pairs.2 = (bf16[2,256,256]{2,1,0:T(8,128)(2,1)}, bf16[2,256,256]{2,1,0:T(8,128)(2,1)}) custom-call(bf16[512,256]{1,0:T(8,128)(2,1)S(1)} %get-tuple-element.45.refs_0_.refs_1_, bf16[512,256]{1,0:T(8,128)(2,1)S(1)} %collective-permute-done.3.refs_1_.refs_2_, bf16[512,256]{1,0:T(8,128)(2,1)S(1)} %collective-permute-done.4.refs_2_.refs_3_, ...), custom_call_target="tpu_custom_call" | custom-call | bytes 1048576 | tf_op jit(solution)/shard_map/only_pairs/pallas_call | solution.py:130
  20.9 0.5 collective-permute-start.7
  21.4 0.1 copy.11.refs_0_
  21.5 1.1 %collective-permute-done.6.refs_5_ = bf16[2,256,256]{2,1,0:T(8,128)(2,1)S(1)} collective-permute-done((bf16[2,256,256]{2,1,0:T(8,128)(2,1)}, bf16[2,256,256]{2,1,0:T(8,128)(2,1)S(1)}, u32[]{:S(2)}, u32[]{:S(2)}) %collective-permute-start.6) | collective-permute-done | bytes 262176 | tf_op jit(solution)/shard_map/ppermute | solution.py:23
  22.6 0.4 collective-permute-done.7.refs_6_
  23.0 5.8 %attend_early.1 = (bf16[128,256]{1,0:T(8,128)(2,1)S(1)}, bf16[128,256]{1,0:T(8,128)(2,1)S(1)}, bf16[128,256]{1,0:T(8,128)(2,1)S(1)}, bf16[128,256]{1,0:T(8,128)(...) custom-call(s32[32,6]{1,0:T(8,128)S(1)} %copy.11.refs_0_, ...), custom_call_target="tpu_custom_call" | custom-call | tf_op jit(solution)/shard_map/attend_early/pallas_call | solution.py:377
  28.8 1.4 %collective-permute-done.1.refs_2_.refs_3_ = bf16[528,256]{1,0:T(8,128)(2,1)S(1)} collective-permute-done((bf16[528,256]{1,0:T(8,128)(2,1)S(1)}, bf16[528,256]{1,0:T(8,128)(2,1)S(1)}, u32[]{:S(2)}, u32[]{:S(2)}) %collective-permute-start.1) | collective-permute-done | bytes 270368 | tf_op jit(solution)/shard_map/ppermute | solution.py:23
  30.2 0.3 collective-permute-done.2.refs_3_.refs_4_
  30.6 0.1 collective-permute-start.8
  30.7 0.5 collective-permute-start.9
  31.2 1.0 %collective-permute-done.8.refs_5_ = bf16[2,256,256]{2,1,0:T(8,128)(2,1)S(1)} collective-permute-done((bf16[2,256,256]{2,1,0:T(8,128)(2,1)S(1)}, bf16[2,256,256]{2,1,0:T(8,128)(2,1)S(1)}, u32[]{:S(2)}, u32[]{:S(2)}) %collective-permute-start.8) | collective-permute-done | bytes 262176 | tf_op jit(solution)/shard_map/ppermute | solution.py:23
  32.2 0.4 collective-permute-done.9.refs_6_
  32.6 5.8 %attend_late.1 = (bf16[256,256]{1,0:T(8,128)(2,1)S(1)}, bf16[256,256]{1,0:T(8,128)(2,1)S(1)}, bf16[256,256]{1,0:T(8,128)(2,1)S(1)}, bf16[256,256]{1,0:T(8,128)(2...) custom-call(s32[32,6]{1,0:T(8,128)S(1)} %copy.11.refs_0_, ...), custom_call_target="tpu_custom_call", output_to_operand_aliasing={{9}: (11, {}), {10}: (12, {})} | custom-call | flops 1342177280 | bytes 4194304 | tf_op jit(solution)/shard_map/attend_late/pallas_call | solution.py:377
  38.4 0.2 collective-permute-start.13
  38.6 2.3 %collective-permute-start.10 = (bf16[256,256]{1,0:T(8,128)(2,1)S(1)}, bf16[256,256]{1,0:T(8,128)(2,1)S(1)}, u32[]{:S(2)}, u32[]{:S(2)}) collective-permute-start(bf16[256,256]{1,0:T(8,128)(2,1)S(1)} %get-tuple-element.59), channel_id=1, source_target_pairs={{0,24},{4,28},{8,16},{12,20},{16,8},{20,12},{24,0},{28,4},{1,25},{... | collective-permute-start | bytes 393224 | tf_op jit(solution)/shard_map/ppermute | solution.py:23
  40.9 0.6 %collective-permute-start.11 = (bf16[256,256]{1,0:T(8,128)(2,1)S(1)}, bf16[256,256]{1,0:T(8,128)(2,1)S(1)}, u32[]{:S(2)}, u32[]{:S(2)}) collective-permute-start(bf16[256,256]{1,0:T(8,128)(2,1)S(1)} %get-tuple-element.60), channel_id=1, source_target_pairs={{0,16},{4,20},{8,24},{12,28},{16,0},{20,4},{24,8},{28,12},{1,17},{... | collective-permute-start | bytes 393224 | tf_op jit(solution)/shard_map/ppermute | solution.py:23
  41.6 0.5 collective-permute-start.12
  42.1 0.3 add_partials.1
  42.4 2.4 %collective-permute-start.14 = (bf16[256,256]{1,0:T(8,128)(2,1)S(1)}, bf16[256,256]{1,0:T(8,128)(2,1)S(1)}, u32[]{:S(2)}, u32[]{:S(2)}) collective-permute-start(bf16[256,256]{1,0:T(8,128)(2,1)S(1)} %get-tuple-element.69), channel_id=1, source_target_pairs={{0,24},{4,28},{8,16},{12,20},{16,8},{20,12},{24,0},{28,4},{1,25},{... | collective-permute-start | bytes 393224 | tf_op jit(solution)/shard_map/ppermute | solution.py:23
  44.8 0.6 %collective-permute-start.15 = (bf16[256,256]{1,0:T(8,128)(2,1)S(1)}, bf16[256,256]{1,0:T(8,128)(2,1)S(1)}, u32[]{:S(2)}, u32[]{:S(2)}) collective-permute-start(bf16[256,256]{1,0:T(8,128)(2,1)S(1)} %get-tuple-element.70), channel_id=1, source_target_pairs={{0,16},{4,20},{8,24},{12,28},{16,0},{20,4},{24,8},{28,12},{1,17},{... | collective-permute-start | bytes 393224 | tf_op jit(solution)/shard_map/ppermute | solution.py:23
  45.4 0.3 collective-permute-done.10.refs_1_
  45.7 1.7 %collective-permute-start.16 = (bf16[256,256]{1,0:T(8,128)(2,1)S(1)}, bf16[256,256]{1,0:T(8,128)(2,1)S(1)}, u32[]{:S(2)}, u32[]{:S(2)}) collective-permute-start(bf16[256,256]{1,0:T(8,128)(2,1)S(1)} %get-tuple-element.71), channel_id=1, source_target_pairs={{0,8},{4,12},{8,0},{12,4},{16,24},{20,28},{24,16},{28,20},{1,9},{5... | collective-permute-start | bytes 393224 | tf_op jit(solution)/shard_map/ppermute | solution.py:23
  47.4 1.5 %collective-permute-done.11.refs_2_ = bf16[256,256]{1,0:T(8,128)(2,1)S(1)} collective-permute-done((bf16[256,256]{1,0:T(8,128)(2,1)S(1)}, bf16[256,256]{1,0:T(8,128)(2,1)S(1)}, u32[]{:S(2)}, u32[]{:S(2)}) %collective-permute-start.11) | collective-permute-done | bytes 131104 | tf_op jit(solution)/shard_map/ppermute | solution.py:23
  48.9 2.2 %collective-permute-start.17 = (bf16[256,256]{1,0:T(8,128)(2,1)S(1)}, bf16[256,256]{1,0:T(8,128)(2,1)S(1)}, u32[]{:S(2)}, u32[]{:S(2)}) collective-permute-start(bf16[256,256]{1,0:T(8,128)(2,1)S(1)} %get-tuple-element.73), channel_id=1, source_target_pairs={{0,24},{4,28},{8,16},{12,20},{16,8},{20,12},{24,0},{28,4},{1,25},{... | collective-permute-start | bytes 393224 | tf_op jit(solution)/shard_map/ppermute | solution.py:23
  51.1 0.6 %collective-permute-start.18 = (bf16[256,256]{1,0:T(8,128)(2,1)S(1)}, bf16[256,256]{1,0:T(8,128)(2,1)S(1)}, u32[]{:S(2)}, u32[]{:S(2)}) collective-permute-start(bf16[256,256]{1,0:T(8,128)(2,1)S(1)} %get-tuple-element.74), channel_id=1, source_target_pairs={{0,16},{4,20},{8,24},{12,28},{16,0},{20,4},{24,8},{28,12},{1,17},{... | collective-permute-start | bytes 393224 | tf_op jit(solution)/shard_map/ppermute | solution.py:23
  51.7 1.3 %collective-permute-start.19 = (bf16[256,256]{1,0:T(8,128)(2,1)S(1)}, bf16[256,256]{1,0:T(8,128)(2,1)S(1)}, u32[]{:S(2)}, u32[]{:S(2)}) collective-permute-start(bf16[256,256]{1,0:T(8,128)(2,1)S(1)} %get-tuple-element.75), channel_id=1, source_target_pairs={{0,8},{4,12},{8,0},{12,4},{16,24},{20,28},{24,16},{28,20},{1,9},{5... | collective-permute-start | bytes 393224 | tf_op jit(solution)/shard_map/ppermute | solution.py:23
  53.0 0.9 %join_queries.1 = (bf16[512,512]{1,0:T(8,128)(2,1)}, f32[8,128]{1,0:T(8,128)S(1)}) custom-call(bf16[256,256]{1,0:T(8,128)(2,1)S(1)} %get-tuple-element.58.refs_0_, bf16[256,256]{1,0:T(8,128)(2,1)S(1)} %collective-permute-done.10.refs_1_, bf16[256,256]{1,0:T(8,128)(2,1)S(1)} %collective-permute-done.11.refs_2_, ...), custom_call_target="tpu_custom_call" | custom-call | bytes 104857600 | tf_op jit(solution)/shard_map/join_queries/pallas_call | solution.py:178
  53.9 0.6 collective-permute-done.15.refs_2_
  54.5 2.8 %collective-permute-done.17.refs_5_ = bf16[256,256]{1,0:T(8,128)(2,1)S(1)} collective-permute-done((bf16[256,256]{1,0:T(8,128)(2,1)S(1)}, bf16[256,256]{1,0:T(8,128)(2,1)S(1)}, u32[]{:S(2)}, u32[]{:S(2)}) %collective-permute-start.17) | collective-permute-done | bytes 131104 | tf_op jit(solution)/shard_map/ppermute | solution.py:23
  57.3 2.0 %collective-permute-done.18.refs_6_ = bf16[256,256]{1,0:T(8,128)(2,1)S(1)} collective-permute-done((bf16[256,256]{1,0:T(8,128)(2,1)S(1)}, bf16[256,256]{1,0:T(8,128)(2,1)S(1)}, u32[]{:S(2)}, u32[]{:S(2)}) %collective-permute-start.18) | collective-permute-done | bytes 131104 | tf_op jit(solution)/shard_map/ppermute | solution.py:23
  59.3 0.1 collective-permute-done.19.refs_7_
  59.4 1.1 %join_pairs.1 = (bf16[512,512]{1,0:T(8,128)(2,1)}, bf16[512,512]{1,0:T(8,128)(2,1)}) custom-call(bf16[256,256]{1,0:T(8,128)(2,1)S(1)} %get-tuple-element.68.refs_0_, bf16[256,256]{1,0:T(8,128)(2,1)S(1)} %collective-permute-done.14.refs_1_, bf16[256,256]{1,0:T(8,128)(2,1)S(1)} %collective-permute-done.15.refs_2_, ...), custom_call_target="tpu_custom_call" | custom-call | bytes 2097152 | tf_op jit(solution)/shard_map/join_pairs/pallas_call | solution.py:189
  (13 shorter events, 0.1 us)
Async XLA Ops:
  0.6 8.5 %copy-start.3 = (bf16[512,512]{1,0:T(8,128)(2,1)S(1)}, bf16[512,512]{1,0:T(8,128)(2,1)}, u32[]{:S(2)}) copy-start(bf16[512,512]{1,0:T(8,128)(2,1)} %refs_3_.5) | copy-start | bytes 1572868
  0.6 8.5 %copy-start.2 = (bf16[512,512]{1,0:T(8,128)(2,1)S(1)}, bf16[512,512]{1,0:T(8,128)(2,1)}, u32[]{:S(2)}) copy-start(bf16[512,512]{1,0:T(8,128)(2,1)} %refs_2_.5) | copy-start | bytes 1572868
  0.7 8.5 %copy-start.1 = (bf16[512,512]{1,0:T(8,128)(2,1)S(1)}, bf16[512,512]{1,0:T(8,128)(2,1)}, u32[]{:S(2)}) copy-start(bf16[512,512]{1,0:T(8,128)(2,1)} %refs_1_.5) | copy-start | bytes 1572868
  0.7 8.4 %copy-start = (bf16[512,512]{1,0:T(8,128)(2,1)S(1)}, bf16[512,512]{1,0:T(8,128)(2,1)}, u32[]{:S(2)}) copy-start(bf16[512,512]{1,0:T(8,128)(2,1)} %refs_0_.7) | copy-start | bytes 1572868
  0.7 20.7 %copy-start.4 = (s32[32,6]{0,1:T(8,128)S(1)}, s32[32,6]{0,1:T(8,128)}, u32[]{:S(2)}) copy-start(s32[32,6]{0,1:T(8,128)} %param.9) | copy-start | bytes 2308
  2.5 11.3 %collective-permute-start.3 = (bf16[512,256]{1,0:T(8,128)(2,1)}, bf16[512,256]{1,0:T(8,128)(2,1)S(1)}, u32[]{:S(2)}, u32[]{:S(2)}) collective-permute-start(bf16[512,256]{1,0:T(8,128)(2,1)} %split_early.2.refs_4_), channel_id=1, source_target_pairs={{0,24},{4,28},{8,16},{12,20},{16,8},{20,12},{24,0},{28,4},{1,25},{... | collective-permute-start | bytes 786440 | tf_op jit(solution)/shard_map/ppermute | solution.py:23
  8.4 11.1 %collective-permute-start.4 = (bf16[512,256]{1,0:T(8,128)(2,1)}, bf16[512,256]{1,0:T(8,128)(2,1)S(1)}, u32[]{:S(2)}, u32[]{:S(2)}) collective-permute-start(bf16[512,256]{1,0:T(8,128)(2,1)} %get-tuple-element.46), channel_id=1, source_target_pairs={{0,16},{4,20},{8,24},{12,28},{16,0},{20,4},{24,8},{28,12},{1,17},{... | collective-permute-start | bytes 786440 | tf_op jit(solution)/shard_map/ppermute | solution.py:23
  9.0 11.1 %collective-permute-start.5 = (bf16[512,256]{1,0:T(8,128)(2,1)}, bf16[512,256]{1,0:T(8,128)(2,1)S(1)}, u32[]{:S(2)}, u32[]{:S(2)}) collective-permute-start(bf16[512,256]{1,0:T(8,128)(2,1)} %get-tuple-element.47), channel_id=1, source_target_pairs={{0,8},{4,12},{8,0},{12,4},{16,24},{20,28},{24,16},{28,20},{1,9},{5... | collective-permute-start | bytes 786440 | tf_op jit(solution)/shard_map/ppermute | solution.py:23
  9.4 19.4 %collective-permute-start = (bf16[528,256]{1,0:T(8,128)(2,1)S(1)}, bf16[528,256]{1,0:T(8,128)(2,1)S(1)}, u32[]{:S(2)}, u32[]{:S(2)}) collective-permute-start(bf16[528,256]{1,0:T(8,128)(2,1)S(1)} %get-tuple-element.42), channel_id=1, source_target_pairs={{0,24},{4,28},{8,16},{12,20},{16,8},{20,12},{24,0},{28,4},{1,25},{... | collective-permute-start | bytes 811016 | tf_op jit(solution)/shard_map/ppermute | solution.py:23
  12.3 17.9 %collective-permute-start.1 = (bf16[528,256]{1,0:T(8,128)(2,1)S(1)}, bf16[528,256]{1,0:T(8,128)(2,1)S(1)}, u32[]{:S(2)}, u32[]{:S(2)}) collective-permute-start(bf16[528,256]{1,0:T(8,128)(2,1)S(1)} %get-tuple-element.43), channel_id=1, source_target_pairs={{0,16},{4,20},{8,24},{12,28},{16,0},{20,4},{24,8},{28,12},{1,17},{... | collective-permute-start | bytes 811016 | tf_op jit(solution)/shard_map/ppermute | solution.py:23
  13.8 16.7 %collective-permute-start.2 = (bf16[528,256]{1,0:T(8,128)(2,1)S(1)}, bf16[528,256]{1,0:T(8,128)(2,1)S(1)}, u32[]{:S(2)}, u32[]{:S(2)}) collective-permute-start(bf16[528,256]{1,0:T(8,128)(2,1)S(1)} %get-tuple-element.44), channel_id=1, source_target_pairs={{0,8},{4,12},{8,0},{12,4},{16,24},{20,28},{24,16},{28,20},{1,9},{5... | collective-permute-start | bytes 811016 | tf_op jit(solution)/shard_map/ppermute | solution.py:23
  20.9 1.7 %collective-permute-start.6 = (bf16[2,256,256]{2,1,0:T(8,128)(2,1)}, bf16[2,256,256]{2,1,0:T(8,128)(2,1)S(1)}, u32[]{:S(2)}, u32[]{:S(2)}) collective-permute-start(bf16[2,256,256]{2,1,0:T(8,128)(2,1)} %get-tuple-element.48), channel_id=1, source_target_pairs={{0,4},{4,0},{8,12},{12,8},{16,20},{20,16},{24,28},{28,24},{1,5},{5... | collective-permute-start | bytes 786440 | tf_op jit(solution)/shard_map/ppermute | solution.py:23
  20.9 2.1 %collective-permute-start.7 = (bf16[2,256,256]{2,1,0:T(8,128)(2,1)}, bf16[2,256,256]{2,1,0:T(8,128)(2,1)S(1)}, u32[]{:S(2)}, u32[]{:S(2)}) collective-permute-start(bf16[2,256,256]{2,1,0:T(8,128)(2,1)} %get-tuple-element.49), channel_id=1, source_target_pairs={{0,4},{4,0},{8,12},{12,8},{16,20},{20,16},{24,28},{28,24},{1,5},{5... | collective-permute-start | bytes 786440 | tf_op jit(solution)/shard_map/ppermute | solution.py:23
  30.6 1.6 %collective-permute-start.8 = (bf16[2,256,256]{2,1,0:T(8,128)(2,1)S(1)}, bf16[2,256,256]{2,1,0:T(8,128)(2,1)S(1)}, u32[]{:S(2)}, u32[]{:S(2)}) collective-permute-start(bf16[2,256,256]{2,1,0:T(8,128)(2,1)S(1)} %get-tuple-element.51), channel_id=1, source_target_pairs={{0,4},{4,0},{8,12},{12,8},{16,20},{20,16},{24,28},{28,24},{1,5},{5... | collective-permute-start | bytes 786440 | tf_op jit(solution)/shard_map/ppermute | solution.py:23
  30.7 1.9 %collective-permute-start.9 = (bf16[2,256,256]{2,1,0:T(8,128)(2,1)S(1)}, bf16[2,256,256]{2,1,0:T(8,128)(2,1)S(1)}, u32[]{:S(2)}, u32[]{:S(2)}) collective-permute-start(bf16[2,256,256]{2,1,0:T(8,128)(2,1)S(1)} %get-tuple-element.52), channel_id=1, source_target_pairs={{0,4},{4,0},{8,12},{12,8},{16,20},{20,16},{24,28},{28,24},{1,5},{5... | collective-permute-start | bytes 786440 | tf_op jit(solution)/shard_map/ppermute | solution.py:23
  38.4 3.7 %collective-permute-start.13 = (bf16[4,512,256]{2,1,0:T(8,128)(2,1)S(1)}, bf16[4,512,256]{2,1,0:T(8,128)(2,1)S(1)}, u32[]{:S(2)}, u32[]{:S(2)}) collective-permute-start(bf16[4,512,256]{2,1,0:T(8,128)(2,1)S(1)} %get-tuple-element.63), channel_id=1, source_target_pairs={{0,4},{4,0},{8,12},{12,8},{16,20},{20,16},{24,28},{28,24},{1,5},{5... | collective-permute-start | bytes 3145736 | tf_op jit(solution)/shard_map/ppermute | solution.py:23
  38.6 7.1 %collective-permute-start.10 = (bf16[256,256]{1,0:T(8,128)(2,1)S(1)}, bf16[256,256]{1,0:T(8,128)(2,1)S(1)}, u32[]{:S(2)}, u32[]{:S(2)}) collective-permute-start(bf16[256,256]{1,0:T(8,128)(2,1)S(1)} %get-tuple-element.59), channel_id=1, source_target_pairs={{0,24},{4,28},{8,16},{12,20},{16,8},{20,12},{24,0},{28,4},{1,25},{... | collective-permute-start | bytes 393224 | tf_op jit(solution)/shard_map/ppermute | solution.py:23
  40.9 7.9 %collective-permute-start.11 = (bf16[256,256]{1,0:T(8,128)(2,1)S(1)}, bf16[256,256]{1,0:T(8,128)(2,1)S(1)}, u32[]{:S(2)}, u32[]{:S(2)}) collective-permute-start(bf16[256,256]{1,0:T(8,128)(2,1)S(1)} %get-tuple-element.60), channel_id=1, source_target_pairs={{0,16},{4,20},{8,24},{12,28},{16,0},{20,4},{24,8},{28,12},{1,17},{... | collective-permute-start | bytes 393224 | tf_op jit(solution)/shard_map/ppermute | solution.py:23
  41.6 9.5 %collective-permute-start.12 = (bf16[256,256]{1,0:T(8,128)(2,1)S(1)}, bf16[256,256]{1,0:T(8,128)(2,1)S(1)}, u32[]{:S(2)}, u32[]{:S(2)}) collective-permute-start(bf16[256,256]{1,0:T(8,128)(2,1)S(1)} %get-tuple-element.61), channel_id=1, source_target_pairs={{0,8},{4,12},{8,0},{12,4},{16,24},{20,28},{24,16},{28,20},{1,9},{5... | collective-permute-start | bytes 393224 | tf_op jit(solution)/shard_map/ppermute | solution.py:23
  42.4 9.3 %collective-permute-start.14 = (bf16[256,256]{1,0:T(8,128)(2,1)S(1)}, bf16[256,256]{1,0:T(8,128)(2,1)S(1)}, u32[]{:S(2)}, u32[]{:S(2)}) collective-permute-start(bf16[256,256]{1,0:T(8,128)(2,1)S(1)} %get-tuple-element.69), channel_id=1, source_target_pairs={{0,24},{4,28},{8,16},{12,20},{16,8},{20,12},{24,0},{28,4},{1,25},{... | collective-permute-start | bytes 393224 | tf_op jit(solution)/shard_map/ppermute | solution.py:23
  44.8 9.7 %collective-permute-start.15 = (bf16[256,256]{1,0:T(8,128)(2,1)S(1)}, bf16[256,256]{1,0:T(8,128)(2,1)S(1)}, u32[]{:S(2)}, u32[]{:S(2)}) collective-permute-start(bf16[256,256]{1,0:T(8,128)(2,1)S(1)} %get-tuple-element.70), channel_id=1, source_target_pairs={{0,16},{4,20},{8,24},{12,28},{16,0},{20,4},{24,8},{28,12},{1,17},{... | collective-permute-start | bytes 393224 | tf_op jit(solution)/shard_map/ppermute | solution.py:23
  45.7 8.8 %collective-permute-start.16 = (bf16[256,256]{1,0:T(8,128)(2,1)S(1)}, bf16[256,256]{1,0:T(8,128)(2,1)S(1)}, u32[]{:S(2)}, u32[]{:S(2)}) collective-permute-start(bf16[256,256]{1,0:T(8,128)(2,1)S(1)} %get-tuple-element.71), channel_id=1, source_target_pairs={{0,8},{4,12},{8,0},{12,4},{16,24},{20,28},{24,16},{28,20},{1,9},{5... | collective-permute-start | bytes 393224 | tf_op jit(solution)/shard_map/ppermute | solution.py:23
  48.9 8.4 %collective-permute-start.17 = (bf16[256,256]{1,0:T(8,128)(2,1)S(1)}, bf16[256,256]{1,0:T(8,128)(2,1)S(1)}, u32[]{:S(2)}, u32[]{:S(2)}) collective-permute-start(bf16[256,256]{1,0:T(8,128)(2,1)S(1)} %get-tuple-element.73), channel_id=1, source_target_pairs={{0,24},{4,28},{8,16},{12,20},{16,8},{20,12},{24,0},{28,4},{1,25},{... | collective-permute-start | bytes 393224 | tf_op jit(solution)/shard_map/ppermute | solution.py:23
  51.1 8.3 %collective-permute-start.18 = (bf16[256,256]{1,0:T(8,128)(2,1)S(1)}, bf16[256,256]{1,0:T(8,128)(2,1)S(1)}, u32[]{:S(2)}, u32[]{:S(2)}) collective-permute-start(bf16[256,256]{1,0:T(8,128)(2,1)S(1)} %get-tuple-element.74), channel_id=1, source_target_pairs={{0,16},{4,20},{8,24},{12,28},{16,0},{20,4},{24,8},{28,12},{1,17},{... | collective-permute-start | bytes 393224 | tf_op jit(solution)/shard_map/ppermute | solution.py:23
  51.7 7.7 %collective-permute-start.19 = (bf16[256,256]{1,0:T(8,128)(2,1)S(1)}, bf16[256,256]{1,0:T(8,128)(2,1)S(1)}, u32[]{:S(2)}, u32[]{:S(2)}) collective-permute-start(bf16[256,256]{1,0:T(8,128)(2,1)S(1)} %get-tuple-element.75), channel_id=1, source_target_pairs={{0,8},{4,12},{8,0},{12,4},{16,24},{20,28},{24,16},{28,20},{1,9},{5... | collective-permute-start | bytes 393224 | tf_op jit(solution)/shard_map/ppermute | solution.py:23

commit v7 on v6

--- a/solution.py
+++ b/solution.py
@@ -340,7 +340,7 @@
                 acc[pl.ds(p, BLK), :] += terms[n][i * BLK : (i + 1) * BLK]
         return 0
 
-    lax.fori_loop(0, groups, step, 0, unroll=2)
+    lax.fori_loop(0, groups, step, 0, unroll=4)
 
     quarter = half // 2
     for s in range(groups):
@@ -423,7 +423,10 @@
     late = to_chips(late, members)
     early = early + with_members(only_pairs(early, rows // 2, [], groups), members)
     dq_early, buffers = attend(links, early, [], [], rows, shards, members, groups)
-    late = late + with_members(only_pairs(late, rows // 2, dq_early[:1], groups), members)
+    lent = []
+    for s in range(0, groups, 2):
+        lent += only_pairs(late[s : s + 2], rows // 2, dq_early[:1], 2)
+    late = late + with_members(lent, members)
     dqs, own, far = attend(links, late, dq_early, buffers, rows, shards, members, groups)
     far = [swapped(part, r) for r, part in enumerate(far, 1)]
     dqs = to_chips(dqs, members)

time: 60.7 us -> 59.9 us (0.987)
  transfers between devices with their start and end apart: 20 -> 20, of which waited for: 15 -> 13; matrix products, arithmetic and copies ran while one was open for 0% -> 0% of each run, Pallas kernels for 16% -> 16%
where the time goes in v7:
time: 59.9 us; the launch traced here: 59.7 us
  starting transfers between devices  23.4 us (39%)
  Pallas kernels  18.2 us (30%)
  waiting for transfers between devices  17.2 us (29%)
  between operations  0.77 us (1%)
    ppermute x20, starting transfers between devices, swapped(): return lax.ppermute(x, 'ctx', [(i, i ^ by) for i in range(count)])  23.4 us
    ppermute x20, waiting for transfers between devices, swapped(): return lax.ppermute(x, 'ctx', [(i, i ^ by) for i in range(count)])  17.2 us
    pallas_call x2, Pallas kernels, attend(): pl.pallas_call(functools.partial(attend_kernel, late, near, shards, membe...  11.1 us
    pallas_call x2, Pallas kernels, split_early(): pl.pallas_call(functools.partial(split_early_kernel, members, groups, wan...  3.76 us
  transfers between devices with their start and end apart: 20, of which 13 were waited for; matrix products, arithmetic and copies ran while one was open for 0% of the time, Pallas kernels for 16%

profile of v7, /device:TPU:0, one launch (start us, length us, event | category | flops | bytes accessed | tf_op | source)
XLA Modules:
  0.0 59.7 jit_solution(7697974423472831889)
XLA Ops:
  0.6 0.0 copy-start.3
  0.6 0.0 copy-start.2
  0.7 0.0 copy-start.1
  0.7 0.0 copy-start
  0.7 1.8 %split_early.2.refs_4_ = bf16[512,256]{1,0:T(8,128)(2,1)} custom-call(bf16[512,512]{1,0:T(8,128)(2,1)} %refs_0_.7, bf16[512,512]{1,0:T(8,128)(2,1)} %refs_1_.5, bf16[512,512]{1,0:T(8,128)(2,1)} %refs_2_.5, bf16[512,512]{1,0:T(8,128)(2,1)} %refs_3_.5), custom_call_target="tpu_custom_call" | custom-call | bytes 524288 | tf_op jit(solution)/shard_map/split_early/pallas_call | solution.py:73
  2.5 4.0 %collective-permute-start.3 = (bf16[512,256]{1,0:T(8,128)(2,1)}, bf16[512,256]{1,0:T(8,128)(2,1)S(1)}, u32[]{:S(2)}, u32[]{:S(2)}) collective-permute-start(bf16[512,256]{1,0:T(8,128)(2,1)} %split_early.2.refs_4_), channel_id=1, source_target_pairs={{0,24},{4,28},{8,16},{12,20},{16,8},{20,12},{24,0},{28,4},{1,25},{... | collective-permute-start | bytes 786440 | tf_op jit(solution)/shard_map/ppermute | solution.py:23
  6.5 1.9 %split_early.3 = (bf16[512,256]{1,0:T(8,128)(2,1)}, bf16[512,256]{1,0:T(8,128)(2,1)}) custom-call(bf16[512,512]{1,0:T(8,128)(2,1)} %refs_0_.7, bf16[512,512]{1,0:T(8,128)(2,1)} %refs_1_.5, bf16[512,512]{1,0:T(8,128)(2,1)} %refs_2_.5, bf16[512,512]{1,0:T(8,128)(2,1)} %refs_3_.5, bf16[512,256]{1,0:T(8,128)(2,1)} %split_early.2.refs_4_), custom_call_target="tpu_custom_call" | custom-call | bytes 1048576 | tf_op jit(solution)/shard_map/split_early/pallas_call | solution.py:73
  8.4 0.6 collective-permute-start.4
  9.0 0.1 collective-permute-start.5
  9.1 0.2 split_rest.1
  9.4 2.9 %collective-permute-start = (bf16[528,256]{1,0:T(8,128)(2,1)S(1)}, bf16[528,256]{1,0:T(8,128)(2,1)S(1)}, u32[]{:S(2)}, u32[]{:S(2)}) collective-permute-start(bf16[528,256]{1,0:T(8,128)(2,1)S(1)} %get-tuple-element.40), channel_id=1, source_target_pairs={{0,24},{4,28},{8,16},{12,20},{16,8},{20,12},{24,0},{28,4},{1,25},{... | collective-permute-start | bytes 811016 | tf_op jit(solution)/shard_map/ppermute | solution.py:23
  12.3 0.5 collective-permute-start.1
  12.8 1.0 %collective-permute-done.3.refs_1_.refs_2_ = bf16[512,256]{1,0:T(8,128)(2,1)S(1)} collective-permute-done((bf16[512,256]{1,0:T(8,128)(2,1)}, bf16[512,256]{1,0:T(8,128)(2,1)S(1)}, u32[]{:S(2)}, u32[]{:S(2)}) %collective-permute-start.3) | collective-permute-done | bytes 262176 | tf_op jit(solution)/shard_map/ppermute | solution.py:23
  13.8 2.0 %collective-permute-start.2 = (bf16[528,256]{1,0:T(8,128)(2,1)S(1)}, bf16[528,256]{1,0:T(8,128)(2,1)S(1)}, u32[]{:S(2)}, u32[]{:S(2)}) collective-permute-start(bf16[528,256]{1,0:T(8,128)(2,1)S(1)} %get-tuple-element.42), channel_id=1, source_target_pairs={{0,8},{4,12},{8,0},{12,4},{16,24},{20,28},{24,16},{28,20},{1,9},{5... | collective-permute-start | bytes 811016 | tf_op jit(solution)/shard_map/ppermute | solution.py:23
  15.9 3.7 %collective-permute-done.4.refs_2_.refs_3_ = bf16[512,256]{1,0:T(8,128)(2,1)S(1)} collective-permute-done((bf16[512,256]{1,0:T(8,128)(2,1)}, bf16[512,256]{1,0:T(8,128)(2,1)S(1)}, u32[]{:S(2)}, u32[]{:S(2)}) %collective-permute-start.4) | collective-permute-done | bytes 262176 | tf_op jit(solution)/shard_map/ppermute | solution.py:23
  19.5 0.5 collective-permute-done.5.refs_3_.refs_4_
  20.1 0.8 %only_pairs.3 = (bf16[2,256,256]{2,1,0:T(8,128)(2,1)}, bf16[2,256,256]{2,1,0:T(8,128)(2,1)}) custom-call(bf16[512,256]{1,0:T(8,128)(2,1)S(1)} %get-tuple-element.43.refs_0_.refs_1_, bf16[512,256]{1,0:T(8,128)(2,1)S(1)} %collective-permute-done.3.refs_1_.refs_2_, bf16[512,256]{1,0:T(8,128)(2,1)S(1)} %collective-permute-done.4.refs_2_.refs_3_, ...), custom_call_target="tpu_custom_call" | custom-call | bytes 1048576 | tf_op jit(solution)/shard_map/only_pairs/pallas_call | solution.py:130
  20.9 0.5 collective-permute-start.7
  21.4 0.1 copy.11.refs_0_
  21.5 1.1 %collective-permute-done.6.refs_5_ = bf16[2,256,256]{2,1,0:T(8,128)(2,1)S(1)} collective-permute-done((bf16[2,256,256]{2,1,0:T(8,128)(2,1)}, bf16[2,256,256]{2,1,0:T(8,128)(2,1)S(1)}, u32[]{:S(2)}, u32[]{:S(2)}) %collective-permute-start.6) | collective-permute-done | bytes 262176 | tf_op jit(solution)/shard_map/ppermute | solution.py:23
  22.6 0.4 collective-permute-done.7.refs_6_
  23.0 5.6 %attend_early.1 = (bf16[128,256]{1,0:T(8,128)(2,1)S(1)}, bf16[128,256]{1,0:T(8,128)(2,1)S(1)}, bf16[128,256]{1,0:T(8,128)(2,1)S(1)}, bf16[128,256]{1,0:T(8,128)(...) custom-call(s32[32,6]{1,0:T(8,128)S(1)} %copy.11.refs_0_, ...), custom_call_target="tpu_custom_call" | custom-call | tf_op jit(solution)/shard_map/attend_early/pallas_call | solution.py:377
  28.6 0.0 collective-permute-done.refs_1_.refs_2_
  28.6 0.2 collective-permute-start.8
  28.9 1.4 %collective-permute-done.1.refs_0_.refs_3_ = bf16[528,256]{1,0:T(8,128)(2,1)S(1)} collective-permute-done((bf16[528,256]{1,0:T(8,128)(2,1)S(1)}, bf16[528,256]{1,0:T(8,128)(2,1)S(1)}, u32[]{:S(2)}, u32[]{:S(2)}) %collective-permute-start.1) | collective-permute-done | bytes 270368 | tf_op jit(solution)/shard_map/ppermute | solution.py:23
  30.2 0.3 collective-permute-done.2.refs_1_.refs_4_
  30.6 0.1 collective-permute-start.9
  30.7 1.5 %collective-permute-done.9.refs_6_ = bf16[2,256,256]{2,1,0:T(8,128)(2,1)S(1)} collective-permute-done((bf16[2,256,256]{2,1,0:T(8,128)(2,1)S(1)}, bf16[2,256,256]{2,1,0:T(8,128)(2,1)S(1)}, u32[]{:S(2)}, u32[]{:S(2)}) %collective-permute-start.9) | collective-permute-done | bytes 262176 | tf_op jit(solution)/shard_map/ppermute | solution.py:23
  32.2 5.5 %attend_late.1 = (bf16[256,256]{1,0:T(8,128)(2,1)S(1)}, bf16[256,256]{1,0:T(8,128)(2,1)S(1)}, bf16[256,256]{1,0:T(8,128)(2,1)S(1)}, bf16[256,256]{1,0:T(8,128)(2...) custom-call(s32[32,6]{1,0:T(8,128)S(1)} %copy.11.refs_0_, ...), custom_call_target="tpu_custom_call", output_to_operand_aliasing={{9}: (11, {}), {10}: (12, {})} | custom-call | flops 1342177280 | bytes 4194304 | tf_op jit(solution)/shard_map/attend_late/pallas_call | solution.py:377
  37.6 0.2 collective-permute-start.13
  37.8 2.3 %collective-permute-start.10 = (bf16[256,256]{1,0:T(8,128)(2,1)S(1)}, bf16[256,256]{1,0:T(8,128)(2,1)S(1)}, u32[]{:S(2)}, u32[]{:S(2)}) collective-permute-start(bf16[256,256]{1,0:T(8,128)(2,1)S(1)} %get-tuple-element.55), channel_id=1, source_target_pairs={{0,24},{4,28},{8,16},{12,20},{16,8},{20,12},{24,0},{28,4},{1,25},{... | collective-permute-start | bytes 393224 | tf_op jit(solution)/shard_map/ppermute | solution.py:23
  40.2 0.6 %collective-permute-start.11 = (bf16[256,256]{1,0:T(8,128)(2,1)S(1)}, bf16[256,256]{1,0:T(8,128)(2,1)S(1)}, u32[]{:S(2)}, u32[]{:S(2)}) collective-permute-start(bf16[256,256]{1,0:T(8,128)(2,1)S(1)} %get-tuple-element.56), channel_id=1, source_target_pairs={{0,16},{4,20},{8,24},{12,28},{16,0},{20,4},{24,8},{28,12},{1,17},{... | collective-permute-start | bytes 393224 | tf_op jit(solution)/shard_map/ppermute | solution.py:23
  40.8 0.5 collective-permute-start.12
  41.3 0.3 add_partials.1
  41.7 2.4 %collective-permute-start.14 = (bf16[256,256]{1,0:T(8,128)(2,1)S(1)}, bf16[256,256]{1,0:T(8,128)(2,1)S(1)}, u32[]{:S(2)}, u32[]{:S(2)}) collective-permute-start(bf16[256,256]{1,0:T(8,128)(2,1)S(1)} %get-tuple-element.65), channel_id=1, source_target_pairs={{0,24},{4,28},{8,16},{12,20},{16,8},{20,12},{24,0},{28,4},{1,25},{... | collective-permute-start | bytes 393224 | tf_op jit(solution)/shard_map/ppermute | solution.py:23
  44.0 0.6 %collective-permute-start.15 = (bf16[256,256]{1,0:T(8,128)(2,1)S(1)}, bf16[256,256]{1,0:T(8,128)(2,1)S(1)}, u32[]{:S(2)}, u32[]{:S(2)}) collective-permute-start(bf16[256,256]{1,0:T(8,128)(2,1)S(1)} %get-tuple-element.66), channel_id=1, source_target_pairs={{0,16},{4,20},{8,24},{12,28},{16,0},{20,4},{24,8},{28,12},{1,17},{... | collective-permute-start | bytes 393224 | tf_op jit(solution)/shard_map/ppermute | solution.py:23
  44.7 0.3 collective-permute-done.10.refs_1_
  45.0 1.6 %collective-permute-start.16 = (bf16[256,256]{1,0:T(8,128)(2,1)S(1)}, bf16[256,256]{1,0:T(8,128)(2,1)S(1)}, u32[]{:S(2)}, u32[]{:S(2)}) collective-permute-start(bf16[256,256]{1,0:T(8,128)(2,1)S(1)} %get-tuple-element.67), channel_id=1, source_target_pairs={{0,8},{4,12},{8,0},{12,4},{16,24},{20,28},{24,16},{28,20},{1,9},{5... | collective-permute-start | bytes 393224 | tf_op jit(solution)/shard_map/ppermute | solution.py:23
  46.6 1.5 %collective-permute-done.11.refs_2_ = bf16[256,256]{1,0:T(8,128)(2,1)S(1)} collective-permute-done((bf16[256,256]{1,0:T(8,128)(2,1)S(1)}, bf16[256,256]{1,0:T(8,128)(2,1)S(1)}, u32[]{:S(2)}, u32[]{:S(2)}) %collective-permute-start.11) | collective-permute-done | bytes 131104 | tf_op jit(solution)/shard_map/ppermute | solution.py:23
  48.1 2.2 %collective-permute-start.17 = (bf16[256,256]{1,0:T(8,128)(2,1)S(1)}, bf16[256,256]{1,0:T(8,128)(2,1)S(1)}, u32[]{:S(2)}, u32[]{:S(2)}) collective-permute-start(bf16[256,256]{1,0:T(8,128)(2,1)S(1)} %get-tuple-element.69), channel_id=1, source_target_pairs={{0,24},{4,28},{8,16},{12,20},{16,8},{20,12},{24,0},{28,4},{1,25},{... | collective-permute-start | bytes 393224 | tf_op jit(solution)/shard_map/ppermute | solution.py:23
  50.3 0.6 %collective-permute-start.18 = (bf16[256,256]{1,0:T(8,128)(2,1)S(1)}, bf16[256,256]{1,0:T(8,128)(2,1)S(1)}, u32[]{:S(2)}, u32[]{:S(2)}) collective-permute-start(bf16[256,256]{1,0:T(8,128)(2,1)S(1)} %get-tuple-element.70), channel_id=1, source_target_pairs={{0,16},{4,20},{8,24},{12,28},{16,0},{20,4},{24,8},{28,12},{1,17},{... | collective-permute-start | bytes 393224 | tf_op jit(solution)/shard_map/ppermute | solution.py:23
  50.9 1.3 %collective-permute-start.19 = (bf16[256,256]{1,0:T(8,128)(2,1)S(1)}, bf16[256,256]{1,0:T(8,128)(2,1)S(1)}, u32[]{:S(2)}, u32[]{:S(2)}) collective-permute-start(bf16[256,256]{1,0:T(8,128)(2,1)S(1)} %get-tuple-element.71), channel_id=1, source_target_pairs={{0,8},{4,12},{8,0},{12,4},{16,24},{20,28},{24,16},{28,20},{1,9},{5... | collective-permute-start | bytes 393224 | tf_op jit(solution)/shard_map/ppermute | solution.py:23
  52.3 0.9 %join_queries.1 = (bf16[512,512]{1,0:T(8,128)(2,1)}, f32[8,128]{1,0:T(8,128)S(1)}) custom-call(bf16[256,256]{1,0:T(8,128)(2,1)S(1)} %get-tuple-element.54.refs_0_, bf16[256,256]{1,0:T(8,128)(2,1)S(1)} %collective-permute-done.10.refs_1_, bf16[256,256]{1,0:T(8,128)(2,1)S(1)} %collective-permute-done.11.refs_2_, ...), custom_call_target="tpu_custom_call" | custom-call | bytes 104857600 | tf_op jit(solution)/shard_map/join_queries/pallas_call | solution.py:178
  53.1 0.6 collective-permute-done.15.refs_2_
  53.7 2.8 %collective-permute-done.17.refs_5_ = bf16[256,256]{1,0:T(8,128)(2,1)S(1)} collective-permute-done((bf16[256,256]{1,0:T(8,128)(2,1)S(1)}, bf16[256,256]{1,0:T(8,128)(2,1)S(1)}, u32[]{:S(2)}, u32[]{:S(2)}) %collective-permute-start.17) | collective-permute-done | bytes 131104 | tf_op jit(solution)/shard_map/ppermute | solution.py:23
  56.5 2.0 %collective-permute-done.18.refs_6_ = bf16[256,256]{1,0:T(8,128)(2,1)S(1)} collective-permute-done((bf16[256,256]{1,0:T(8,128)(2,1)S(1)}, bf16[256,256]{1,0:T(8,128)(2,1)S(1)}, u32[]{:S(2)}, u32[]{:S(2)}) %collective-permute-start.18) | collective-permute-done | bytes 131104 | tf_op jit(solution)/shard_map/ppermute | solution.py:23
  58.6 0.0 collective-permute-done.19.refs_7_
  58.6 1.1 %join_pairs.1 = (bf16[512,512]{1,0:T(8,128)(2,1)}, bf16[512,512]{1,0:T(8,128)(2,1)}) custom-call(bf16[256,256]{1,0:T(8,128)(2,1)S(1)} %get-tuple-element.64.refs_0_, bf16[256,256]{1,0:T(8,128)(2,1)S(1)} %collective-permute-done.14.refs_1_, bf16[256,256]{1,0:T(8,128)(2,1)S(1)} %collective-permute-done.15.refs_2_, ...), custom_call_target="tpu_custom_call" | custom-call | bytes 2097152 | tf_op jit(solution)/shard_map/join_pairs/pallas_call | solution.py:189
  (14 shorter events, 0.1 us)
Async XLA Ops:
  0.6 8.5 %copy-start.3 = (bf16[512,512]{1,0:T(8,128)(2,1)S(1)}, bf16[512,512]{1,0:T(8,128)(2,1)}, u32[]{:S(2)}) copy-start(bf16[512,512]{1,0:T(8,128)(2,1)} %refs_3_.5) | copy-start | bytes 1572868
  0.6 8.5 %copy-start.2 = (bf16[512,512]{1,0:T(8,128)(2,1)S(1)}, bf16[512,512]{1,0:T(8,128)(2,1)}, u32[]{:S(2)}) copy-start(bf16[512,512]{1,0:T(8,128)(2,1)} %refs_2_.5) | copy-start | bytes 1572868
  0.7 8.5 %copy-start.1 = (bf16[512,512]{1,0:T(8,128)(2,1)S(1)}, bf16[512,512]{1,0:T(8,128)(2,1)}, u32[]{:S(2)}) copy-start(bf16[512,512]{1,0:T(8,128)(2,1)} %refs_1_.5) | copy-start | bytes 1572868
  0.7 8.4 %copy-start = (bf16[512,512]{1,0:T(8,128)(2,1)S(1)}, bf16[512,512]{1,0:T(8,128)(2,1)}, u32[]{:S(2)}) copy-start(bf16[512,512]{1,0:T(8,128)(2,1)} %refs_0_.7) | copy-start | bytes 1572868
  0.7 20.7 %copy-start.4 = (s32[32,6]{0,1:T(8,128)S(1)}, s32[32,6]{0,1:T(8,128)}, u32[]{:S(2)}) copy-start(s32[32,6]{0,1:T(8,128)} %param.9) | copy-start | bytes 2308
  2.5 11.3 %collective-permute-start.3 = (bf16[512,256]{1,0:T(8,128)(2,1)}, bf16[512,256]{1,0:T(8,128)(2,1)S(1)}, u32[]{:S(2)}, u32[]{:S(2)}) collective-permute-start(bf16[512,256]{1,0:T(8,128)(2,1)} %split_early.2.refs_4_), channel_id=1, source_target_pairs={{0,24},{4,28},{8,16},{12,20},{16,8},{20,12},{24,0},{28,4},{1,25},{... | collective-permute-start | bytes 786440 | tf_op jit(solution)/shard_map/ppermute | solution.py:23
  8.4 11.1 %collective-permute-start.4 = (bf16[512,256]{1,0:T(8,128)(2,1)}, bf16[512,256]{1,0:T(8,128)(2,1)S(1)}, u32[]{:S(2)}, u32[]{:S(2)}) collective-permute-start(bf16[512,256]{1,0:T(8,128)(2,1)} %get-tuple-element.44), channel_id=1, source_target_pairs={{0,16},{4,20},{8,24},{12,28},{16,0},{20,4},{24,8},{28,12},{1,17},{... | collective-permute-start | bytes 786440 | tf_op jit(solution)/shard_map/ppermute | solution.py:23
  9.0 11.1 %collective-permute-start.5 = (bf16[512,256]{1,0:T(8,128)(2,1)}, bf16[512,256]{1,0:T(8,128)(2,1)S(1)}, u32[]{:S(2)}, u32[]{:S(2)}) collective-permute-start(bf16[512,256]{1,0:T(8,128)(2,1)} %get-tuple-element.45), channel_id=1, source_target_pairs={{0,8},{4,12},{8,0},{12,4},{16,24},{20,28},{24,16},{28,20},{1,9},{5... | collective-permute-start | bytes 786440 | tf_op jit(solution)/shard_map/ppermute | solution.py:23
  9.4 19.2 %collective-permute-start = (bf16[528,256]{1,0:T(8,128)(2,1)S(1)}, bf16[528,256]{1,0:T(8,128)(2,1)S(1)}, u32[]{:S(2)}, u32[]{:S(2)}) collective-permute-start(bf16[528,256]{1,0:T(8,128)(2,1)S(1)} %get-tuple-element.40), channel_id=1, source_target_pairs={{0,24},{4,28},{8,16},{12,20},{16,8},{20,12},{24,0},{28,4},{1,25},{... | collective-permute-start | bytes 811016 | tf_op jit(solution)/shard_map/ppermute | solution.py:23
  12.3 17.9 %collective-permute-start.1 = (bf16[528,256]{1,0:T(8,128)(2,1)S(1)}, bf16[528,256]{1,0:T(8,128)(2,1)S(1)}, u32[]{:S(2)}, u32[]{:S(2)}) collective-permute-start(bf16[528,256]{1,0:T(8,128)(2,1)S(1)} %get-tuple-element.41), channel_id=1, source_target_pairs={{0,16},{4,20},{8,24},{12,28},{16,0},{20,4},{24,8},{28,12},{1,17},{... | collective-permute-start | bytes 811016 | tf_op jit(solution)/shard_map/ppermute | solution.py:23
  13.8 16.7 %collective-permute-start.2 = (bf16[528,256]{1,0:T(8,128)(2,1)S(1)}, bf16[528,256]{1,0:T(8,128)(2,1)S(1)}, u32[]{:S(2)}, u32[]{:S(2)}) collective-permute-start(bf16[528,256]{1,0:T(8,128)(2,1)S(1)} %get-tuple-element.42), channel_id=1, source_target_pairs={{0,8},{4,12},{8,0},{12,4},{16,24},{20,28},{24,16},{28,20},{1,9},{5... | collective-permute-start | bytes 811016 | tf_op jit(solution)/shard_map/ppermute | solution.py:23
  20.9 1.7 %collective-permute-start.6 = (bf16[2,256,256]{2,1,0:T(8,128)(2,1)}, bf16[2,256,256]{2,1,0:T(8,128)(2,1)S(1)}, u32[]{:S(2)}, u32[]{:S(2)}) collective-permute-start(bf16[2,256,256]{2,1,0:T(8,128)(2,1)} %get-tuple-element.46), channel_id=1, source_target_pairs={{0,4},{4,0},{8,12},{12,8},{16,20},{20,16},{24,28},{28,24},{1,5},{5... | collective-permute-start | bytes 786440 | tf_op jit(solution)/shard_map/ppermute | solution.py:23
  20.9 2.1 %collective-permute-start.7 = (bf16[2,256,256]{2,1,0:T(8,128)(2,1)}, bf16[2,256,256]{2,1,0:T(8,128)(2,1)S(1)}, u32[]{:S(2)}, u32[]{:S(2)}) collective-permute-start(bf16[2,256,256]{2,1,0:T(8,128)(2,1)} %get-tuple-element.47), channel_id=1, source_target_pairs={{0,4},{4,0},{8,12},{12,8},{16,20},{20,16},{24,28},{28,24},{1,5},{5... | collective-permute-start | bytes 786440 | tf_op jit(solution)/shard_map/ppermute | solution.py:23
  28.6 2.0 %collective-permute-start.8 = (bf16[2,256,256]{2,1,0:T(8,128)(2,1)S(1)}, bf16[2,256,256]{2,1,0:T(8,128)(2,1)S(1)}, u32[]{:S(2)}, u32[]{:S(2)}) collective-permute-start(bf16[2,256,256]{2,1,0:T(8,128)(2,1)S(1)} %only_pairs.4), channel_id=1, source_target_pairs={{0,4},{4,0},{8,12},{12,8},{16,20},{20,16},{24,28},{28,24},{1,5},{5... | collective-permute-start | bytes 786440 | tf_op jit(solution)/shard_map/ppermute | solution.py:23
  30.6 1.6 %collective-permute-start.9 = (bf16[2,256,256]{2,1,0:T(8,128)(2,1)S(1)}, bf16[2,256,256]{2,1,0:T(8,128)(2,1)S(1)}, u32[]{:S(2)}, u32[]{:S(2)}) collective-permute-start(bf16[2,256,256]{2,1,0:T(8,128)(2,1)S(1)} %only_pairs.5), channel_id=1, source_target_pairs={{0,4},{4,0},{8,12},{12,8},{16,20},{20,16},{24,28},{28,24},{1,5},{5... | collective-permute-start | bytes 786440 | tf_op jit(solution)/shard_map/ppermute | solution.py:23
  37.6 3.7 %collective-permute-start.13 = (bf16[4,512,256]{2,1,0:T(8,128)(2,1)S(1)}, bf16[4,512,256]{2,1,0:T(8,128)(2,1)S(1)}, u32[]{:S(2)}, u32[]{:S(2)}) collective-permute-start(bf16[4,512,256]{2,1,0:T(8,128)(2,1)S(1)} %get-tuple-element.59), channel_id=1, source_target_pairs={{0,4},{4,0},{8,12},{12,8},{16,20},{20,16},{24,28},{28,24},{1,5},{5... | collective-permute-start | bytes 3145736 | tf_op jit(solution)/shard_map/ppermute | solution.py:23
  37.8 7.1 %collective-permute-start.10 = (bf16[256,256]{1,0:T(8,128)(2,1)S(1)}, bf16[256,256]{1,0:T(8,128)(2,1)S(1)}, u32[]{:S(2)}, u32[]{:S(2)}) collective-permute-start(bf16[256,256]{1,0:T(8,128)(2,1)S(1)} %get-tuple-element.55), channel_id=1, source_target_pairs={{0,24},{4,28},{8,16},{12,20},{16,8},{20,12},{24,0},{28,4},{1,25},{... | collective-permute-start | bytes 393224 | tf_op jit(solution)/shard_map/ppermute | solution.py:23
  40.2 8.0 %collective-permute-start.11 = (bf16[256,256]{1,0:T(8,128)(2,1)S(1)}, bf16[256,256]{1,0:T(8,128)(2,1)S(1)}, u32[]{:S(2)}, u32[]{:S(2)}) collective-permute-start(bf16[256,256]{1,0:T(8,128)(2,1)S(1)} %get-tuple-element.56), channel_id=1, source_target_pairs={{0,16},{4,20},{8,24},{12,28},{16,0},{20,4},{24,8},{28,12},{1,17},{... | collective-permute-start | bytes 393224 | tf_op jit(solution)/shard_map/ppermute | solution.py:23
  40.8 9.5 %collective-permute-start.12 = (bf16[256,256]{1,0:T(8,128)(2,1)S(1)}, bf16[256,256]{1,0:T(8,128)(2,1)S(1)}, u32[]{:S(2)}, u32[]{:S(2)}) collective-permute-start(bf16[256,256]{1,0:T(8,128)(2,1)S(1)} %get-tuple-element.57), channel_id=1, source_target_pairs={{0,8},{4,12},{8,0},{12,4},{16,24},{20,28},{24,16},{28,20},{1,9},{5... | collective-permute-start | bytes 393224 | tf_op jit(solution)/shard_map/ppermute | solution.py:23
  41.7 9.3 %collective-permute-start.14 = (bf16[256,256]{1,0:T(8,128)(2,1)S(1)}, bf16[256,256]{1,0:T(8,128)(2,1)S(1)}, u32[]{:S(2)}, u32[]{:S(2)}) collective-permute-start(bf16[256,256]{1,0:T(8,128)(2,1)S(1)} %get-tuple-element.65), channel_id=1, source_target_pairs={{0,24},{4,28},{8,16},{12,20},{16,8},{20,12},{24,0},{28,4},{1,25},{... | collective-permute-start | bytes 393224 | tf_op jit(solution)/shard_map/ppermute | solution.py:23
  44.0 9.7 %collective-permute-start.15 = (bf16[256,256]{1,0:T(8,128)(2,1)S(1)}, bf16[256,256]{1,0:T(8,128)(2,1)S(1)}, u32[]{:S(2)}, u32[]{:S(2)}) collective-permute-start(bf16[256,256]{1,0:T(8,128)(2,1)S(1)} %get-tuple-element.66), channel_id=1, source_target_pairs={{0,16},{4,20},{8,24},{12,28},{16,0},{20,4},{24,8},{28,12},{1,17},{... | collective-permute-start | bytes 393224 | tf_op jit(solution)/shard_map/ppermute | solution.py:23
  45.0 8.8 %collective-permute-start.16 = (bf16[256,256]{1,0:T(8,128)(2,1)S(1)}, bf16[256,256]{1,0:T(8,128)(2,1)S(1)}, u32[]{:S(2)}, u32[]{:S(2)}) collective-permute-start(bf16[256,256]{1,0:T(8,128)(2,1)S(1)} %get-tuple-element.67), channel_id=1, source_target_pairs={{0,8},{4,12},{8,0},{12,4},{16,24},{20,28},{24,16},{28,20},{1,9},{5... | collective-permute-start | bytes 393224 | tf_op jit(solution)/shard_map/ppermute | solution.py:23
  48.1 8.4 %collective-permute-start.17 = (bf16[256,256]{1,0:T(8,128)(2,1)S(1)}, bf16[256,256]{1,0:T(8,128)(2,1)S(1)}, u32[]{:S(2)}, u32[]{:S(2)}) collective-permute-start(bf16[256,256]{1,0:T(8,128)(2,1)S(1)} %get-tuple-element.69), channel_id=1, source_target_pairs={{0,24},{4,28},{8,16},{12,20},{16,8},{20,12},{24,0},{28,4},{1,25},{... | collective-permute-start | bytes 393224 | tf_op jit(solution)/shard_map/ppermute | solution.py:23
  50.3 8.3 %collective-permute-start.18 = (bf16[256,256]{1,0:T(8,128)(2,1)S(1)}, bf16[256,256]{1,0:T(8,128)(2,1)S(1)}, u32[]{:S(2)}, u32[]{:S(2)}) collective-permute-start(bf16[256,256]{1,0:T(8,128)(2,1)S(1)} %get-tuple-element.70), channel_id=1, source_target_pairs={{0,16},{4,20},{8,24},{12,28},{16,0},{20,4},{24,8},{28,12},{1,17},{... | collective-permute-start | bytes 393224 | tf_op jit(solution)/shard_map/ppermute | solution.py:23
  50.9 7.7 %collective-permute-start.19 = (bf16[256,256]{1,0:T(8,128)(2,1)S(1)}, bf16[256,256]{1,0:T(8,128)(2,1)S(1)}, u32[]{:S(2)}, u32[]{:S(2)}) collective-permute-start(bf16[256,256]{1,0:T(8,128)(2,1)S(1)} %get-tuple-element.71), channel_id=1, source_target_pairs={{0,8},{4,12},{8,0},{12,4},{16,24},{20,28},{24,16},{28,20},{1,9},{5... | collective-permute-start | bytes 393224 | tf_op jit(solution)/shard_map/ppermute | solution.py:23

commit v8 on v7

--- a/solution.py
+++ b/solution.py
@@ -140,62 +140,70 @@
     )(*packs, *after)
 
 
-def join_queries_kernel(members, groups, *refs):
-    out, token = refs[-2:]
-    token[...] = jnp.zeros_like(token)
+def write_half(members, groups, h, parts, outs, held, sems):
+    half = held[0].shape[0]
+    copies = []
+    for t in range(2):
+        lanes = slice(t * HEAD_DIM, (t + 1) * HEAD_DIM)
+        for s in range(groups):
+            held[t][:, chip_column(members, groups, s)] = parts[s][:, lanes]
+        copy = pltpu.make_async_copy(held[t], outs[t].at[pl.ds(h * half, half)], sems.at[t])
+        copy.start()
+        copies.append(copy)
+    return copies
+
+
+def join_first_kernel(members, groups, *refs):
+    dqs, pairs = refs[:groups], refs[groups : 2 * groups]
+    out, *outs = refs[2 * groups : 2 * groups + 3]
+    *held, sems = refs[2 * groups + 3 :]
+    copies = write_half(members, groups, 0, pairs, outs, held, sems)
     for s in range(groups):
         column = chip_column(members, groups, s)
         for n in range(out.shape[0] // BLK):
             packed = slice(n // 2 * BLK, (n // 2 + 1) * BLK)
             lanes = slice(n % 2 * HEAD_DIM, (n % 2 + 1) * HEAD_DIM)
-            out[n * BLK : (n + 1) * BLK, column] = refs[s][packed, lanes]
-
-
-def join_pairs_kernel(members, groups, *refs):
-    outs, held, sems = refs[-5:-3], refs[-3:-1], refs[-1]
-    half = refs[0].shape[0]
-    copies = []
-    for h in range(2):
-        at = pl.ds(h * half, half)
-        for t in range(2):
-            lanes = slice(t * HEAD_DIM, (t + 1) * HEAD_DIM)
-            for s in range(groups):
-                column = chip_column(members, groups, s)
-                held[t][at, column] = refs[h * groups + s][:, lanes]
-            copy = pltpu.make_async_copy(held[t].at[at], outs[t].at[at], sems.at[2 * h + t])
-            copy.start()
-            copies.append(copy)
+            out[n * BLK : (n + 1) * BLK, column] = dqs[s][packed, lanes]
     for copy in copies:
         copy.wait()
 
 
+def join_second_kernel(members, groups, *refs):
+    outs = refs[groups + 2 : groups + 4]
+    *held, sems = refs[groups + 4 :]
+    for copy in write_half(members, groups, 1, refs[:groups], outs, held, sems):
+        copy.wait()
+
+
 def join_heads(dqs, pairs, members, groups):
-    rows = 2 * pairs[0].shape[0]
+    half = pairs[0].shape[0]
     vmem = pl.BlockSpec(memory_space=pltpu.VMEM)
-    out = jax.ShapeDtypeStruct((rows, groups * HEAD_DIM), jnp.bfloat16)
-    token = jax.ShapeDtypeStruct((8, HEAD_DIM), jnp.float32)
-    bytes_out = 2 * rows * groups * HEAD_DIM
-    query_grad, token = pl.pallas_call(
-        functools.partial(join_queries_kernel, members, groups),
-        out_shape=[out, token],
-        in_specs=[vmem] * groups,
-        out_specs=[vmem] * 2,
-        compiler_params=pltpu.CompilerParams(vmem_limit_bytes=SMALL_LIMIT),
-        cost_estimate=pl.CostEstimate(
-            flops=0, bytes_accessed=200 * bytes_out, transcendentals=0
-        ),
-        name="join_queries",
-    )(*dqs)
+    hbm = pl.BlockSpec(memory_space=pl.ANY)
+    out = jax.ShapeDtypeStruct((2 * half, groups * HEAD_DIM), jnp.bfloat16)
+    scratch = [pltpu.VMEM((half, groups * HEAD_DIM), jnp.bfloat16)] * 2
+    scratch += [pltpu.SemaphoreType.DMA((2,))]
+    bytes_out = 2 * half * groups * HEAD_DIM
+    query_grad, key_grad, value_grad = pl.pallas_call(
+        functools.partial(join_first_kernel, members, groups),
+        out_shape=[out] * 3,
+        in_specs=[vmem] * (2 * groups),
+        out_specs=[vmem, hbm, hbm],
+        scratch_shapes=scratch,
+        compiler_params=pltpu.CompilerParams(vmem_limit_bytes=SMALL_LIMIT),
+        cost_estimate=pl.CostEstimate(flops=0, bytes_accessed=8 * bytes_out, transcendentals=0),
+        name="join_first",
+    )(*dqs, *pairs[:groups])
     key_grad, value_grad = pl.pallas_call(
-        functools.partial(join_pairs_kernel, members, groups),
+        functools.partial(join_second_kernel, members, groups),
         out_shape=[out] * 2,
-        in_specs=[vmem] * (2 * groups + 1),
-        out_specs=[pl.BlockSpec(memory_space=pl.ANY)] * 2,
-        scratch_shapes=[pltpu.VMEM(out.shape, out.dtype)] * 2 + [pltpu.SemaphoreType.DMA((4,))],
+        in_specs=[vmem] * groups + [hbm] * 2,
+        out_specs=[hbm] * 2,
+        scratch_shapes=scratch,
+        input_output_aliases={groups: 0, groups + 1: 1},
         compiler_params=pltpu.CompilerParams(vmem_limit_bytes=SMALL_LIMIT),
         cost_estimate=pl.CostEstimate(flops=0, bytes_accessed=4 * bytes_out, transcendentals=0),
-        name="join_pairs",
-    )(*pairs, token)
+        name="join_second",
+    )(*pairs[groups:], key_grad, value_grad)
     return query_grad, key_grad, value_grad
 
 

time: 59.9 us -> 59.7 us (level)
  waiting for transfers between devices: 17.2 us -> 16.3 us
  Pallas kernels: 18.2 us -> 18.8 us
    ppermute x20, waiting for transfers between devices: 17.2 us -> 16.3 us  [swapped(): return lax.ppermute(x, 'ctx', [(i, i ^ by) for i in range(count)])]
    pallas_call x2, Pallas kernels: 1.97 us -> 2.61 us  [the longest x1 1.72 us: join_heads(): pl.pallas_call(functools.partial(join_first_kernel, members, groups), out...]
  transfers between devices with their start and end apart: 20 -> 20, of which waited for: 13 -> 13; matrix products, arithmetic and copies ran while one was open for 0% -> 0% of each run, Pallas kernels for 16% -> 18%
where the time goes in v8:
time: 59.7 us; the launch traced here: 59.5 us
  starting transfers between devices  23.4 us (39%)
  Pallas kernels  18.8 us (31%)
  waiting for transfers between devices  16.3 us (27%)
  between operations  0.78 us (1%)
    ppermute x20, starting transfers between devices, swapped(): return lax.ppermute(x, 'ctx', [(i, i ^ by) for i in range(count)])  23.4 us
    ppermute x20, waiting for transfers between devices, swapped(): return lax.ppermute(x, 'ctx', [(i, i ^ by) for i in range(count)])  16.3 us
    pallas_call x2, Pallas kernels, attend(): pl.pallas_call(functools.partial(attend_kernel, late, near, shards, membe...  11.1 us
    pallas_call x2, Pallas kernels, split_early(): pl.pallas_call(functools.partial(split_early_kernel, members, groups, wan...  3.76 us
    pallas_call x1, Pallas kernels, join_heads(): pl.pallas_call(functools.partial(join_first_kernel, members, groups), out...  1.72 us
  transfers between devices with their start and end apart: 20, of which 13 were waited for; matrix products, arithmetic and copies ran while one was open for 0% of the time, Pallas kernels for 18%

profile of v8, /device:TPU:0, one launch (start us, length us, event | category | flops | bytes accessed | tf_op | source)
XLA Modules:
  0.0 59.5 jit_solution(5367127572527709705)
XLA Ops:
  0.6 0.0 copy-start.3
  0.6 0.0 copy-start.2
  0.7 0.0 copy-start.1
  0.7 0.0 copy-start
  0.7 1.8 %split_early.2.refs_4_ = bf16[512,256]{1,0:T(8,128)(2,1)} custom-call(bf16[512,512]{1,0:T(8,128)(2,1)} %refs_0_.7, bf16[512,512]{1,0:T(8,128)(2,1)} %refs_1_.5, bf16[512,512]{1,0:T(8,128)(2,1)} %refs_2_.5, bf16[512,512]{1,0:T(8,128)(2,1)} %refs_3_.5), custom_call_target="tpu_custom_call" | custom-call | bytes 524288 | tf_op jit(solution)/shard_map/split_early/pallas_call | solution.py:73
  2.5 4.0 %collective-permute-start.3 = (bf16[512,256]{1,0:T(8,128)(2,1)}, bf16[512,256]{1,0:T(8,128)(2,1)S(1)}, u32[]{:S(2)}, u32[]{:S(2)}) collective-permute-start(bf16[512,256]{1,0:T(8,128)(2,1)} %split_early.2.refs_4_), channel_id=1, source_target_pairs={{0,24},{4,28},{8,16},{12,20},{16,8},{20,12},{24,0},{28,4},{1,25},{... | collective-permute-start | bytes 786440 | tf_op jit(solution)/shard_map/ppermute | solution.py:23
  6.5 1.9 %split_early.3 = (bf16[512,256]{1,0:T(8,128)(2,1)}, bf16[512,256]{1,0:T(8,128)(2,1)}) custom-call(bf16[512,512]{1,0:T(8,128)(2,1)} %refs_0_.7, bf16[512,512]{1,0:T(8,128)(2,1)} %refs_1_.5, bf16[512,512]{1,0:T(8,128)(2,1)} %refs_2_.5, bf16[512,512]{1,0:T(8,128)(2,1)} %refs_3_.5, bf16[512,256]{1,0:T(8,128)(2,1)} %split_early.2.refs_4_), custom_call_target="tpu_custom_call" | custom-call | bytes 1048576 | tf_op jit(solution)/shard_map/split_early/pallas_call | solution.py:73
  8.4 0.6 collective-permute-start.4
  9.0 0.1 collective-permute-start.5
  9.1 0.2 split_rest.1
  9.4 2.9 %collective-permute-start = (bf16[528,256]{1,0:T(8,128)(2,1)S(1)}, bf16[528,256]{1,0:T(8,128)(2,1)S(1)}, u32[]{:S(2)}, u32[]{:S(2)}) collective-permute-start(bf16[528,256]{1,0:T(8,128)(2,1)S(1)} %get-tuple-element.41), channel_id=1, source_target_pairs={{0,24},{4,28},{8,16},{12,20},{16,8},{20,12},{24,0},{28,4},{1,25},{... | collective-permute-start | bytes 811016 | tf_op jit(solution)/shard_map/ppermute | solution.py:23
  12.3 0.5 collective-permute-start.1
  12.8 1.0 %collective-permute-done.3.refs_1_.refs_2_ = bf16[512,256]{1,0:T(8,128)(2,1)S(1)} collective-permute-done((bf16[512,256]{1,0:T(8,128)(2,1)}, bf16[512,256]{1,0:T(8,128)(2,1)S(1)}, u32[]{:S(2)}, u32[]{:S(2)}) %collective-permute-start.3) | collective-permute-done | bytes 262176 | tf_op jit(solution)/shard_map/ppermute | solution.py:23
  13.8 2.0 %collective-permute-start.2 = (bf16[528,256]{1,0:T(8,128)(2,1)S(1)}, bf16[528,256]{1,0:T(8,128)(2,1)S(1)}, u32[]{:S(2)}, u32[]{:S(2)}) collective-permute-start(bf16[528,256]{1,0:T(8,128)(2,1)S(1)} %get-tuple-element.43), channel_id=1, source_target_pairs={{0,8},{4,12},{8,0},{12,4},{16,24},{20,28},{24,16},{28,20},{1,9},{5... | collective-permute-start | bytes 811016 | tf_op jit(solution)/shard_map/ppermute | solution.py:23
  15.9 3.7 %collective-permute-done.4.refs_2_.refs_3_ = bf16[512,256]{1,0:T(8,128)(2,1)S(1)} collective-permute-done((bf16[512,256]{1,0:T(8,128)(2,1)}, bf16[512,256]{1,0:T(8,128)(2,1)S(1)}, u32[]{:S(2)}, u32[]{:S(2)}) %collective-permute-start.4) | collective-permute-done | bytes 262176 | tf_op jit(solution)/shard_map/ppermute | solution.py:23
  19.5 0.5 collective-permute-done.5.refs_3_.refs_4_
  20.1 0.8 %only_pairs.3 = (bf16[2,256,256]{2,1,0:T(8,128)(2,1)}, bf16[2,256,256]{2,1,0:T(8,128)(2,1)}) custom-call(bf16[512,256]{1,0:T(8,128)(2,1)S(1)} %get-tuple-element.44.refs_0_.refs_1_, bf16[512,256]{1,0:T(8,128)(2,1)S(1)} %collective-permute-done.3.refs_1_.refs_2_, bf16[512,256]{1,0:T(8,128)(2,1)S(1)} %collective-permute-done.4.refs_2_.refs_3_, ...), custom_call_target="tpu_custom_call" | custom-call | bytes 1048576 | tf_op jit(solution)/shard_map/only_pairs/pallas_call | solution.py:130
  20.9 0.5 collective-permute-start.7
  21.4 0.1 copy.13.refs_0_
  21.5 1.1 %collective-permute-done.6.refs_5_ = bf16[2,256,256]{2,1,0:T(8,128)(2,1)S(1)} collective-permute-done((bf16[2,256,256]{2,1,0:T(8,128)(2,1)}, bf16[2,256,256]{2,1,0:T(8,128)(2,1)S(1)}, u32[]{:S(2)}, u32[]{:S(2)}) %collective-permute-start.6) | collective-permute-done | bytes 262176 | tf_op jit(solution)/shard_map/ppermute | solution.py:23
  22.6 0.4 collective-permute-done.7.refs_6_
  23.0 5.6 %attend_early.1 = (bf16[128,256]{1,0:T(8,128)(2,1)S(1)}, bf16[128,256]{1,0:T(8,128)(2,1)S(1)}, bf16[128,256]{1,0:T(8,128)(2,1)S(1)}, bf16[128,256]{1,0:T(8,128)(...) custom-call(s32[32,6]{1,0:T(8,128)S(1)} %copy.13.refs_0_, ...), custom_call_target="tpu_custom_call" | custom-call | tf_op jit(solution)/shard_map/attend_early/pallas_call | solution.py:385
  28.6 0.0 collective-permute-done.refs_1_.refs_2_
  28.6 0.2 collective-permute-start.8
  28.9 1.4 %collective-permute-done.1.refs_0_.refs_3_ = bf16[528,256]{1,0:T(8,128)(2,1)S(1)} collective-permute-done((bf16[528,256]{1,0:T(8,128)(2,1)S(1)}, bf16[528,256]{1,0:T(8,128)(2,1)S(1)}, u32[]{:S(2)}, u32[]{:S(2)}) %collective-permute-start.1) | collective-permute-done | bytes 270368 | tf_op jit(solution)/shard_map/ppermute | solution.py:23
  30.2 0.3 collective-permute-done.2.refs_1_.refs_4_
  30.6 0.1 collective-permute-start.9
  30.7 1.5 %collective-permute-done.9.refs_6_ = bf16[2,256,256]{2,1,0:T(8,128)(2,1)S(1)} collective-permute-done((bf16[2,256,256]{2,1,0:T(8,128)(2,1)S(1)}, bf16[2,256,256]{2,1,0:T(8,128)(2,1)S(1)}, u32[]{:S(2)}, u32[]{:S(2)}) %collective-permute-start.9) | collective-permute-done | bytes 262176 | tf_op jit(solution)/shard_map/ppermute | solution.py:23
  32.2 5.5 %attend_late.1 = (bf16[256,256]{1,0:T(8,128)(2,1)S(1)}, bf16[256,256]{1,0:T(8,128)(2,1)S(1)}, bf16[256,256]{1,0:T(8,128)(2,1)S(1)}, bf16[256,256]{1,0:T(8,128)(2...) custom-call(s32[32,6]{1,0:T(8,128)S(1)} %copy.13.refs_0_, ...), custom_call_target="tpu_custom_call", output_to_operand_aliasing={{9}: (11, {}), {10}: (12, {})} | custom-call | flops 1342177280 | bytes 4194304 | tf_op jit(solution)/shard_map/attend_late/pallas_call | solution.py:385
  37.6 0.2 collective-permute-start.13
  37.8 2.3 %collective-permute-start.10 = (bf16[256,256]{1,0:T(8,128)(2,1)S(1)}, bf16[256,256]{1,0:T(8,128)(2,1)S(1)}, u32[]{:S(2)}, u32[]{:S(2)}) collective-permute-start(bf16[256,256]{1,0:T(8,128)(2,1)S(1)} %get-tuple-element.56), channel_id=1, source_target_pairs={{0,24},{4,28},{8,16},{12,20},{16,8},{20,12},{24,0},{28,4},{1,25},{... | collective-permute-start | bytes 393224 | tf_op jit(solution)/shard_map/ppermute | solution.py:23
  40.2 0.6 %collective-permute-start.11 = (bf16[256,256]{1,0:T(8,128)(2,1)S(1)}, bf16[256,256]{1,0:T(8,128)(2,1)S(1)}, u32[]{:S(2)}, u32[]{:S(2)}) collective-permute-start(bf16[256,256]{1,0:T(8,128)(2,1)S(1)} %get-tuple-element.57), channel_id=1, source_target_pairs={{0,16},{4,20},{8,24},{12,28},{16,0},{20,4},{24,8},{28,12},{1,17},{... | collective-permute-start | bytes 393224 | tf_op jit(solution)/shard_map/ppermute | solution.py:23
  40.8 0.5 collective-permute-start.12
  41.3 0.3 add_partials.1
  41.7 2.4 %collective-permute-start.14 = (bf16[256,256]{1,0:T(8,128)(2,1)S(1)}, bf16[256,256]{1,0:T(8,128)(2,1)S(1)}, u32[]{:S(2)}, u32[]{:S(2)}) collective-permute-start(bf16[256,256]{1,0:T(8,128)(2,1)S(1)} %get-tuple-element.65), channel_id=1, source_target_pairs={{0,24},{4,28},{8,16},{12,20},{16,8},{20,12},{24,0},{28,4},{1,25},{... | collective-permute-start | bytes 393224 | tf_op jit(solution)/shard_map/ppermute | solution.py:23
  44.0 0.6 %collective-permute-start.15 = (bf16[256,256]{1,0:T(8,128)(2,1)S(1)}, bf16[256,256]{1,0:T(8,128)(2,1)S(1)}, u32[]{:S(2)}, u32[]{:S(2)}) collective-permute-start(bf16[256,256]{1,0:T(8,128)(2,1)S(1)} %get-tuple-element.66), channel_id=1, source_target_pairs={{0,16},{4,20},{8,24},{12,28},{16,0},{20,4},{24,8},{28,12},{1,17},{... | collective-permute-start | bytes 393224 | tf_op jit(solution)/shard_map/ppermute | solution.py:23
  44.7 0.3 collective-permute-done.10.refs_1_
  45.0 1.6 %collective-permute-start.16 = (bf16[256,256]{1,0:T(8,128)(2,1)S(1)}, bf16[256,256]{1,0:T(8,128)(2,1)S(1)}, u32[]{:S(2)}, u32[]{:S(2)}) collective-permute-start(bf16[256,256]{1,0:T(8,128)(2,1)S(1)} %get-tuple-element.67), channel_id=1, source_target_pairs={{0,8},{4,12},{8,0},{12,4},{16,24},{20,28},{24,16},{28,20},{1,9},{5... | collective-permute-start | bytes 393224 | tf_op jit(solution)/shard_map/ppermute | solution.py:23
  46.6 1.5 %collective-permute-done.11.refs_2_ = bf16[256,256]{1,0:T(8,128)(2,1)S(1)} collective-permute-done((bf16[256,256]{1,0:T(8,128)(2,1)S(1)}, bf16[256,256]{1,0:T(8,128)(2,1)S(1)}, u32[]{:S(2)}, u32[]{:S(2)}) %collective-permute-start.11) | collective-permute-done | bytes 131104 | tf_op jit(solution)/shard_map/ppermute | solution.py:23
  48.1 2.2 %collective-permute-start.17 = (bf16[256,256]{1,0:T(8,128)(2,1)S(1)}, bf16[256,256]{1,0:T(8,128)(2,1)S(1)}, u32[]{:S(2)}, u32[]{:S(2)}) collective-permute-start(bf16[256,256]{1,0:T(8,128)(2,1)S(1)} %get-tuple-element.70), channel_id=1, source_target_pairs={{0,24},{4,28},{8,16},{12,20},{16,8},{20,12},{24,0},{28,4},{1,25},{... | collective-permute-start | bytes 393224 | tf_op jit(solution)/shard_map/ppermute | solution.py:23
  50.3 0.6 %collective-permute-start.18 = (bf16[256,256]{1,0:T(8,128)(2,1)S(1)}, bf16[256,256]{1,0:T(8,128)(2,1)S(1)}, u32[]{:S(2)}, u32[]{:S(2)}) collective-permute-start(bf16[256,256]{1,0:T(8,128)(2,1)S(1)} %get-tuple-element.71), channel_id=1, source_target_pairs={{0,16},{4,20},{8,24},{12,28},{16,0},{20,4},{24,8},{28,12},{1,17},{... | collective-permute-start | bytes 393224 | tf_op jit(solution)/shard_map/ppermute | solution.py:23
  50.9 1.3 %collective-permute-start.19 = (bf16[256,256]{1,0:T(8,128)(2,1)S(1)}, bf16[256,256]{1,0:T(8,128)(2,1)S(1)}, u32[]{:S(2)}, u32[]{:S(2)}) collective-permute-start(bf16[256,256]{1,0:T(8,128)(2,1)S(1)} %get-tuple-element.72), channel_id=1, source_target_pairs={{0,8},{4,12},{8,0},{12,4},{16,24},{20,28},{24,16},{28,20},{1,9},{5... | collective-permute-start | bytes 393224 | tf_op jit(solution)/shard_map/ppermute | solution.py:23
  52.3 1.5 %collective-permute-done.15.refs_6_ = bf16[256,256]{1,0:T(8,128)(2,1)S(1)} collective-permute-done((bf16[256,256]{1,0:T(8,128)(2,1)S(1)}, bf16[256,256]{1,0:T(8,128)(2,1)S(1)}, u32[]{:S(2)}, u32[]{:S(2)}) %collective-permute-start.15) | collective-permute-done | bytes 131104 | tf_op jit(solution)/shard_map/ppermute | solution.py:23
  53.7 1.7 %join_first.1 = (bf16[512,512]{1,0:T(8,128)(2,1)}, bf16[512,512]{1,0:T(8,128)(2,1)}, bf16[512,512]{1,0:T(8,128)(2,1)}) custom-call(bf16[256,256]{1,0:T(8,128)(2,1)S(1)} %get-tuple-element.55.refs_0_, bf16[256,256]{1,0:T(8,128)(2,1)S(1)} %collective-permute-done.10.refs_1_, bf16[256,256]{1,0:T(8,128)(2,1)S(1)} %collective-permute-done.11.refs_2_, ...), custom_call_target="tpu_custom_call" | custom-call | bytes 2097152 | tf_op jit(solution)/shard_map/join_first/pallas_call | solution.py:186
  55.5 1.1 %collective-permute-done.17.refs_1_ = bf16[256,256]{1,0:T(8,128)(2,1)S(1)} collective-permute-done((bf16[256,256]{1,0:T(8,128)(2,1)S(1)}, bf16[256,256]{1,0:T(8,128)(2,1)S(1)}, u32[]{:S(2)}, u32[]{:S(2)}) %collective-permute-start.17) | collective-permute-done | bytes 131104 | tf_op jit(solution)/shard_map/ppermute | solution.py:23
  56.5 2.0 %collective-permute-done.18.refs_2_ = bf16[256,256]{1,0:T(8,128)(2,1)S(1)} collective-permute-done((bf16[256,256]{1,0:T(8,128)(2,1)S(1)}, bf16[256,256]{1,0:T(8,128)(2,1)S(1)}, u32[]{:S(2)}, u32[]{:S(2)}) %collective-permute-start.18) | collective-permute-done | bytes 131104 | tf_op jit(solution)/shard_map/ppermute | solution.py:23
  58.6 0.0 collective-permute-done.19.refs_3_
  58.6 0.9 %join_second.1 = (bf16[512,512]{1,0:T(8,128)(2,1)}, bf16[512,512]{1,0:T(8,128)(2,1)}) custom-call(bf16[256,256]{1,0:T(8,128)(2,1)S(1)} %get-tuple-element.69.refs_0_, bf16[256,256]{1,0:T(8,128)(2,1)S(1)} %collective-permute-done.17.refs_1_, bf16[256,256]{1,0:T(8,128)(2,1)S(1)} %collective-permute-done.18.refs_2_, ...), custom_call_target="tpu_custom_call", output_to_operand_aliasing={{0}: (4, {}), {1}: (5, {})} | custom-call | bytes 1048576 | tf_op jit(solution)/shard_map/join_second/pallas_call | solution.py:196
  (14 shorter events, 0.1 us)
Async XLA Ops:
  0.6 8.5 %copy-start.3 = (bf16[512,512]{1,0:T(8,128)(2,1)S(1)}, bf16[512,512]{1,0:T(8,128)(2,1)}, u32[]{:S(2)}) copy-start(bf16[512,512]{1,0:T(8,128)(2,1)} %refs_3_.5) | copy-start | bytes 1572868
  0.6 8.5 %copy-start.2 = (bf16[512,512]{1,0:T(8,128)(2,1)S(1)}, bf16[512,512]{1,0:T(8,128)(2,1)}, u32[]{:S(2)}) copy-start(bf16[512,512]{1,0:T(8,128)(2,1)} %refs_2_.5) | copy-start | bytes 1572868
  0.7 8.5 %copy-start.1 = (bf16[512,512]{1,0:T(8,128)(2,1)S(1)}, bf16[512,512]{1,0:T(8,128)(2,1)}, u32[]{:S(2)}) copy-start(bf16[512,512]{1,0:T(8,128)(2,1)} %refs_1_.5) | copy-start | bytes 1572868
  0.7 8.4 %copy-start = (bf16[512,512]{1,0:T(8,128)(2,1)S(1)}, bf16[512,512]{1,0:T(8,128)(2,1)}, u32[]{:S(2)}) copy-start(bf16[512,512]{1,0:T(8,128)(2,1)} %refs_0_.7) | copy-start | bytes 1572868
  0.7 20.7 %copy-start.4 = (s32[32,6]{0,1:T(8,128)S(1)}, s32[32,6]{0,1:T(8,128)}, u32[]{:S(2)}) copy-start(s32[32,6]{0,1:T(8,128)} %param.9) | copy-start | bytes 2308
  2.5 11.3 %collective-permute-start.3 = (bf16[512,256]{1,0:T(8,128)(2,1)}, bf16[512,256]{1,0:T(8,128)(2,1)S(1)}, u32[]{:S(2)}, u32[]{:S(2)}) collective-permute-start(bf16[512,256]{1,0:T(8,128)(2,1)} %split_early.2.refs_4_), channel_id=1, source_target_pairs={{0,24},{4,28},{8,16},{12,20},{16,8},{20,12},{24,0},{28,4},{1,25},{... | collective-permute-start | bytes 786440 | tf_op jit(solution)/shard_map/ppermute | solution.py:23
  8.4 11.1 %collective-permute-start.4 = (bf16[512,256]{1,0:T(8,128)(2,1)}, bf16[512,256]{1,0:T(8,128)(2,1)S(1)}, u32[]{:S(2)}, u32[]{:S(2)}) collective-permute-start(bf16[512,256]{1,0:T(8,128)(2,1)} %get-tuple-element.45), channel_id=1, source_target_pairs={{0,16},{4,20},{8,24},{12,28},{16,0},{20,4},{24,8},{28,12},{1,17},{... | collective-permute-start | bytes 786440 | tf_op jit(solution)/shard_map/ppermute | solution.py:23
  9.0 11.1 %collective-permute-start.5 = (bf16[512,256]{1,0:T(8,128)(2,1)}, bf16[512,256]{1,0:T(8,128)(2,1)S(1)}, u32[]{:S(2)}, u32[]{:S(2)}) collective-permute-start(bf16[512,256]{1,0:T(8,128)(2,1)} %get-tuple-element.46), channel_id=1, source_target_pairs={{0,8},{4,12},{8,0},{12,4},{16,24},{20,28},{24,16},{28,20},{1,9},{5... | collective-permute-start | bytes 786440 | tf_op jit(solution)/shard_map/ppermute | solution.py:23
  9.4 19.2 %collective-permute-start = (bf16[528,256]{1,0:T(8,128)(2,1)S(1)}, bf16[528,256]{1,0:T(8,128)(2,1)S(1)}, u32[]{:S(2)}, u32[]{:S(2)}) collective-permute-start(bf16[528,256]{1,0:T(8,128)(2,1)S(1)} %get-tuple-element.41), channel_id=1, source_target_pairs={{0,24},{4,28},{8,16},{12,20},{16,8},{20,12},{24,0},{28,4},{1,25},{... | collective-permute-start | bytes 811016 | tf_op jit(solution)/shard_map/ppermute | solution.py:23
  12.3 17.9 %collective-permute-start.1 = (bf16[528,256]{1,0:T(8,128)(2,1)S(1)}, bf16[528,256]{1,0:T(8,128)(2,1)S(1)}, u32[]{:S(2)}, u32[]{:S(2)}) collective-permute-start(bf16[528,256]{1,0:T(8,128)(2,1)S(1)} %get-tuple-element.42), channel_id=1, source_target_pairs={{0,16},{4,20},{8,24},{12,28},{16,0},{20,4},{24,8},{28,12},{1,17},{... | collective-permute-start | bytes 811016 | tf_op jit(solution)/shard_map/ppermute | solution.py:23
  13.8 16.7 %collective-permute-start.2 = (bf16[528,256]{1,0:T(8,128)(2,1)S(1)}, bf16[528,256]{1,0:T(8,128)(2,1)S(1)}, u32[]{:S(2)}, u32[]{:S(2)}) collective-permute-start(bf16[528,256]{1,0:T(8,128)(2,1)S(1)} %get-tuple-element.43), channel_id=1, source_target_pairs={{0,8},{4,12},{8,0},{12,4},{16,24},{20,28},{24,16},{28,20},{1,9},{5... | collective-permute-start | bytes 811016 | tf_op jit(solution)/shard_map/ppermute | solution.py:23
  20.9 1.7 %collective-permute-start.6 = (bf16[2,256,256]{2,1,0:T(8,128)(2,1)}, bf16[2,256,256]{2,1,0:T(8,128)(2,1)S(1)}, u32[]{:S(2)}, u32[]{:S(2)}) collective-permute-start(bf16[2,256,256]{2,1,0:T(8,128)(2,1)} %get-tuple-element.47), channel_id=1, source_target_pairs={{0,4},{4,0},{8,12},{12,8},{16,20},{20,16},{24,28},{28,24},{1,5},{5... | collective-permute-start | bytes 786440 | tf_op jit(solution)/shard_map/ppermute | solution.py:23
  20.9 2.1 %collective-permute-start.7 = (bf16[2,256,256]{2,1,0:T(8,128)(2,1)}, bf16[2,256,256]{2,1,0:T(8,128)(2,1)S(1)}, u32[]{:S(2)}, u32[]{:S(2)}) collective-permute-start(bf16[2,256,256]{2,1,0:T(8,128)(2,1)} %get-tuple-element.48), channel_id=1, source_target_pairs={{0,4},{4,0},{8,12},{12,8},{16,20},{20,16},{24,28},{28,24},{1,5},{5... | collective-permute-start | bytes 786440 | tf_op jit(solution)/shard_map/ppermute | solution.py:23
  28.6 2.0 %collective-permute-start.8 = (bf16[2,256,256]{2,1,0:T(8,128)(2,1)S(1)}, bf16[2,256,256]{2,1,0:T(8,128)(2,1)S(1)}, u32[]{:S(2)}, u32[]{:S(2)}) collective-permute-start(bf16[2,256,256]{2,1,0:T(8,128)(2,1)S(1)} %only_pairs.4), channel_id=1, source_target_pairs={{0,4},{4,0},{8,12},{12,8},{16,20},{20,16},{24,28},{28,24},{1,5},{5... | collective-permute-start | bytes 786440 | tf_op jit(solution)/shard_map/ppermute | solution.py:23
  30.6 1.6 %collective-permute-start.9 = (bf16[2,256,256]{2,1,0:T(8,128)(2,1)S(1)}, bf16[2,256,256]{2,1,0:T(8,128)(2,1)S(1)}, u32[]{:S(2)}, u32[]{:S(2)}) collective-permute-start(bf16[2,256,256]{2,1,0:T(8,128)(2,1)S(1)} %only_pairs.5), channel_id=1, source_target_pairs={{0,4},{4,0},{8,12},{12,8},{16,20},{20,16},{24,28},{28,24},{1,5},{5... | collective-permute-start | bytes 786440 | tf_op jit(solution)/shard_map/ppermute | solution.py:23
  37.6 3.7 %collective-permute-start.13 = (bf16[4,512,256]{2,1,0:T(8,128)(2,1)S(1)}, bf16[4,512,256]{2,1,0:T(8,128)(2,1)S(1)}, u32[]{:S(2)}, u32[]{:S(2)}) collective-permute-start(bf16[4,512,256]{2,1,0:T(8,128)(2,1)S(1)} %get-tuple-element.59), channel_id=1, source_target_pairs={{0,4},{4,0},{8,12},{12,8},{16,20},{20,16},{24,28},{28,24},{1,5},{5... | collective-permute-start | bytes 3145736 | tf_op jit(solution)/shard_map/ppermute | solution.py:23
  37.8 7.1 %collective-permute-start.10 = (bf16[256,256]{1,0:T(8,128)(2,1)S(1)}, bf16[256,256]{1,0:T(8,128)(2,1)S(1)}, u32[]{:S(2)}, u32[]{:S(2)}) collective-permute-start(bf16[256,256]{1,0:T(8,128)(2,1)S(1)} %get-tuple-element.56), channel_id=1, source_target_pairs={{0,24},{4,28},{8,16},{12,20},{16,8},{20,12},{24,0},{28,4},{1,25},{... | collective-permute-start | bytes 393224 | tf_op jit(solution)/shard_map/ppermute | solution.py:23
  40.2 8.0 %collective-permute-start.11 = (bf16[256,256]{1,0:T(8,128)(2,1)S(1)}, bf16[256,256]{1,0:T(8,128)(2,1)S(1)}, u32[]{:S(2)}, u32[]{:S(2)}) collective-permute-start(bf16[256,256]{1,0:T(8,128)(2,1)S(1)} %get-tuple-element.57), channel_id=1, source_target_pairs={{0,16},{4,20},{8,24},{12,28},{16,0},{20,4},{24,8},{28,12},{1,17},{... | collective-permute-start | bytes 393224 | tf_op jit(solution)/shard_map/ppermute | solution.py:23
  40.8 9.5 %collective-permute-start.12 = (bf16[256,256]{1,0:T(8,128)(2,1)S(1)}, bf16[256,256]{1,0:T(8,128)(2,1)S(1)}, u32[]{:S(2)}, u32[]{:S(2)}) collective-permute-start(bf16[256,256]{1,0:T(8,128)(2,1)S(1)} %get-tuple-element.58), channel_id=1, source_target_pairs={{0,8},{4,12},{8,0},{12,4},{16,24},{20,28},{24,16},{28,20},{1,9},{5... | collective-permute-start | bytes 393224 | tf_op jit(solution)/shard_map/ppermute | solution.py:23
  41.7 9.3 %collective-permute-start.14 = (bf16[256,256]{1,0:T(8,128)(2,1)S(1)}, bf16[256,256]{1,0:T(8,128)(2,1)S(1)}, u32[]{:S(2)}, u32[]{:S(2)}) collective-permute-start(bf16[256,256]{1,0:T(8,128)(2,1)S(1)} %get-tuple-element.65), channel_id=1, source_target_pairs={{0,24},{4,28},{8,16},{12,20},{16,8},{20,12},{24,0},{28,4},{1,25},{... | collective-permute-start | bytes 393224 | tf_op jit(solution)/shard_map/ppermute | solution.py:23
  44.0 9.7 %collective-permute-start.15 = (bf16[256,256]{1,0:T(8,128)(2,1)S(1)}, bf16[256,256]{1,0:T(8,128)(2,1)S(1)}, u32[]{:S(2)}, u32[]{:S(2)}) collective-permute-start(bf16[256,256]{1,0:T(8,128)(2,1)S(1)} %get-tuple-element.66), channel_id=1, source_target_pairs={{0,16},{4,20},{8,24},{12,28},{16,0},{20,4},{24,8},{28,12},{1,17},{... | collective-permute-start | bytes 393224 | tf_op jit(solution)/shard_map/ppermute | solution.py:23
  45.0 8.8 %collective-permute-start.16 = (bf16[256,256]{1,0:T(8,128)(2,1)S(1)}, bf16[256,256]{1,0:T(8,128)(2,1)S(1)}, u32[]{:S(2)}, u32[]{:S(2)}) collective-permute-start(bf16[256,256]{1,0:T(8,128)(2,1)S(1)} %get-tuple-element.67), channel_id=1, source_target_pairs={{0,8},{4,12},{8,0},{12,4},{16,24},{20,28},{24,16},{28,20},{1,9},{5... | collective-permute-start | bytes 393224 | tf_op jit(solution)/shard_map/ppermute | solution.py:23
  48.1 8.4 %collective-permute-start.17 = (bf16[256,256]{1,0:T(8,128)(2,1)S(1)}, bf16[256,256]{1,0:T(8,128)(2,1)S(1)}, u32[]{:S(2)}, u32[]{:S(2)}) collective-permute-start(bf16[256,256]{1,0:T(8,128)(2,1)S(1)} %get-tuple-element.70), channel_id=1, source_target_pairs={{0,24},{4,28},{8,16},{12,20},{16,8},{20,12},{24,0},{28,4},{1,25},{... | collective-permute-start | bytes 393224 | tf_op jit(solution)/shard_map/ppermute | solution.py:23
  50.3 8.3 %collective-permute-start.18 = (bf16[256,256]{1,0:T(8,128)(2,1)S(1)}, bf16[256,256]{1,0:T(8,128)(2,1)S(1)}, u32[]{:S(2)}, u32[]{:S(2)}) collective-permute-start(bf16[256,256]{1,0:T(8,128)(2,1)S(1)} %get-tuple-element.71), channel_id=1, source_target_pairs={{0,16},{4,20},{8,24},{12,28},{16,0},{20,4},{24,8},{28,12},{1,17},{... | collective-permute-start | bytes 393224 | tf_op jit(solution)/shard_map/ppermute | solution.py:23
  50.9 7.7 %collective-permute-start.19 = (bf16[256,256]{1,0:T(8,128)(2,1)S(1)}, bf16[256,256]{1,0:T(8,128)(2,1)S(1)}, u32[]{:S(2)}, u32[]{:S(2)}) collective-permute-start(bf16[256,256]{1,0:T(8,128)(2,1)S(1)} %get-tuple-element.72), channel_id=1, source_target_pairs={{0,8},{4,12},{8,0},{12,4},{16,24},{20,28},{24,16},{28,20},{1,9},{5... | collective-permute-start | bytes 393224 | tf_op jit(solution)/shard_map/ppermute | solution.py:23

commit v9 on v8

--- a/solution.py
+++ b/solution.py
@@ -116,25 +116,24 @@
     return [own, *early], late
 
 
-def pairs_kernel(groups, *refs):
-    outs = refs[-(groups // 2) :]
-    for s in range(groups):
-        out = outs[s // 2]
-        out[s % 2] = refs[s][: out.shape[1], :]
-
-
-def only_pairs(packs, half, after, groups):
+def pairs_kernel(per, outs, *refs):
+    for s in range(per * outs):
+        out = refs[s // per - outs]
+        out[s % per] = refs[s][: out.shape[1], :]
+
+
+def only_pairs(packs, half, after, per):
     hbm = pl.BlockSpec(memory_space=pl.ANY)
     vmem = pl.BlockSpec(memory_space=pltpu.VMEM)
-    outs = groups // 2
+    outs = len(packs) // per
     return pl.pallas_call(
-        functools.partial(pairs_kernel, groups),
-        out_shape=[jax.ShapeDtypeStruct((2, half, 2 * HEAD_DIM), jnp.bfloat16)] * outs,
-        in_specs=[vmem] * groups + [hbm] * len(after),
+        functools.partial(pairs_kernel, per, outs),
+        out_shape=[jax.ShapeDtypeStruct((per, half, 2 * HEAD_DIM), jnp.bfloat16)] * outs,
+        in_specs=[vmem] * len(packs) + [hbm] * len(after),
         out_specs=[vmem] * outs,
         compiler_params=pltpu.CompilerParams(vmem_limit_bytes=SMALL_LIMIT),
         cost_estimate=pl.CostEstimate(
-            flops=0, bytes_accessed=8 * groups * half * HEAD_DIM, transcendentals=0
+            flops=0, bytes_accessed=8 * len(packs) * half * HEAD_DIM, transcendentals=0
         ),
         name="only_pairs",
     )(*packs, *after)
@@ -251,9 +250,9 @@
     stretch = half // BLK
     links = refs[0]
     packs = [*refs[1 : 1 + groups]]
-    lent = (members - 1) * (groups // 2)
+    lent = (members - 1) * (groups - 1 if late else groups // 2)
     for part in refs[1 + groups : 1 + groups + lent]:
-        packs += [part.at[n] for n in range(2)]
+        packs += [part.at[n] for n in range(part.shape[0])]
     refs = refs[1 + groups + lent :]
     if late:
         dq_early = refs[:groups]
@@ -429,11 +428,11 @@
     early, late = split_heads(arrays, members, groups)
     early = to_chips(early, members)
     late = to_chips(late, members)
-    early = early + with_members(only_pairs(early, rows // 2, [], groups), members)
+    early = early + with_members(only_pairs(early, rows // 2, [], 2), members)
     dq_early, buffers = attend(links, early, [], [], rows, shards, members, groups)
-    lent = []
-    for s in range(0, groups, 2):
-        lent += only_pairs(late[s : s + 2], rows // 2, dq_early[:1], 2)
+    lent = only_pairs(late[:2], rows // 2, dq_early[:1], 2)
+    for s in range(2, groups):
+        lent += only_pairs(late[s : s + 1], rows // 2, dq_early[:1], 1)
     late = late + with_members(lent, members)
     dqs, own, far = attend(links, late, dq_early, buffers, rows, shards, members, groups)
     far = [swapped(part, r) for r, part in enumerate(far, 1)]

time: 59.7 us -> 59.8 us (level)
    ppermute x20 -> x21, starting transfers between devices: 23.4 us -> 23.8 us  [swapped(): return lax.ppermute(x, 'ctx', [(i, i ^ by) for i in range(count)])]
    ppermute x20 -> x21, waiting for transfers between devices: 16.3 us -> 16 us  [swapped(): return lax.ppermute(x, 'ctx', [(i, i ^ by) for i in range(count)])]
  transfers between devices with their start and end apart: 20 -> 21, of which waited for: 13 -> 13; matrix products, arithmetic and copies ran while one was open for 0% -> 0% of each run, Pallas kernels for 18% -> 18%
where the time goes in v9:
time: 59.8 us; the launch traced here: 59.6 us
  starting transfers between devices  23.8 us (40%)
  Pallas kernels  18.9 us (32%)
  waiting for transfers between devices  16 us (27%)
  between operations  0.79 us (1%)
    ppermute x21, starting transfers between devices, swapped(): return lax.ppermute(x, 'ctx', [(i, i ^ by) for i in range(count)])  23.8 us
    ppermute x21, waiting for transfers between devices, swapped(): return lax.ppermute(x, 'ctx', [(i, i ^ by) for i in range(count)])  16 us
    pallas_call x2, Pallas kernels, attend(): pl.pallas_call(functools.partial(attend_kernel, late, near, shards, membe...  11.1 us
    pallas_call x2, Pallas kernels, split_early(): pl.pallas_call(functools.partial(split_early_kernel, members, groups, wan...  3.76 us
    pallas_call x1, Pallas kernels, join_heads(): pl.pallas_call(functools.partial(join_first_kernel, members, groups), out...  1.72 us
  transfers between devices with their start and end apart: 21, of which 13 were waited for; matrix products, arithmetic and copies ran while one was open for 0% of the time, Pallas kernels for 18%

profile of v9, /device:TPU:0, one launch (start us, length us, event | category | flops | bytes accessed | tf_op | source)
XLA Modules:
  0.0 59.6 jit_solution(8346450690581213199)
XLA Ops:
  0.6 0.0 copy-start.3
  0.6 0.0 copy-start.2
  0.7 0.0 copy-start.1
  0.7 0.0 copy-start
  0.7 1.8 %split_early.2.refs_4_ = bf16[512,256]{1,0:T(8,128)(2,1)} custom-call(bf16[512,512]{1,0:T(8,128)(2,1)} %refs_0_.7, bf16[512,512]{1,0:T(8,128)(2,1)} %refs_1_.5, bf16[512,512]{1,0:T(8,128)(2,1)} %refs_2_.5, bf16[512,512]{1,0:T(8,128)(2,1)} %refs_3_.5), custom_call_target="tpu_custom_call" | custom-call | bytes 524288 | tf_op jit(solution)/shard_map/split_early/pallas_call | solution.py:73
  2.5 4.0 %collective-permute-start.3 = (bf16[512,256]{1,0:T(8,128)(2,1)}, bf16[512,256]{1,0:T(8,128)(2,1)S(1)}, u32[]{:S(2)}, u32[]{:S(2)}) collective-permute-start(bf16[512,256]{1,0:T(8,128)(2,1)} %split_early.2.refs_4_), channel_id=1, source_target_pairs={{0,24},{4,28},{8,16},{12,20},{16,8},{20,12},{24,0},{28,4},{1,25},{... | collective-permute-start | bytes 786440 | tf_op jit(solution)/shard_map/ppermute | solution.py:23
  6.5 1.9 %split_early.3 = (bf16[512,256]{1,0:T(8,128)(2,1)}, bf16[512,256]{1,0:T(8,128)(2,1)}) custom-call(bf16[512,512]{1,0:T(8,128)(2,1)} %refs_0_.7, bf16[512,512]{1,0:T(8,128)(2,1)} %refs_1_.5, bf16[512,512]{1,0:T(8,128)(2,1)} %refs_2_.5, bf16[512,512]{1,0:T(8,128)(2,1)} %refs_3_.5, bf16[512,256]{1,0:T(8,128)(2,1)} %split_early.2.refs_4_), custom_call_target="tpu_custom_call" | custom-call | bytes 1048576 | tf_op jit(solution)/shard_map/split_early/pallas_call | solution.py:73
  8.4 0.6 collective-permute-start.4
  9.0 0.1 collective-permute-start.5
  9.1 0.2 split_rest.1
  9.4 2.9 %collective-permute-start = (bf16[528,256]{1,0:T(8,128)(2,1)S(1)}, bf16[528,256]{1,0:T(8,128)(2,1)S(1)}, u32[]{:S(2)}, u32[]{:S(2)}) collective-permute-start(bf16[528,256]{1,0:T(8,128)(2,1)S(1)} %get-tuple-element.41), channel_id=1, source_target_pairs={{0,24},{4,28},{8,16},{12,20},{16,8},{20,12},{24,0},{28,4},{1,25},{... | collective-permute-start | bytes 811016 | tf_op jit(solution)/shard_map/ppermute | solution.py:23
  12.3 1.5 %collective-permute-done.3.refs_1_.refs_2_ = bf16[512,256]{1,0:T(8,128)(2,1)S(1)} collective-permute-done((bf16[512,256]{1,0:T(8,128)(2,1)}, bf16[512,256]{1,0:T(8,128)(2,1)S(1)}, u32[]{:S(2)}, u32[]{:S(2)}) %collective-permute-start.3) | collective-permute-done | bytes 262176 | tf_op jit(solution)/shard_map/ppermute | solution.py:23
  13.8 5.6 %collective-permute-done.4.refs_2_.refs_3_ = bf16[512,256]{1,0:T(8,128)(2,1)S(1)} collective-permute-done((bf16[512,256]{1,0:T(8,128)(2,1)}, bf16[512,256]{1,0:T(8,128)(2,1)S(1)}, u32[]{:S(2)}, u32[]{:S(2)}) %collective-permute-start.4) | collective-permute-done | bytes 262176 | tf_op jit(solution)/shard_map/ppermute | solution.py:23
  19.4 0.6 %collective-permute-done.5.refs_3_.refs_4_ = bf16[512,256]{1,0:T(8,128)(2,1)S(1)} collective-permute-done((bf16[512,256]{1,0:T(8,128)(2,1)}, bf16[512,256]{1,0:T(8,128)(2,1)S(1)}, u32[]{:S(2)}, u32[]{:S(2)}) %collective-permute-start.5) | collective-permute-done | bytes 262176 | tf_op jit(solution)/shard_map/ppermute | solution.py:23
  20.1 0.8 %only_pairs.4 = (bf16[2,256,256]{2,1,0:T(8,128)(2,1)}, bf16[2,256,256]{2,1,0:T(8,128)(2,1)}) custom-call(bf16[512,256]{1,0:T(8,128)(2,1)S(1)} %get-tuple-element.44.refs_0_.refs_1_, bf16[512,256]{1,0:T(8,128)(2,1)S(1)} %collective-permute-done.3.refs_1_.refs_2_, bf16[512,256]{1,0:T(8,128)(2,1)S(1)} %collective-permute-done.4.refs_2_.refs_3_, ...), custom_call_target="tpu_custom_call" | custom-call | bytes 1048576 | tf_op jit(solution)/shard_map/only_pairs/pallas_call | solution.py:129
  20.9 0.5 collective-permute-start.7
  21.4 1.4 %collective-permute-start.1 = (bf16[528,256]{1,0:T(8,128)(2,1)S(1)}, bf16[528,256]{1,0:T(8,128)(2,1)S(1)}, u32[]{:S(2)}, u32[]{:S(2)}) collective-permute-start(bf16[528,256]{1,0:T(8,128)(2,1)S(1)} %get-tuple-element.42), channel_id=1, source_target_pairs={{0,16},{4,20},{8,24},{12,28},{16,0},{20,4},{24,8},{28,12},{1,17},{... | collective-permute-start | bytes 811016 | tf_op jit(solution)/shard_map/ppermute | solution.py:23
  22.8 1.5 %collective-permute-start.2 = (bf16[528,256]{1,0:T(8,128)(2,1)S(1)}, bf16[528,256]{1,0:T(8,128)(2,1)S(1)}, u32[]{:S(2)}, u32[]{:S(2)}) collective-permute-start(bf16[528,256]{1,0:T(8,128)(2,1)S(1)} %get-tuple-element.43), channel_id=1, source_target_pairs={{0,8},{4,12},{8,0},{12,4},{16,24},{20,28},{24,16},{28,20},{1,9},{5... | collective-permute-start | bytes 811016 | tf_op jit(solution)/shard_map/ppermute | solution.py:23
  24.3 0.1 copy.13.refs_0_
  24.4 0.0 collective-permute-done.6.refs_5_
  24.4 5.6 %attend_early.1 = (bf16[128,256]{1,0:T(8,128)(2,1)S(1)}, bf16[128,256]{1,0:T(8,128)(2,1)S(1)}, bf16[128,256]{1,0:T(8,128)(2,1)S(1)}, bf16[128,256]{1,0:T(8,128)(...) custom-call(s32[32,6]{1,0:T(8,128)S(1)} %copy.13.refs_0_, ...), custom_call_target="tpu_custom_call" | custom-call | tf_op jit(solution)/shard_map/attend_early/pallas_call | solution.py:384
  30.0 0.1 collective-permute-start.8
  30.1 0.1 collective-permute-done.1.refs_0_.refs_3_
  30.2 0.5 collective-permute-start.9
  30.7 0.2 collective-permute-done.2.refs_0_.refs_4_
  30.9 0.1 collective-permute-start.10
  31.0 0.8 %collective-permute-done.9.refs_6_ = bf16[1,256,256]{2,1,0:T(8,128)(2,1)S(1)} collective-permute-done((bf16[1,256,256]{2,1,0:T(8,128)(2,1)S(1)}, bf16[1,256,256]{2,1,0:T(8,128)(2,1)S(1)}, u32[]{:S(2)}, u32[]{:S(2)}) %collective-permute-start.9) | collective-permute-done | bytes 131104 | tf_op jit(solution)/shard_map/ppermute | solution.py:23
  31.8 0.5 collective-permute-done.10.refs_7_
  32.3 5.5 %attend_late.1 = (bf16[256,256]{1,0:T(8,128)(2,1)S(1)}, bf16[256,256]{1,0:T(8,128)(2,1)S(1)}, bf16[256,256]{1,0:T(8,128)(2,1)S(1)}, bf16[256,256]{1,0:T(8,128)(2...) custom-call(s32[32,6]{1,0:T(8,128)S(1)} %copy.13.refs_0_, ...), custom_call_target="tpu_custom_call", output_to_operand_aliasing={{9}: (12, {}), {10}: (13, {})} | custom-call | flops 1342177280 | bytes 4194304 | tf_op jit(solution)/shard_map/attend_late/pallas_call | solution.py:384
  37.8 0.2 collective-permute-start.14
  38.0 2.5 %collective-permute-start.11 = (bf16[256,256]{1,0:T(8,128)(2,1)S(1)}, bf16[256,256]{1,0:T(8,128)(2,1)S(1)}, u32[]{:S(2)}, u32[]{:S(2)}) collective-permute-start(bf16[256,256]{1,0:T(8,128)(2,1)S(1)} %get-tuple-element.56), channel_id=1, source_target_pairs={{0,24},{4,28},{8,16},{12,20},{16,8},{20,12},{24,0},{28,4},{1,25},{... | collective-permute-start | bytes 393224 | tf_op jit(solution)/shard_map/ppermute | solution.py:23
  40.5 0.5 collective-permute-start.12
  41.0 0.5 collective-permute-start.13
  41.5 0.3 add_partials.1
  41.8 2.5 %collective-permute-start.15 = (bf16[256,256]{1,0:T(8,128)(2,1)S(1)}, bf16[256,256]{1,0:T(8,128)(2,1)S(1)}, u32[]{:S(2)}, u32[]{:S(2)}) collective-permute-start(bf16[256,256]{1,0:T(8,128)(2,1)S(1)} %get-tuple-element.65), channel_id=1, source_target_pairs={{0,24},{4,28},{8,16},{12,20},{16,8},{20,12},{24,0},{28,4},{1,25},{... | collective-permute-start | bytes 393224 | tf_op jit(solution)/shard_map/ppermute | solution.py:23
  44.3 0.5 collective-permute-start.16
  44.8 0.3 collective-permute-done.11.refs_1_
  45.2 1.6 %collective-permute-start.17 = (bf16[256,256]{1,0:T(8,128)(2,1)S(1)}, bf16[256,256]{1,0:T(8,128)(2,1)S(1)}, u32[]{:S(2)}, u32[]{:S(2)}) collective-permute-start(bf16[256,256]{1,0:T(8,128)(2,1)S(1)} %get-tuple-element.67), channel_id=1, source_target_pairs={{0,8},{4,12},{8,0},{12,4},{16,24},{20,28},{24,16},{28,20},{1,9},{5... | collective-permute-start | bytes 393224 | tf_op jit(solution)/shard_map/ppermute | solution.py:23
  46.8 1.7 %collective-permute-done.12.refs_2_ = bf16[256,256]{1,0:T(8,128)(2,1)S(1)} collective-permute-done((bf16[256,256]{1,0:T(8,128)(2,1)S(1)}, bf16[256,256]{1,0:T(8,128)(2,1)S(1)}, u32[]{:S(2)}, u32[]{:S(2)}) %collective-permute-start.12) | collective-permute-done | bytes 131104 | tf_op jit(solution)/shard_map/ppermute | solution.py:23
  48.4 2.2 %collective-permute-start.18 = (bf16[256,256]{1,0:T(8,128)(2,1)S(1)}, bf16[256,256]{1,0:T(8,128)(2,1)S(1)}, u32[]{:S(2)}, u32[]{:S(2)}) collective-permute-start(bf16[256,256]{1,0:T(8,128)(2,1)S(1)} %get-tuple-element.70), channel_id=1, source_target_pairs={{0,24},{4,28},{8,16},{12,20},{16,8},{20,12},{24,0},{28,4},{1,25},{... | collective-permute-start | bytes 393224 | tf_op jit(solution)/shard_map/ppermute | solution.py:23
  50.6 0.5 collective-permute-start.19
  51.1 0.1 collective-permute-done.15.refs_5_
  51.2 1.2 %collective-permute-start.20 = (bf16[256,256]{1,0:T(8,128)(2,1)S(1)}, bf16[256,256]{1,0:T(8,128)(2,1)S(1)}, u32[]{:S(2)}, u32[]{:S(2)}) collective-permute-start(bf16[256,256]{1,0:T(8,128)(2,1)S(1)} %get-tuple-element.72), channel_id=1, source_target_pairs={{0,8},{4,12},{8,0},{12,4},{16,24},{20,28},{24,16},{28,20},{1,9},{5... | collective-permute-start | bytes 393224 | tf_op jit(solution)/shard_map/ppermute | solution.py:23
  52.4 1.6 %collective-permute-done.16.refs_6_ = bf16[256,256]{1,0:T(8,128)(2,1)S(1)} collective-permute-done((bf16[256,256]{1,0:T(8,128)(2,1)S(1)}, bf16[256,256]{1,0:T(8,128)(2,1)S(1)}, u32[]{:S(2)}, u32[]{:S(2)}) %collective-permute-start.16) | collective-permute-done | bytes 131104 | tf_op jit(solution)/shard_map/ppermute | solution.py:23
  54.1 1.7 %join_first.1 = (bf16[512,512]{1,0:T(8,128)(2,1)}, bf16[512,512]{1,0:T(8,128)(2,1)}, bf16[512,512]{1,0:T(8,128)(2,1)}) custom-call(bf16[256,256]{1,0:T(8,128)(2,1)S(1)} %get-tuple-element.55.refs_0_, bf16[256,256]{1,0:T(8,128)(2,1)S(1)} %collective-permute-done.11.refs_1_, bf16[256,256]{1,0:T(8,128)(2,1)S(1)} %collective-permute-done.12.refs_2_, ...), custom_call_target="tpu_custom_call" | custom-call | bytes 2097152 | tf_op jit(solution)/shard_map/join_first/pallas_call | solution.py:185
  55.8 1.1 %collective-permute-done.18.refs_1_ = bf16[256,256]{1,0:T(8,128)(2,1)S(1)} collective-permute-done((bf16[256,256]{1,0:T(8,128)(2,1)S(1)}, bf16[256,256]{1,0:T(8,128)(2,1)S(1)}, u32[]{:S(2)}, u32[]{:S(2)}) %collective-permute-start.18) | collective-permute-done | bytes 131104 | tf_op jit(solution)/shard_map/ppermute | solution.py:23
  56.9 1.9 %collective-permute-done.19.refs_2_ = bf16[256,256]{1,0:T(8,128)(2,1)S(1)} collective-permute-done((bf16[256,256]{1,0:T(8,128)(2,1)S(1)}, bf16[256,256]{1,0:T(8,128)(2,1)S(1)}, u32[]{:S(2)}, u32[]{:S(2)}) %collective-permute-start.19) | collective-permute-done | bytes 131104 | tf_op jit(solution)/shard_map/ppermute | solution.py:23
  58.7 0.9 %join_second.1 = (bf16[512,512]{1,0:T(8,128)(2,1)}, bf16[512,512]{1,0:T(8,128)(2,1)}) custom-call(bf16[256,256]{1,0:T(8,128)(2,1)S(1)} %get-tuple-element.69.refs_0_, bf16[256,256]{1,0:T(8,128)(2,1)S(1)} %collective-permute-done.18.refs_1_, bf16[256,256]{1,0:T(8,128)(2,1)S(1)} %collective-permute-done.19.refs_2_, ...), custom_call_target="tpu_custom_call", output_to_operand_aliasing={{0}: (4, {}), {1}: (5, {})} | custom-call | bytes 1048576 | tf_op jit(solution)/shard_map/join_second/pallas_call | solution.py:195
  (17 shorter events, 0.1 us)
Async XLA Ops:
  0.6 8.5 %copy-start.3 = (bf16[512,512]{1,0:T(8,128)(2,1)S(1)}, bf16[512,512]{1,0:T(8,128)(2,1)}, u32[]{:S(2)}) copy-start(bf16[512,512]{1,0:T(8,128)(2,1)} %refs_3_.5) | copy-start | bytes 1572868
  0.6 8.5 %copy-start.2 = (bf16[512,512]{1,0:T(8,128)(2,1)S(1)}, bf16[512,512]{1,0:T(8,128)(2,1)}, u32[]{:S(2)}) copy-start(bf16[512,512]{1,0:T(8,128)(2,1)} %refs_2_.5) | copy-start | bytes 1572868
  0.7 8.5 %copy-start.1 = (bf16[512,512]{1,0:T(8,128)(2,1)S(1)}, bf16[512,512]{1,0:T(8,128)(2,1)}, u32[]{:S(2)}) copy-start(bf16[512,512]{1,0:T(8,128)(2,1)} %refs_1_.5) | copy-start | bytes 1572868
  0.7 8.4 %copy-start = (bf16[512,512]{1,0:T(8,128)(2,1)S(1)}, bf16[512,512]{1,0:T(8,128)(2,1)}, u32[]{:S(2)}) copy-start(bf16[512,512]{1,0:T(8,128)(2,1)} %refs_0_.7) | copy-start | bytes 1572868
  0.7 23.6 %copy-start.4 = (s32[32,6]{0,1:T(8,128)S(1)}, s32[32,6]{0,1:T(8,128)}, u32[]{:S(2)}) copy-start(s32[32,6]{0,1:T(8,128)} %param.9) | copy-start | bytes 2308
  2.5 11.3 %collective-permute-start.3 = (bf16[512,256]{1,0:T(8,128)(2,1)}, bf16[512,256]{1,0:T(8,128)(2,1)S(1)}, u32[]{:S(2)}, u32[]{:S(2)}) collective-permute-start(bf16[512,256]{1,0:T(8,128)(2,1)} %split_early.2.refs_4_), channel_id=1, source_target_pairs={{0,24},{4,28},{8,16},{12,20},{16,8},{20,12},{24,0},{28,4},{1,25},{... | collective-permute-start | bytes 786440 | tf_op jit(solution)/shard_map/ppermute | solution.py:23
  8.4 11.0 %collective-permute-start.4 = (bf16[512,256]{1,0:T(8,128)(2,1)}, bf16[512,256]{1,0:T(8,128)(2,1)S(1)}, u32[]{:S(2)}, u32[]{:S(2)}) collective-permute-start(bf16[512,256]{1,0:T(8,128)(2,1)} %get-tuple-element.45), channel_id=1, source_target_pairs={{0,16},{4,20},{8,24},{12,28},{16,0},{20,4},{24,8},{28,12},{1,17},{... | collective-permute-start | bytes 786440 | tf_op jit(solution)/shard_map/ppermute | solution.py:23
  9.0 11.1 %collective-permute-start.5 = (bf16[512,256]{1,0:T(8,128)(2,1)}, bf16[512,256]{1,0:T(8,128)(2,1)S(1)}, u32[]{:S(2)}, u32[]{:S(2)}) collective-permute-start(bf16[512,256]{1,0:T(8,128)(2,1)} %get-tuple-element.46), channel_id=1, source_target_pairs={{0,8},{4,12},{8,0},{12,4},{16,24},{20,28},{24,16},{28,20},{1,9},{5... | collective-permute-start | bytes 786440 | tf_op jit(solution)/shard_map/ppermute | solution.py:23
  9.4 20.6 %collective-permute-start = (bf16[528,256]{1,0:T(8,128)(2,1)S(1)}, bf16[528,256]{1,0:T(8,128)(2,1)S(1)}, u32[]{:S(2)}, u32[]{:S(2)}) collective-permute-start(bf16[528,256]{1,0:T(8,128)(2,1)S(1)} %get-tuple-element.41), channel_id=1, source_target_pairs={{0,24},{4,28},{8,16},{12,20},{16,8},{20,12},{24,0},{28,4},{1,25},{... | collective-permute-start | bytes 811016 | tf_op jit(solution)/shard_map/ppermute | solution.py:23
  20.9 3.5 %collective-permute-start.6 = (bf16[2,256,256]{2,1,0:T(8,128)(2,1)}, bf16[2,256,256]{2,1,0:T(8,128)(2,1)S(1)}, u32[]{:S(2)}, u32[]{:S(2)}) collective-permute-start(bf16[2,256,256]{2,1,0:T(8,128)(2,1)} %get-tuple-element.47), channel_id=1, source_target_pairs={{0,4},{4,0},{8,12},{12,8},{16,20},{20,16},{24,28},{28,24},{1,5},{5... | collective-permute-start | bytes 786440 | tf_op jit(solution)/shard_map/ppermute | solution.py:23
  20.9 3.5 %collective-permute-start.7 = (bf16[2,256,256]{2,1,0:T(8,128)(2,1)}, bf16[2,256,256]{2,1,0:T(8,128)(2,1)S(1)}, u32[]{:S(2)}, u32[]{:S(2)}) collective-permute-start(bf16[2,256,256]{2,1,0:T(8,128)(2,1)} %get-tuple-element.48), channel_id=1, source_target_pairs={{0,4},{4,0},{8,12},{12,8},{16,20},{20,16},{24,28},{28,24},{1,5},{5... | collective-permute-start | bytes 786440 | tf_op jit(solution)/shard_map/ppermute | solution.py:23
  21.4 8.8 %collective-permute-start.1 = (bf16[528,256]{1,0:T(8,128)(2,1)S(1)}, bf16[528,256]{1,0:T(8,128)(2,1)S(1)}, u32[]{:S(2)}, u32[]{:S(2)}) collective-permute-start(bf16[528,256]{1,0:T(8,128)(2,1)S(1)} %get-tuple-element.42), channel_id=1, source_target_pairs={{0,16},{4,20},{8,24},{12,28},{16,0},{20,4},{24,8},{28,12},{1,17},{... | collective-permute-start | bytes 811016 | tf_op jit(solution)/shard_map/ppermute | solution.py:23
  22.8 8.1 %collective-permute-start.2 = (bf16[528,256]{1,0:T(8,128)(2,1)S(1)}, bf16[528,256]{1,0:T(8,128)(2,1)S(1)}, u32[]{:S(2)}, u32[]{:S(2)}) collective-permute-start(bf16[528,256]{1,0:T(8,128)(2,1)S(1)} %get-tuple-element.43), channel_id=1, source_target_pairs={{0,8},{4,12},{8,0},{12,4},{16,24},{20,28},{24,16},{28,20},{1,9},{5... | collective-permute-start | bytes 811016 | tf_op jit(solution)/shard_map/ppermute | solution.py:23
  30.0 2.3 %collective-permute-start.8 = (bf16[2,256,256]{2,1,0:T(8,128)(2,1)S(1)}, bf16[2,256,256]{2,1,0:T(8,128)(2,1)S(1)}, u32[]{:S(2)}, u32[]{:S(2)}) collective-permute-start(bf16[2,256,256]{2,1,0:T(8,128)(2,1)S(1)} %only_pairs.5), channel_id=1, source_target_pairs={{0,4},{4,0},{8,12},{12,8},{16,20},{20,16},{24,28},{28,24},{1,5},{5... | collective-permute-start | bytes 786440 | tf_op jit(solution)/shard_map/ppermute | solution.py:23
  30.2 1.6 %collective-permute-start.9 = (bf16[1,256,256]{2,1,0:T(8,128)(2,1)S(1)}, bf16[1,256,256]{2,1,0:T(8,128)(2,1)S(1)}, u32[]{:S(2)}, u32[]{:S(2)}) collective-permute-start(bf16[1,256,256]{2,1,0:T(8,128)(2,1)S(1)} %only_pairs.6), channel_id=1, source_target_pairs={{0,4},{4,0},{8,12},{12,8},{16,20},{20,16},{24,28},{28,24},{1,5},{5... | collective-permute-start | bytes 393224 | tf_op jit(solution)/shard_map/ppermute | solution.py:23
  30.9 1.4 %collective-permute-start.10 = (bf16[1,256,256]{2,1,0:T(8,128)(2,1)S(1)}, bf16[1,256,256]{2,1,0:T(8,128)(2,1)S(1)}, u32[]{:S(2)}, u32[]{:S(2)}) collective-permute-start(bf16[1,256,256]{2,1,0:T(8,128)(2,1)S(1)} %only_pairs.7), channel_id=1, source_target_pairs={{0,4},{4,0},{8,12},{12,8},{16,20},{20,16},{24,28},{28,24},{1,5},{5... | collective-permute-start | bytes 393224 | tf_op jit(solution)/shard_map/ppermute | solution.py:23
  37.8 3.7 %collective-permute-start.14 = (bf16[4,512,256]{2,1,0:T(8,128)(2,1)S(1)}, bf16[4,512,256]{2,1,0:T(8,128)(2,1)S(1)}, u32[]{:S(2)}, u32[]{:S(2)}) collective-permute-start(bf16[4,512,256]{2,1,0:T(8,128)(2,1)S(1)} %get-tuple-element.59), channel_id=1, source_target_pairs={{0,4},{4,0},{8,12},{12,8},{16,20},{20,16},{24,28},{28,24},{1,5},{5... | collective-permute-start | bytes 3145736 | tf_op jit(solution)/shard_map/ppermute | solution.py:23
  38.0 7.2 %collective-permute-start.11 = (bf16[256,256]{1,0:T(8,128)(2,1)S(1)}, bf16[256,256]{1,0:T(8,128)(2,1)S(1)}, u32[]{:S(2)}, u32[]{:S(2)}) collective-permute-start(bf16[256,256]{1,0:T(8,128)(2,1)S(1)} %get-tuple-element.56), channel_id=1, source_target_pairs={{0,24},{4,28},{8,16},{12,20},{16,8},{20,12},{24,0},{28,4},{1,25},{... | collective-permute-start | bytes 393224 | tf_op jit(solution)/shard_map/ppermute | solution.py:23
  40.5 8.0 %collective-permute-start.12 = (bf16[256,256]{1,0:T(8,128)(2,1)S(1)}, bf16[256,256]{1,0:T(8,128)(2,1)S(1)}, u32[]{:S(2)}, u32[]{:S(2)}) collective-permute-start(bf16[256,256]{1,0:T(8,128)(2,1)S(1)} %get-tuple-element.57), channel_id=1, source_target_pairs={{0,16},{4,20},{8,24},{12,28},{16,0},{20,4},{24,8},{28,12},{1,17},{... | collective-permute-start | bytes 393224 | tf_op jit(solution)/shard_map/ppermute | solution.py:23
  41.0 9.6 %collective-permute-start.13 = (bf16[256,256]{1,0:T(8,128)(2,1)S(1)}, bf16[256,256]{1,0:T(8,128)(2,1)S(1)}, u32[]{:S(2)}, u32[]{:S(2)}) collective-permute-start(bf16[256,256]{1,0:T(8,128)(2,1)S(1)} %get-tuple-element.58), channel_id=1, source_target_pairs={{0,8},{4,12},{8,0},{12,4},{16,24},{20,28},{24,16},{28,20},{1,9},{5... | collective-permute-start | bytes 393224 | tf_op jit(solution)/shard_map/ppermute | solution.py:23
  41.8 9.4 %collective-permute-start.15 = (bf16[256,256]{1,0:T(8,128)(2,1)S(1)}, bf16[256,256]{1,0:T(8,128)(2,1)S(1)}, u32[]{:S(2)}, u32[]{:S(2)}) collective-permute-start(bf16[256,256]{1,0:T(8,128)(2,1)S(1)} %get-tuple-element.65), channel_id=1, source_target_pairs={{0,24},{4,28},{8,16},{12,20},{16,8},{20,12},{24,0},{28,4},{1,25},{... | collective-permute-start | bytes 393224 | tf_op jit(solution)/shard_map/ppermute | solution.py:23
  44.3 9.7 %collective-permute-start.16 = (bf16[256,256]{1,0:T(8,128)(2,1)S(1)}, bf16[256,256]{1,0:T(8,128)(2,1)S(1)}, u32[]{:S(2)}, u32[]{:S(2)}) collective-permute-start(bf16[256,256]{1,0:T(8,128)(2,1)S(1)} %get-tuple-element.66), channel_id=1, source_target_pairs={{0,16},{4,20},{8,24},{12,28},{16,0},{20,4},{24,8},{28,12},{1,17},{... | collective-permute-start | bytes 393224 | tf_op jit(solution)/shard_map/ppermute | solution.py:23
  45.2 8.9 %collective-permute-start.17 = (bf16[256,256]{1,0:T(8,128)(2,1)S(1)}, bf16[256,256]{1,0:T(8,128)(2,1)S(1)}, u32[]{:S(2)}, u32[]{:S(2)}) collective-permute-start(bf16[256,256]{1,0:T(8,128)(2,1)S(1)} %get-tuple-element.67), channel_id=1, source_target_pairs={{0,8},{4,12},{8,0},{12,4},{16,24},{20,28},{24,16},{28,20},{1,9},{5... | collective-permute-start | bytes 393224 | tf_op jit(solution)/shard_map/ppermute | solution.py:23
  48.4 8.4 %collective-permute-start.18 = (bf16[256,256]{1,0:T(8,128)(2,1)S(1)}, bf16[256,256]{1,0:T(8,128)(2,1)S(1)}, u32[]{:S(2)}, u32[]{:S(2)}) collective-permute-start(bf16[256,256]{1,0:T(8,128)(2,1)S(1)} %get-tuple-element.70), channel_id=1, source_target_pairs={{0,24},{4,28},{8,16},{12,20},{16,8},{20,12},{24,0},{28,4},{1,25},{... | collective-permute-start | bytes 393224 | tf_op jit(solution)/shard_map/ppermute | solution.py:23
  50.6 8.1 %collective-permute-start.19 = (bf16[256,256]{1,0:T(8,128)(2,1)S(1)}, bf16[256,256]{1,0:T(8,128)(2,1)S(1)}, u32[]{:S(2)}, u32[]{:S(2)}) collective-permute-start(bf16[256,256]{1,0:T(8,128)(2,1)S(1)} %get-tuple-element.71), channel_id=1, source_target_pairs={{0,16},{4,20},{8,24},{12,28},{16,0},{20,4},{24,8},{28,12},{1,17},{... | collective-permute-start | bytes 393224 | tf_op jit(solution)/shard_map/ppermute | solution.py:23
  51.2 7.5 %collective-permute-start.20 = (bf16[256,256]{1,0:T(8,128)(2,1)S(1)}, bf16[256,256]{1,0:T(8,128)(2,1)S(1)}, u32[]{:S(2)}, u32[]{:S(2)}) collective-permute-start(bf16[256,256]{1,0:T(8,128)(2,1)S(1)} %get-tuple-element.72), channel_id=1, source_target_pairs={{0,8},{4,12},{8,0},{12,4},{16,24},{20,28},{24,16},{28,20},{1,9},{5... | collective-permute-start | bytes 393224 | tf_op jit(solution)/shard_map/ppermute | solution.py:23
